TPU v7x, 32 devices: a whole 2x2x4 slice. The times are simulated.
32 devices in a mesh: ctx: 4 (over y, core), enc: 8 (over z, x).
Axes of the slice: x: 2, y: 2, z: 4, core: 2. Of those that a mesh axis runs over, the one named last changes fastest.
Arguments:
- queries: bfloat16 [8, 512, 4096], P('enc', 'ctx'), may hold values from -200 to 200
- d_out: bfloat16 [8, 512, 4096], P('enc', 'ctx'), may hold values from -24 to 24
- text_sample: int32 [8, 512], P('enc', 'ctx'), may hold values from 0 to 1, as said below
- tiles: int32 [8, 2], P('enc'), may hold values from 1 to 4
- img_k: bfloat16 [8, 512, 1024], P(None, ('ctx', 'enc')), may hold values from -20 to 20
- img_v: bfloat16 [8, 512, 1024], P(None, ('ctx', 'enc')), may hold values from -6 to 6
Outputs:
- d_queries: bfloat16 [8, 512, 4096], P('enc', 'ctx')
- d_img_k: bfloat16 [8, 512, 1024], P(None, ('ctx', 'enc'))
- d_img_v: bfloat16 [8, 512, 1024], P(None, ('ctx', 'enc'))
Inputs may be any that keep to these rules, and one draw needn't show every extreme that they name: `text_sample`: within each group the sample numbers never fall along the text, and each of the 2 samples has at least one token.
All inputs are finite; a program needn't handle non-finite values.
Results may differ from a plain program's by a relative error of at most 0.022.
Values may be sent and summed in bfloat16 or wider, within the bound.
No kernel may reach another device: no remote copies, remote signals or barrier semaphores. Data moves between devices by JAX's collectives and lax.ppermute only.
A program may use at most 128 MiB of HBM per device.

v0:
```python
import functools

import jax
import jax.numpy as jnp
from jax import lax
from jax.experimental import pallas as pl
from jax.experimental.pallas import tpu as pltpu
from jax.sharding import PartitionSpec as P

H = 32
KVH = 8
HD = 128
SAMP = 2
MAX_TILES = 4
TILE_TOK = 64
RATIO = H // KVH
CORES = 2
SLOT_ROWS = MAX_TILES * TILE_TOK
HALF_KV = KVH // CORES
HALF_KCOLS = HALF_KV * HD
HALF_QCOLS = HALF_KCOLS * RATIO
WIDE = RATIO * HD
SAMP_ROWS = 16
DQ_PARTS = 2
SCALE = HD ** (-0.5)
LOG2E = 1.4426950408889634
BIG_NEGATIVE = -1e30
NT = (((1,), (1,)), ((), ()))
TN = (((0,), (0,)), ((), ()))
BF16 = jnp.bfloat16
F32 = jnp.float32

IN_VMEM = pl.BlockSpec(memory_space=pltpu.VMEM)
IN_HBM = pl.BlockSpec(memory_space=pltpu.HBM)


def local_call(body, ins, outs, scratch=(), flops=0, moved=2**19, aliases={}):
    return pl.pallas_call(
        body,
        in_specs=ins,
        out_specs=[spec for _, _, spec in outs],
        out_shape=[jax.ShapeDtypeStruct(s, d) for s, d, _ in outs],
        scratch_shapes=list(scratch),
        compiler_params=pltpu.CompilerParams(vmem_limit_bytes=8 * 2**20),
        input_output_aliases=aliases,
        cost_estimate=pl.CostEstimate(
            flops=flops, bytes_accessed=moved, transcendentals=flops // 1280
        ),
    )


def in_vmem(body, outs, **more):
    def call(*args):
        spec = [(shape, dtype, IN_VMEM) for shape, dtype in outs]
        return local_call(body, [IN_VMEM] * len(args), spec, **more)(*args)

    return call


def core_of():
    return lax.rem(lax.axis_index("ctx"), CORES)


def at_rows(first, count):
    return pl.ds(pl.multiple_of(first, count), count)


def at_cols(first, width, step):
    return pl.ds(pl.multiple_of(first, step), width)


def start_copies(pairs, sems):
    copies = [pltpu.make_async_copy(src, dst, sems.at[i]) for i, (src, dst) in enumerate(pairs)]
    for copy in copies:
        copy.start()
    return copies


def run_copies(pairs, sems):
    for copy in start_copies(pairs, sems):
        copy.wait()


def in_hbm(*arrays):
    return [pltpu.with_memory_space_constraint(a, pltpu.HBM) for a in arrays]


def split_kernel(k_ref, v_ref, mine, peer, sems):
    core = core_of()
    pairs = []
    for half, out in ((1 - core, peer), (core, mine)):
        cols = at_cols(half * HALF_KCOLS, HALF_KCOLS, HALF_KCOLS)
        for i, ref in enumerate((k_ref, v_ref)):
            pairs.append((ref.at[:, :, cols], out.at[i]))
    run_copies(pairs, sems)


def near_place():
    return lax.div(lax.axis_index("ctx"), CORES), lax.axis_index("enc")


def split_text(n_blocks, pieces, where, q_ref, g_ref, samp_hbm, tiles_hbm, peer, q_own, g_own, bias, samp, tiles, sems):
    core = core_of()
    tokens = q_ref.shape[1]
    own_cols = at_cols(core * HALF_QCOLS, HALF_QCOLS, HALF_QCOLS)
    peer_cols = at_cols((1 - core) * HALF_QCOLS, HALF_QCOLS, HALF_QCOLS)
    copies = start_copies(
        [
            (samp_hbm, samp),
            (tiles_hbm, tiles),
            (q_ref.at[0, :, peer_cols], peer.at[:tokens]),
            (g_ref.at[0, :, peer_cols], peer.at[tokens : 2 * tokens]),
            (q_ref.at[0, :, own_cols], q_own.at[:tokens]),
            (g_ref.at[0, :, own_cols], g_own),
        ],
        sems,
    )
    for copy in copies[:2]:
        copy.wait()
    row = jnp.broadcast_to(samp[...].astype(F32), (SAMP_ROWS, tokens)).astype(BF16)
    for out, first in ((q_own, tokens), (peer, 2 * tokens)):
        out[first:, :] = jnp.zeros((SAMP_ROWS, HALF_QCOLS), BF16)
        out[first:, :tokens] = row

    sample, enc = where()
    block_rows = SLOT_ROWS // n_blocks
    slots = block_rows // pieces
    line = lax.broadcasted_iota(jnp.int32, (SLOT_ROWS, HD), 0)
    block = lax.div(line, block_rows)
    if n_blocks > 1:
        low, high = block & 1, lax.div(block, 2) & 1
        block = block - low - 2 * high + 2 * low + high
    owner = block ^ enc
    piece = lax.rem(lax.div(line, slots), pieces)
    slot = piece * (SLOT_ROWS // pieces) + owner * slots + lax.rem(line, slots)
    for i in range(SAMP):
        count = jnp.where((sample ^ i) == 0, tiles[0:1, 0:1], tiles[0:1, 1:2])
        bias[i] = jnp.where(slot < count * TILE_TOK, 0.0, BIG_NEGATIVE)
    for copy in copies[2:]:
        copy.wait()


def carry_kernel(slots, own, got, text, *outs):
    core = core_of()
    enc = lax.axis_index("enc")
    for dz, out in enumerate(outs[:-1]):
        for dx in range(2):
            group = enc ^ (2 * dz + dx)
            for i in range(2):
                first = i * CORES * slots
                out[dx, at_rows(first + core * slots, slots), :] = own[i, group]
                out[dx, at_rows(first + (1 - core) * slots, slots), :] = got[i, group]


def join_kernel(*refs):
    parts, outs = refs[:2], refs[-2:]
    rows = parts[0].shape[1]
    for dx, out in enumerate(outs):
        for dz, part in enumerate(parts):
            out[dz * rows : (dz + 1) * rows, :] = part[dx]


def block_place(b, n_outs):
    half, x, z = b // 4, b // 2 % 2, b % 2
    return {1: (0, b), 2: (x, 2 * half + z), 4: (2 * half + x, z)}[n_outs]


def add_kernel(z, own, back_x, back_y, back_xy, *outs):
    rows = outs[0].shape[1]
    for dz, out in enumerate(outs):
        near = slice((z + dz) * rows, (z + dz + 1) * rows)
        far = slice(dz * rows, (dz + 1) * rows)
        for dx, (here, back) in enumerate(((own, back_y), (back_x, back_xy))):
            out[dx] = (here[near, :].astype(F32) + back[far, :].astype(F32)).astype(out.dtype)


def nothing_kernel(*refs):
    pass


def hand_on(array, *after):
    return in_vmem(nothing_kernel, [(array.shape, array.dtype)], aliases={0: 0})(array, *after)


def far_rows_kernel(slots, *refs):
    core = core_of()
    parts, outs = refs[:2], refs[-2:]
    for dz, part in enumerate(parts):
        for dx in range(2):
            for i in range(2):
                first = i * CORES * slots
                for who, out in zip((core, 1 - core), outs):
                    out[i, 2 * dz + dx] = part[dx, at_rows(first + who * slots, slots), :]


def owner_rows_kernel(slots, *refs):
    core = core_of()
    enc = lax.axis_index("enc")
    parts, far, outs = refs[:2], refs[2:4], refs[4:]
    for dz, part in enumerate(parts):
        for dx in range(2):
            d = 2 * dz + dx
            for i in range(2):
                first = i * CORES * slots
                for who, from_far, out in zip((core, 1 - core), far, outs):
                    out[i, enc ^ d] = part[dx, at_rows(first + who * slots, slots), :]
                    out[i, enc ^ (2 * len(parts) + d)] = from_far[i, d]


def finish_kernel(mine, got, _, dk, dv, sems):
    core = core_of()
    pairs = []
    for half, ref in ((core, mine), (1 - core, got)):
        cols = at_cols(half * HALF_KCOLS, HALF_KCOLS, HALF_KCOLS)
        for i, out in enumerate((dk, dv)):
            pairs.append((ref.at[i], out.at[:, :, cols]))
    run_copies(pairs, sems)


def split_rows_kernel(whole, *refs):
    outs = refs[-DQ_PARTS:]
    rows = outs[0].shape[0]
    for i, out in enumerate(outs):
        out[...] = whole[i * rows : (i + 1) * rows, :]


def finish_text_kernel(mine, *refs):
    got, (out, token, sems) = refs[:-3], refs[-3:]
    core = core_of()
    token[...] = jnp.zeros_like(token)
    own_cols = at_cols(core * HALF_QCOLS, HALF_QCOLS, HALF_QCOLS)
    got_cols = at_cols((1 - core) * HALF_QCOLS, HALF_QCOLS, HALF_QCOLS)
    pairs = [(mine, out.at[0, :, own_cols])]
    rows = got[0].shape[0]
    for i, ref in enumerate(got):
        pairs.append((ref, out.at[0, i * rows : (i + 1) * rows, got_cols]))
    run_copies(pairs, sems)


def blocks_with(sample, q_own, got):
    tokens = q_own.shape[0] - SAMP_ROWS
    rows = (q_own[tokens : tokens + 1, :tokens], got[2 * tokens : 2 * tokens + 1, :tokens])
    rows = [row.astype(F32) for row in rows]
    wanted = sample.astype(F32)
    return rows, [jnp.max(jnp.where(row == wanted, 1.0, 0.0)) > 0.5 for row in rows]


def key_rows(kvs, block_rows, first, h):
    parts = []
    for kv in kvs:
        for at in range(first, kv.shape[0], 2 * block_rows):
            parts.append(kv[at : at + block_rows, h * HD : (h + 1) * HD])
    return jnp.concatenate(parts, axis=0)


def choose(flags, branch):
    for which in ((0, 1), (0,), (1,), ()):
        wants = [flags[t] if t in which else jnp.logical_not(flags[t]) for t in range(2)]

        @pl.when(wants[0] & wants[1])
        def _():
            branch(which)


def pass_kernel(role, n_blocks, n_kv, n_grads, where, bias, q_a, g_a, got, *rest):
    kvs, (ds_out, *grads) = rest[:n_kv], rest[-1 - n_grads :]
    sample = where()[0] ^ role
    tokens = g_a.shape[0]
    block_rows = SLOT_ROWS // n_blocks
    rows, present = blocks_with(sample, q_a, got)
    sources = ((q_a, 0, g_a, 0), (got, 0, got, tokens))

    def one_pass(which):
        if not which:
            for out in grads:
                out[...] = jnp.zeros_like(out)
            return
        mine = jnp.concatenate([rows[t] for t in which for _ in range(RATIO)], axis=1)
        mine = mine == sample.astype(F32)
        masks = jnp.concatenate([bias[role]] * (len(which) * RATIO), axis=1)

        def products(h):
            def stacked(part):
                parts = []
                for t in which:
                    ref, first = sources[t][part : part + 2]
                    for r in range(RATIO):
                        at = h * WIDE + r * HD
                        parts.append(ref[first : first + tokens, at : at + HD])
                return jnp.concatenate(parts, axis=0)

            q, g = stacked(0), stacked(2)
            k, v = (key_rows(kvs, block_rows, first, h) for first in (0, block_rows))
            s = lax.dot_general(k, q, NT, preferred_element_type=F32)
            gp = lax.dot_general(v, g, NT, preferred_element_type=F32)
            return q, g, s, gp

        early = len(which) == 1
        ahead = products(0)
        for h in range(HALF_KV):
            q, g, s, gp = ahead
            if early and h + 1 < HALF_KV:
                ahead = products(h + 1)
            s = s + masks
            top = jnp.max(s, axis=0, keepdims=True)
            e = jnp.exp2((s - top) * (SCALE * LOG2E))
            total = jnp.sum(e, axis=0, keepdims=True)
            p = e * jnp.where(mine, 1.0 / total, 0.0)
            row_dot = jnp.sum(p * gp, axis=0, keepdims=True)
            ds = (p * (gp - row_dot)).astype(BF16)
            dv = jnp.dot(p.astype(BF16), g, preferred_element_type=F32)
            dk = jnp.dot(ds, q, preferred_element_type=F32) * SCALE
            wide = RATIO * tokens
            for i, t in enumerate(which):
                ds_out[h, :, t * wide : (t + 1) * wide] = ds[:, i * wide : (i + 1) * wide]
            cols = slice(h * HD, (h + 1) * HD)
            for b in range(n_blocks):
                block = slice(b * block_rows, (b + 1) * block_rows)
                dx, at = block_place(b, len(grads))
                out, first = grads[dx], at * 2 * block_rows
                out[first : first + block_rows, cols] = dk[block].astype(out.dtype)
                out[first + block_rows : first + 2 * block_rows, cols] = dv[block].astype(out.dtype)
            if not early and h + 1 < HALF_KV:
                ahead = products(h + 1)

    choose(present, one_pass)


def dq_kernel(n_blocks, n_kv, where, q_a, got, *rest):
    keys = rest[:n_kv], rest[n_kv : 2 * n_kv]
    ds, dqs = rest[2 * n_kv : 2 * n_kv + 2], rest[-2:]
    tokens = dqs[0].shape[0]
    block_rows = SLOT_ROWS // n_blocks
    first = where()[0]
    present = [blocks_with(first ^ role, q_a, got)[1] for role in range(SAMP)]
    wide = RATIO * tokens
    for t, dq_ref in enumerate(dqs):

        def one_block(roles):
            for h in range(HALF_KV):
                total = 0.0
                for role in roles:
                    k = key_rows(keys[role], block_rows, 0, h)
                    part = ds[role][h, :, t * wide : (t + 1) * wide]
                    total += lax.dot_general(part, k, TN, preferred_element_type=F32)
                if roles:
                    for r in range(RATIO):
                        at = h * WIDE + r * HD
                        rows = total[r * tokens : (r + 1) * tokens] * SCALE
                        dq_ref[:, at : at + HD] = rows.astype(dq_ref.dtype)

        choose([present[role][t] for role in range(SAMP)], one_block)


def sample_pass(where, role, n_blocks, bias, text, kvs, grads, after=()):
    tokens = text[1].shape[0]
    ds = ((HALF_KV, SLOT_ROWS, CORES * RATIO * tokens), BF16)
    return in_vmem(
        functools.partial(pass_kernel, role, n_blocks, len(kvs), len(grads), where),
        [ds, *grads],
        flops=8 * tokens * WIDE * SLOT_ROWS * CORES * HALF_KV,
        moved=16 * 2**20,
    )(bias, *text, *kvs, *after)


def text_grads(where, n_blocks, text, keys, ds):
    tokens = text[1].shape[0]
    return in_vmem(
        functools.partial(dq_kernel, n_blocks, len(keys[0]), where),
        [((tokens, HALF_QCOLS), BF16)] * 2,
        flops=4 * tokens * WIDE * SLOT_ROWS * CORES * HALF_KV,
        moved=8 * 2**20,
    )(text[0], text[2], *keys[0], *keys[1], *ds)


def shards(n_ctx, n_enc, queries, d_out, text_sample, tiles, img_k, img_v):
    n_y = n_ctx // CORES
    slots = img_k.shape[1]
    tokens = queries.shape[1]
    swap_core = [(i, i ^ 1) for i in range(n_ctx)]
    near = n_y == SAMP and slots % 16 == 0 and n_enc == 8
    text_outs = [
        ((2 * tokens + SAMP_ROWS, HALF_QCOLS), BF16, IN_VMEM),
        ((tokens + SAMP_ROWS, HALF_QCOLS), BF16, IN_VMEM),
        ((tokens, HALF_QCOLS), BF16, IN_VMEM),
        ((SAMP, SLOT_ROWS, HD), F32, IN_VMEM),
    ]

    def split_the_text(n_blocks, pieces, where):
        return local_call(
            functools.partial(split_text, n_blocks, pieces, where),
            [IN_HBM] * 4,
            text_outs,
            [
                pltpu.VMEM(text_sample.shape, jnp.int32),
                pltpu.VMEM(tiles.shape, jnp.int32),
                pltpu.SemaphoreType.DMA((6,)),
            ],
            moved=4 * 2**20,
        )(*in_hbm(queries, d_out, text_sample, tiles))

    if near:
        swap_y = [(i, (i + CORES) % n_ctx) for i in range(n_ctx)]
        n_z = n_enc // 2
        block_rows = 2 * CORES * slots
        pair = (2, block_rows, HALF_KCOLS)
        quarter = (2 * block_rows, HALF_KCOLS)
        whole = (SLOT_ROWS, HALF_KCOLS)
        kv_halves = (2, n_enc, slots, HALF_KCOLS)
        swap_x = [(i, i ^ 1) for i in range(n_enc)]
        swap_xy = [
            (i * n_enc + e, (i + CORES) % n_ctx * n_enc + (e ^ 1))
            for i in range(n_ctx)
            for e in range(n_enc)
        ]

        def along_z(part, dz):
            return lax.ppermute(part, "enc", [(i, i ^ (2 * dz)) for i in range(n_enc)]) if dz else part

        def along_x(part):
            return lax.ppermute(part, "enc", swap_x)

        def along_y(part):
            return lax.ppermute(part, "ctx", swap_y)

        def along_xy(part):
            return lax.ppermute(part, ("ctx", "enc"), swap_xy)

        mine, for_peer = local_call(
            split_kernel,
            [IN_HBM] * 2,
            [(kv_halves, BF16, IN_VMEM)] * 2,
            [pltpu.SemaphoreType.DMA((4,))],
        )(*in_hbm(img_k, img_v))
        text_peer, q_own, g_own, bias = split_the_text(n_enc, CORES, near_place)
        *carry, text_peer = in_vmem(
            functools.partial(carry_kernel, slots),
            [(pair, BF16)] * n_z + [(text_peer.shape, BF16)],
            aliases={2: n_z},
        )(mine, lax.ppermute(for_peer, "ctx", swap_core), text_peer)
        text = (q_own, g_own, lax.ppermute(text_peer, "ctx", swap_core))

        came = [along_z(part, dz) for dz, part in enumerate(carry)]
        own, far = [], []
        for z in (0, 2):
            here, beside = in_vmem(join_kernel, [(quarter, BF16)] * 2)(
                *came[z : z + 2], text[2], *far
            )
            own += [here, along_x(beside)]
            far += [along_y(here), along_xy(beside)]
        own_ds, own_here, own_beside = sample_pass(
            near_place, 0, n_enc, bias, text, own, [(whole, F32), (whole, BF16)]
        )
        (own_beside,) = hand_on(own_beside, far[2])
        back_x = along_x(own_beside)
        far_ds, *far_grads = sample_pass(
            near_place, 1, n_enc, bias, text, far, [(quarter, BF16)] * 4, (own_beside,)
        )
        dq = text_grads(near_place, n_enc, text, (own, far), (own_ds, far_ds))
        returned = [None] * n_z
        for z in (2, 0):
            here, beside = far_grads[z : z + 2]
            back_y = along_y(here)
            totals = in_vmem(functools.partial(add_kernel, z), [(pair, BF16)] * 2)(
                own_here, back_x, back_y, along_xy(beside)
            )
            for dz, total in enumerate(totals, z):
                returned[dz] = along_z(total, dz)
            if z:
                sent = totals[0]
        dq_parts = in_vmem(split_rows_kernel, [((tokens // DQ_PARTS, HALF_QCOLS), BF16)] * DQ_PARTS)(
            dq[1], sent, totals[0]
        )
        dq_got = [lax.ppermute(part, "ctx", swap_core) for part in dq_parts]
    else:
        both = ("ctx", "enc")
        same_y = [
            [yy * CORES * n_enc + i for i in range(CORES * n_enc)] for yy in range(n_y)
        ]
        same_column = [
            [(yy * CORES + c) * n_enc + e for yy in range(n_y)]
            for c in range(CORES)
            for e in range(n_enc)
        ]
        core = core_of()

        def exchange(parts):
            return lax.all_to_all(
                parts, both, split_axis=0, concat_axis=0, axis_index_groups=same_y, tiled=True
            )

        def to_groups(owned):
            parts = owned.reshape(n_enc, slots, CORES, HALF_KCOLS).transpose(2, 0, 1, 3)
            got = exchange(parts.reshape(CORES * n_enc, slots, HALF_KCOLS))
            got = got.reshape(CORES * n_enc * slots, HALF_KCOLS)
            return lax.all_gather(got, both, axis=0, axis_index_groups=same_column, tiled=True)

        def to_owners(grads):
            grads = lax.psum_scatter(
                grads, both, scatter_dimension=0, axis_index_groups=same_column, tiled=True
            )
            got = exchange(grads.reshape(CORES * n_enc, slots, HALF_KCOLS))
            got = got.reshape(CORES, n_enc, slots, HALF_KCOLS).transpose(1, 2, 0, 3)
            return got.reshape(n_enc, slots, CORES * HALF_KCOLS)

        def no_place():
            return jnp.int32(0), jnp.int32(0)

        all_k = to_groups(img_k)
        all_v = to_groups(img_v)
        text_peer, q_own, g_own, bias = split_the_text(1, 1, no_place)
        text = (q_own, g_own, lax.ppermute(text_peer, "ctx", swap_core))
        kvs = [
            jnp.concatenate([part[s * SLOT_ROWS : (s + 1) * SLOT_ROWS] for part in (all_k, all_v)], axis=0)
            for s in range(SAMP)
        ]
        all_ds, grads = [], []
        for sample, kv in enumerate(kvs):
            ds, grad = sample_pass(no_place, sample, 1, bias, text, [kv], [(kv.shape, BF16)])
            all_ds.append(ds)
            grads.append(grad)
        dq = text_grads(no_place, 1, text, [[kv] for kv in kvs], all_ds)
        d_img_k = to_owners(jnp.concatenate([g[:SLOT_ROWS] for g in grads], axis=0))
        d_img_v = to_owners(jnp.concatenate([g[SLOT_ROWS:] for g in grads], axis=0))
        dq_got = [lax.ppermute(dq[1], "ctx", swap_core)]

    d_queries, token = local_call(
        finish_text_kernel,
        [IN_VMEM] * (1 + len(dq_got)),
        [(queries.shape, BF16, IN_HBM), ((8, HD), F32, IN_VMEM)],
        [pltpu.SemaphoreType.DMA((1 + len(dq_got),))],
    )(dq[0], *dq_got)
    if near:
        far_rows = in_vmem(
            functools.partial(far_rows_kernel, slots),
            [((2, n_enc // 2, slots, HALF_KCOLS), BF16)] * 2,
        )(*returned[2:])
        mine, for_peer = in_vmem(
            functools.partial(owner_rows_kernel, slots),
            [(kv_halves, BF16)] * 2,
        )(*returned[:2], *far_rows)
        d_img_k, d_img_v = local_call(
            finish_kernel,
            [IN_VMEM] * 3,
            [(img_k.shape, BF16, IN_HBM)] * 2,
            [pltpu.SemaphoreType.DMA((4,))],
        )(mine, lax.ppermute(for_peer, "ctx", swap_core), token)
    return (d_queries, d_img_k, d_img_v)


def solution(mesh):
    in_specs = (
        P("enc", "ctx", None),
        P("enc", "ctx", None),
        P("enc", "ctx"),
        P("enc", None),
        P(None, ("ctx", "enc"), None),
        P(None, ("ctx", "enc"), None),
    )
    out_specs = (
        P("enc", "ctx", None),
        P(None, ("ctx", "enc"), None),
        P(None, ("ctx", "enc"), None),
    )
    body = functools.partial(shards, mesh.shape["ctx"], mesh.shape["enc"])
    return jax.shard_map(body, mesh=mesh, in_specs=in_specs, out_specs=out_specs, check_vma=False)
```

profile of v0, /device:TPU:0, one launch (start us, length us, event | category | flops | bytes accessed | tf_op | source)
XLA Modules:
  0.0 57.4 jit_solution(8132251792179585881)
XLA Ops:
  0.6 1.1 %shard_map.86 = (bf16[2,8,16,512]{3,2,1,0:T(8,128)(2,1)S(1)}, bf16[2,8,16,512]{3,2,1,0:T(8,128)(2,1)S(1)}) custom-call(bf16[8,16,1024]{2,1,0:T(8,128)(2,1)} %k_ref.1, bf16[8,16,1024]{2,1,0:T(8,128)(2,1)} %v_ref.1), custom_call_target="tpu_custom_call" | custom-call | bytes 524288 | tf_op jit(solution)/shard_map/pallas_call | solution.py:429
  1.8 0.5 collective-permute-start
  2.3 1.6 %shard_map.85 = (bf16[272,2048]{1,0:T(8,128)(2,1)S(1)}, bf16[144,2048]{1,0:T(8,128)(2,1)S(1)}, bf16[128,2048]{1,0:T(8,128)(2,1)S(1)}, f32[2,256,128]{2,1,0:T(8,128)S(1)}) custom-call(bf16[1,128,4096]{2,1,0:T(8,128)(2,1)} %q_ref.1, bf16[1,128,4096]{2,1,0:T(8,128)(2,1)} %g_ref.1, s32[1,128]{1,0:T(1,128)} %samp_hbm.1, s32[1,2]{1,0:T(1,128)} %tiles_hbm.1), custom_call_target="tpu_custom_call" | custom-call | bytes 4194304 | tf_op jit(solution)/shard_map/pallas_call | solution.py:390
  3.9 0.0 collective-permute-done.got
  3.9 0.1 shard_map.87
  4.0 0.1 collective-permute-start.1
  4.1 3.0 %collective-permute-start.2 = (bf16[2,64,512]{2,1,0:T(8,128)(2,1)S(1)}, bf16[2,64,512]{2,1,0:T(8,128)(2,1)S(1)}, u32[]{:S(2)}, u32[]{:S(2)}) collective-permute-start(bf16[2,64,512]{2,1,0:T(8,128)(2,1)S(1)} %get-tuple-element.48), channel_id=1, source_target_pairs={{0,2},{1,3},{2,0},{3,1},{4,6},{5,7},{6,4},{7,5},{8,10},{9,11},{10,... | collective-permute-start | bytes 393224 | tf_op jit(solution)/shard_map/ppermute | solution.py:418
  7.1 2.6 %collective-permute-start.4 = (bf16[2,64,512]{2,1,0:T(8,128)(2,1)S(1)}, bf16[2,64,512]{2,1,0:T(8,128)(2,1)S(1)}, u32[]{:S(2)}, u32[]{:S(2)}) collective-permute-start(bf16[2,64,512]{2,1,0:T(8,128)(2,1)S(1)} %get-tuple-element.51), channel_id=1, source_target_pairs={{0,4},{1,5},{2,6},{3,7},{4,0},{5,1},{6,2},{7,3},{8,12},{9,13},{10,... | collective-permute-start | bytes 393224 | tf_op jit(solution)/shard_map/ppermute | solution.py:418
  9.7 0.0 collective-permute-start.5
  9.7 3.0 %collective-permute-done.2.refs_1_ = bf16[2,64,512]{2,1,0:T(8,128)(2,1)S(1)} collective-permute-done((bf16[2,64,512]{2,1,0:T(8,128)(2,1)S(1)}, bf16[2,64,512]{2,1,0:T(8,128)(2,1)S(1)}, u32[]{:S(2)}, u32[]{:S(2)}) %collective-permute-start.2) | collective-permute-done | bytes 131104 | tf_op jit(solution)/shard_map/ppermute | solution.py:418
  12.7 0.0 collective-permute-done.1.refs_2_.got
  12.7 1.8 %collective-permute-start.6 = (bf16[128,512]{1,0:T(8,128)(2,1)S(1)}, bf16[128,512]{1,0:T(8,128)(2,1)S(1)}, u32[]{:S(2)}, u32[]{:S(2)}) collective-permute-start(bf16[128,512]{1,0:T(8,128)(2,1)S(1)} %get-tuple-element.49.rest_0_), channel_id=1, source_target_pairs={{0,16},{8,24},{16,0},{24,8},{1,17},{9,25},{17,1},{25,9},{2,18},{10... | collective-permute-start | bytes 393224 | tf_op jit(solution)/shard_map/ppermute | solution.py:424
  14.5 1.4 %collective-permute-start.7 = (bf16[128,512]{1,0:T(8,128)(2,1)S(1)}, bf16[128,512]{1,0:T(8,128)(2,1)S(1)}, u32[]{:S(2)}, u32[]{:S(2)}) collective-permute-start(bf16[128,512]{1,0:T(8,128)(2,1)S(1)} %get-tuple-element.50), channel_id=1, source_target_pairs={{0,17},{1,16},{2,19},{3,18},{4,21},{5,20},{6,23},{7,22},{8,25},{9,... | collective-permute-start | bytes 393224 | tf_op jit(solution)/shard_map/ppermute | solution.py:427
  15.9 0.3 collective-permute-start.3
  16.3 3.8 %collective-permute-done.4.refs_0_ = bf16[2,64,512]{2,1,0:T(8,128)(2,1)S(1)} collective-permute-done((bf16[2,64,512]{2,1,0:T(8,128)(2,1)S(1)}, bf16[2,64,512]{2,1,0:T(8,128)(2,1)S(1)}, u32[]{:S(2)}, u32[]{:S(2)}) %collective-permute-start.4) | collective-permute-done | bytes 131104 | tf_op jit(solution)/shard_map/ppermute | solution.py:418
  20.0 0.0 collective-permute-done.5.refs_1_
  20.0 0.0 collective-permute-done.6.refs_3_.rest_0_.rest_4_
  20.0 0.3 collective-permute-done.7.refs_4_.rest_1_.rest_5_
  20.4 1.6 %collective-permute-start.8 = (bf16[128,512]{1,0:T(8,128)(2,1)S(1)}, bf16[128,512]{1,0:T(8,128)(2,1)S(1)}, u32[]{:S(2)}, u32[]{:S(2)}) collective-permute-start(bf16[128,512]{1,0:T(8,128)(2,1)S(1)} %get-tuple-element.54), channel_id=1, source_target_pairs={{0,1},{1,0},{2,3},{3,2},{4,5},{5,4},{6,7},{7,6},{8,9},{9,8},{10,11... | collective-permute-start | bytes 393224 | tf_op jit(solution)/shard_map/ppermute | solution.py:421
  22.0 1.2 %collective-permute-start.9 = (bf16[128,512]{1,0:T(8,128)(2,1)S(1)}, bf16[128,512]{1,0:T(8,128)(2,1)S(1)}, u32[]{:S(2)}, u32[]{:S(2)}) collective-permute-start(bf16[128,512]{1,0:T(8,128)(2,1)S(1)} %get-tuple-element.53.rest_2_), channel_id=1, source_target_pairs={{0,16},{8,24},{16,0},{24,8},{1,17},{9,25},{17,1},{25,9},{2,18},{10... | collective-permute-start | bytes 393224 | tf_op jit(solution)/shard_map/ppermute | solution.py:424
  23.1 0.8 %collective-permute-start.10 = (bf16[128,512]{1,0:T(8,128)(2,1)S(1)}, bf16[128,512]{1,0:T(8,128)(2,1)S(1)}, u32[]{:S(2)}, u32[]{:S(2)}) collective-permute-start(bf16[128,512]{1,0:T(8,128)(2,1)S(1)} %get-tuple-element.54), channel_id=1, source_target_pairs={{0,17},{1,16},{2,19},{3,18},{4,21},{5,20},{6,23},{7,22},{8,25},{9,... | collective-permute-start | bytes 393224 | tf_op jit(solution)/shard_map/ppermute | solution.py:427
  24.0 1.9 %collective-permute-done.8.rest_3_ = bf16[128,512]{1,0:T(8,128)(2,1)S(1)} collective-permute-done((bf16[128,512]{1,0:T(8,128)(2,1)S(1)}, bf16[128,512]{1,0:T(8,128)(2,1)S(1)}, u32[]{:S(2)}, u32[]{:S(2)}) %collective-permute-start.8) | collective-permute-done | bytes 131104 | tf_op jit(solution)/shard_map/ppermute | solution.py:421
  25.9 2.6 %shard_map.90 = (bf16[4,256,1024]{2,1,0:T(8,128)(2,1)S(1)}, f32[256,512]{1,0:T(8,128)S(1)}, bf16[256,512]{1,0:T(8,128)(2,1)S(1)}) custom-call(f32[2,256,128]{2,1,0:T(8,128)S(1)} %get-tuple-element.55.bias, bf16[144,2048]{1,0:T(8,128)(2,1)S(1)} %get-tuple-element.42.q_a, bf16[128,2048]{1,0:T(8,128)(2,1)S(1)} %get-tuple-element.56.g_a, ...), custom_call_target="tpu_custom_call" | custom-call | flops 1073741824 | bytes 16777216 | tf_op jit(solution)/shard_map/pallas_call | solution.py:55
  28.5 0.0 collective-permute-done.9.refs_1_.rest_2_.rest_6_
  28.5 2.9 %collective-permute-start.11 = (bf16[256,512]{1,0:T(8,128)(2,1)S(1)}, bf16[256,512]{1,0:T(8,128)(2,1)S(1)}, u32[]{:S(2)}, u32[]{:S(2)}) collective-permute-start(bf16[256,512]{1,0:T(8,128)(2,1)S(1)} %shard_map.91.rest_4_), channel_id=1, source_target_pairs={{0,1},{1,0},{2,3},{3,2},{4,5},{5,4},{6,7},{7,6},{8,9},{9,8},{10,11... | collective-permute-start | bytes 786440 | tf_op jit(solution)/shard_map/ppermute | solution.py:421
  31.4 4.6 %shard_map.92 = (bf16[4,256,1024]{2,1,0:T(8,128)(2,1)S(1)}, bf16[128,512]{1,0:T(8,128)(2,1)S(1)}, bf16[128,512]{1,0:T(8,128)(2,1)S(1)}, bf16[128,512]{1,0:T(8,128)(2,1)S(1)}, bf16[128,512]{1,0:T(8,128)(2,1)S(1)}) custom-call(f32[2,256,128]{2,1,0:T(8,128)S(1)} %get-tuple-element.55.bias, bf16[144,2048]{1,0:T(8,128)(2,1)S(1)} %get-tuple-element.42.q_a, ...), custom_call_target="tpu_custom_call" | custom-call | flops 1073741824 | bytes 16777216 | tf_op jit(solution)/shard_map/pallas_call | solution.py:55
  36.0 0.1 collective-permute-start.12
  36.1 2.0 %collective-permute-start.13 = (bf16[128,512]{1,0:T(8,128)(2,1)S(1)}, bf16[128,512]{1,0:T(8,128)(2,1)S(1)}, u32[]{:S(2)}, u32[]{:S(2)}) collective-permute-start(bf16[128,512]{1,0:T(8,128)(2,1)S(1)} %get-tuple-element.64), channel_id=1, source_target_pairs={{0,17},{1,16},{2,19},{3,18},{4,21},{5,20},{6,23},{7,22},{8,25},{9,... | collective-permute-start | bytes 393224 | tf_op jit(solution)/shard_map/ppermute | solution.py:427
  38.1 1.9 %collective-permute-start.14 = (bf16[128,512]{1,0:T(8,128)(2,1)S(1)}, bf16[128,512]{1,0:T(8,128)(2,1)S(1)}, u32[]{:S(2)}, u32[]{:S(2)}) collective-permute-start(bf16[128,512]{1,0:T(8,128)(2,1)S(1)} %get-tuple-element.66), channel_id=1, source_target_pairs={{0,16},{8,24},{16,0},{24,8},{1,17},{9,25},{17,1},{25,9},{2,18},{10... | collective-permute-start | bytes 393224 | tf_op jit(solution)/shard_map/ppermute | solution.py:424
  40.0 1.0 %collective-permute-start.15 = (bf16[128,512]{1,0:T(8,128)(2,1)S(1)}, bf16[128,512]{1,0:T(8,128)(2,1)S(1)}, u32[]{:S(2)}, u32[]{:S(2)}) collective-permute-start(bf16[128,512]{1,0:T(8,128)(2,1)S(1)} %get-tuple-element.67), channel_id=1, source_target_pairs={{0,17},{1,16},{2,19},{3,18},{4,21},{5,20},{6,23},{7,22},{8,25},{9,... | collective-permute-start | bytes 393224 | tf_op jit(solution)/shard_map/ppermute | solution.py:427
  41.0 2.4 %collective-permute-done.12.back_y = bf16[128,512]{1,0:T(8,128)(2,1)S(1)} collective-permute-done((bf16[128,512]{1,0:T(8,128)(2,1)S(1)}, bf16[128,512]{1,0:T(8,128)(2,1)S(1)}, u32[]{:S(2)}, u32[]{:S(2)}) %collective-permute-start.12) | collective-permute-done | bytes 131104 | tf_op jit(solution)/shard_map/ppermute | solution.py:424
  43.4 0.0 collective-permute-done.13.back_xy
  43.5 0.1 shard_map.94
  43.5 2.7 %collective-permute-start.19 = (bf16[2,64,512]{2,1,0:T(8,128)(2,1)S(1)}, bf16[2,64,512]{2,1,0:T(8,128)(2,1)S(1)}, u32[]{:S(2)}, u32[]{:S(2)}) collective-permute-start(bf16[2,64,512]{2,1,0:T(8,128)(2,1)S(1)} %get-tuple-element.65.refs_0_), channel_id=1, source_target_pairs={{0,4},{1,5},{2,6},{3,7},{4,0},{5,1},{6,2},{7,3},{8,12},{9,13},{10,... | collective-permute-start | bytes 393224 | tf_op jit(solution)/shard_map/ppermute | solution.py:418
  46.2 2.8 %collective-permute-start.20 = (bf16[2,64,512]{2,1,0:T(8,128)(2,1)S(1)}, bf16[2,64,512]{2,1,0:T(8,128)(2,1)S(1)}, u32[]{:S(2)}, u32[]{:S(2)}) collective-permute-start(bf16[2,64,512]{2,1,0:T(8,128)(2,1)S(1)} %get-tuple-element.73), channel_id=1, source_target_pairs={{0,6},{1,7},{2,4},{3,5},{4,2},{5,3},{6,0},{7,1},{8,14},{9,15},{10,... | collective-permute-start | bytes 393224 | tf_op jit(solution)/shard_map/ppermute | solution.py:418
  49.0 0.1 shard_map.95
  49.1 0.6 collective-permute-start.18
  49.7 1.4 %shard_map.93 = (bf16[128,2048]{1,0:T(8,128)(2,1)S(1)}, bf16[128,2048]{1,0:T(8,128)(2,1)S(1)}) custom-call(bf16[144,2048]{1,0:T(8,128)(2,1)S(1)} %get-tuple-element.42.q_a, bf16[272,2048]{1,0:T(8,128)(2,1)S(1)} %collective-permute-done.1.refs_2_.got, bf16[128,512]{1,0:T(8,128)(2,1)S(1)} %get-tuple-element.49.rest_0_, ...), custom_call_target="tpu_custom_call" | custom-call | flops 536870912 | bytes 8388608 | tf_op jit(solution)/shard_map/pallas_call | solution.py:55
  51.2 0.1 collective-permute-start.16
  51.2 0.5 collective-permute-start.17
  51.7 0.0 collective-permute-done.19.refs_0_
  51.7 1.6 %collective-permute-done.20.refs_1_ = bf16[2,64,512]{2,1,0:T(8,128)(2,1)S(1)} collective-permute-done((bf16[2,64,512]{2,1,0:T(8,128)(2,1)S(1)}, bf16[2,64,512]{2,1,0:T(8,128)(2,1)S(1)}, u32[]{:S(2)}, u32[]{:S(2)}) %collective-permute-start.20) | collective-permute-done | bytes 131104 | tf_op jit(solution)/shard_map/ppermute | solution.py:418
  53.4 1.3 %collective-permute-done.18.refs_1_ = bf16[2,64,512]{2,1,0:T(8,128)(2,1)S(1)} collective-permute-done((bf16[2,64,512]{2,1,0:T(8,128)(2,1)S(1)}, bf16[2,64,512]{2,1,0:T(8,128)(2,1)S(1)}, u32[]{:S(2)}, u32[]{:S(2)}) %collective-permute-start.18) | collective-permute-done | bytes 131104 | tf_op jit(solution)/shard_map/ppermute | solution.py:418
  54.8 0.1 collective-permute-start.21
  54.9 0.0 collective-permute-done.16.refs_0_
  54.9 1.0 %shard_map.97 = (bf16[1,128,4096]{2,1,0:T(8,128)(2,1)}, f32[8,128]{1,0:T(8,128)S(1)}) custom-call(bf16[128,2048]{1,0:T(8,128)(2,1)S(1)} %get-tuple-element.60.mine, bf16[64,2048]{1,0:T(8,128)(2,1)S(1)} %collective-permute-done.16.refs_0_, bf16[64,2048]{1,0:T(8,128)(2,1)S(1)} %collective-permute-done.17.refs_1_), custom_call_target="tpu_custom_call" | custom-call | bytes 524288 | tf_op jit(solution)/shard_map/pallas_call | solution.py:527
  55.9 0.5 collective-permute-done.21.got
  56.4 0.8 %shard_map.100 = (bf16[8,16,1024]{2,1,0:T(8,128)(2,1)}, bf16[8,16,1024]{2,1,0:T(8,128)(2,1)}) custom-call(bf16[2,8,16,512]{3,2,1,0:T(8,128)(2,1)S(1)} %get-tuple-element.76.mine, bf16[2,8,16,512]{3,2,1,0:T(8,128)(2,1)S(1)} %collective-permute-done.21.got, f32[8,128]{1,0:T(8,128)S(1)} %get-tuple-element.78._), custom_call_target="tpu_custom_call" | custom-call | bytes 524288 | tf_op jit(solution)/shard_map/pallas_call | solution.py:542
  (12 shorter events, 0.2 us)
Async XLA Ops:
  1.8 2.1 %collective-permute-start = (bf16[2,8,16,512]{3,2,1,0:T(8,128)(2,1)S(1)}, bf16[2,8,16,512]{3,2,1,0:T(8,128)(2,1)S(1)}, u32[]{:S(2)}, u32[]{:S(2)}) collective-permute-start(bf16[2,8,16,512]{3,2,1,0:T(8,128)(2,1)S(1)} %get-tuple-element.44), channel_id=1, source_target_pairs={{0,8},{8,0},{16,24},{24,16},{1,9},{9,1},{17,25},{25,17},{2,10},{10... | collective-permute-start | bytes 786440 | tf_op jit(solution)/shard_map/ppermute | solution.py:440
  4.0 8.7 %collective-permute-start.1 = (bf16[272,2048]{1,0:T(8,128)(2,1)S(1)}, bf16[272,2048]{1,0:T(8,128)(2,1)S(1)}, u32[]{:S(2)}, u32[]{:S(2)}) collective-permute-start(bf16[272,2048]{1,0:T(8,128)(2,1)S(1)} %get-tuple-element.46), channel_id=1, source_target_pairs={{0,8},{8,0},{16,24},{24,16},{1,9},{9,1},{17,25},{25,17},{2,10},{10... | collective-permute-start | bytes 3342344 | tf_op jit(solution)/shard_map/ppermute | solution.py:441
  4.1 8.6 %collective-permute-start.2 = (bf16[2,64,512]{2,1,0:T(8,128)(2,1)S(1)}, bf16[2,64,512]{2,1,0:T(8,128)(2,1)S(1)}, u32[]{:S(2)}, u32[]{:S(2)}) collective-permute-start(bf16[2,64,512]{2,1,0:T(8,128)(2,1)S(1)} %get-tuple-element.48), channel_id=1, source_target_pairs={{0,2},{1,3},{2,0},{3,1},{4,6},{5,7},{6,4},{7,5},{8,10},{9,11},{10,... | collective-permute-start | bytes 393224 | tf_op jit(solution)/shard_map/ppermute | solution.py:418
  7.1 12.9 %collective-permute-start.4 = (bf16[2,64,512]{2,1,0:T(8,128)(2,1)S(1)}, bf16[2,64,512]{2,1,0:T(8,128)(2,1)S(1)}, u32[]{:S(2)}, u32[]{:S(2)}) collective-permute-start(bf16[2,64,512]{2,1,0:T(8,128)(2,1)S(1)} %get-tuple-element.51), channel_id=1, source_target_pairs={{0,4},{1,5},{2,6},{3,7},{4,0},{5,1},{6,2},{7,3},{8,12},{9,13},{10,... | collective-permute-start | bytes 393224 | tf_op jit(solution)/shard_map/ppermute | solution.py:418
  9.7 10.3 %collective-permute-start.5 = (bf16[2,64,512]{2,1,0:T(8,128)(2,1)S(1)}, bf16[2,64,512]{2,1,0:T(8,128)(2,1)S(1)}, u32[]{:S(2)}, u32[]{:S(2)}) collective-permute-start(bf16[2,64,512]{2,1,0:T(8,128)(2,1)S(1)} %get-tuple-element.52), channel_id=1, source_target_pairs={{0,6},{1,7},{2,4},{3,5},{4,2},{5,3},{6,0},{7,1},{8,14},{9,15},{10,... | collective-permute-start | bytes 393224 | tf_op jit(solution)/shard_map/ppermute | solution.py:418
  12.7 7.3 %collective-permute-start.6 = (bf16[128,512]{1,0:T(8,128)(2,1)S(1)}, bf16[128,512]{1,0:T(8,128)(2,1)S(1)}, u32[]{:S(2)}, u32[]{:S(2)}) collective-permute-start(bf16[128,512]{1,0:T(8,128)(2,1)S(1)} %get-tuple-element.49.rest_0_), channel_id=1, source_target_pairs={{0,16},{8,24},{16,0},{24,8},{1,17},{9,25},{17,1},{25,9},{2,18},{10... | collective-permute-start | bytes 393224 | tf_op jit(solution)/shard_map/ppermute | solution.py:424
  14.5 5.9 %collective-permute-start.7 = (bf16[128,512]{1,0:T(8,128)(2,1)S(1)}, bf16[128,512]{1,0:T(8,128)(2,1)S(1)}, u32[]{:S(2)}, u32[]{:S(2)}) collective-permute-start(bf16[128,512]{1,0:T(8,128)(2,1)S(1)} %get-tuple-element.50), channel_id=1, source_target_pairs={{0,17},{1,16},{2,19},{3,18},{4,21},{5,20},{6,23},{7,22},{8,25},{9,... | collective-permute-start | bytes 393224 | tf_op jit(solution)/shard_map/ppermute | solution.py:427
  15.9 8.0 %collective-permute-start.3 = (bf16[128,512]{1,0:T(8,128)(2,1)S(1)}, bf16[128,512]{1,0:T(8,128)(2,1)S(1)}, u32[]{:S(2)}, u32[]{:S(2)}) collective-permute-start(bf16[128,512]{1,0:T(8,128)(2,1)S(1)} %get-tuple-element.50), channel_id=1, source_target_pairs={{0,1},{1,0},{2,3},{3,2},{4,5},{5,4},{6,7},{7,6},{8,9},{9,8},{10,11... | collective-permute-start | bytes 393224 | tf_op jit(solution)/shard_map/ppermute | solution.py:421
  20.4 5.5 %collective-permute-start.8 = (bf16[128,512]{1,0:T(8,128)(2,1)S(1)}, bf16[128,512]{1,0:T(8,128)(2,1)S(1)}, u32[]{:S(2)}, u32[]{:S(2)}) collective-permute-start(bf16[128,512]{1,0:T(8,128)(2,1)S(1)} %get-tuple-element.54), channel_id=1, source_target_pairs={{0,1},{1,0},{2,3},{3,2},{4,5},{5,4},{6,7},{7,6},{8,9},{9,8},{10,11... | collective-permute-start | bytes 393224 | tf_op jit(solution)/shard_map/ppermute | solution.py:421
  22.0 6.5 %collective-permute-start.9 = (bf16[128,512]{1,0:T(8,128)(2,1)S(1)}, bf16[128,512]{1,0:T(8,128)(2,1)S(1)}, u32[]{:S(2)}, u32[]{:S(2)}) collective-permute-start(bf16[128,512]{1,0:T(8,128)(2,1)S(1)} %get-tuple-element.53.rest_2_), channel_id=1, source_target_pairs={{0,16},{8,24},{16,0},{24,8},{1,17},{9,25},{17,1},{25,9},{2,18},{10... | collective-permute-start | bytes 393224 | tf_op jit(solution)/shard_map/ppermute | solution.py:424
  23.1 8.3 %collective-permute-start.10 = (bf16[128,512]{1,0:T(8,128)(2,1)S(1)}, bf16[128,512]{1,0:T(8,128)(2,1)S(1)}, u32[]{:S(2)}, u32[]{:S(2)}) collective-permute-start(bf16[128,512]{1,0:T(8,128)(2,1)S(1)} %get-tuple-element.54), channel_id=1, source_target_pairs={{0,17},{1,16},{2,19},{3,18},{4,21},{5,20},{6,23},{7,22},{8,25},{9,... | collective-permute-start | bytes 393224 | tf_op jit(solution)/shard_map/ppermute | solution.py:427
  28.5 15.0 %collective-permute-start.11 = (bf16[256,512]{1,0:T(8,128)(2,1)S(1)}, bf16[256,512]{1,0:T(8,128)(2,1)S(1)}, u32[]{:S(2)}, u32[]{:S(2)}) collective-permute-start(bf16[256,512]{1,0:T(8,128)(2,1)S(1)} %shard_map.91.rest_4_), channel_id=1, source_target_pairs={{0,1},{1,0},{2,3},{3,2},{4,5},{5,4},{6,7},{7,6},{8,9},{9,8},{10,11... | collective-permute-start | bytes 786440 | tf_op jit(solution)/shard_map/ppermute | solution.py:421
  36.0 7.4 %collective-permute-start.12 = (bf16[128,512]{1,0:T(8,128)(2,1)S(1)}, bf16[128,512]{1,0:T(8,128)(2,1)S(1)}, u32[]{:S(2)}, u32[]{:S(2)}) collective-permute-start(bf16[128,512]{1,0:T(8,128)(2,1)S(1)} %get-tuple-element.63), channel_id=1, source_target_pairs={{0,16},{8,24},{16,0},{24,8},{1,17},{9,25},{17,1},{25,9},{2,18},{10... | collective-permute-start | bytes 393224 | tf_op jit(solution)/shard_map/ppermute | solution.py:424
  36.1 7.4 %collective-permute-start.13 = (bf16[128,512]{1,0:T(8,128)(2,1)S(1)}, bf16[128,512]{1,0:T(8,128)(2,1)S(1)}, u32[]{:S(2)}, u32[]{:S(2)}) collective-permute-start(bf16[128,512]{1,0:T(8,128)(2,1)S(1)} %get-tuple-element.64), channel_id=1, source_target_pairs={{0,17},{1,16},{2,19},{3,18},{4,21},{5,20},{6,23},{7,22},{8,25},{9,... | collective-permute-start | bytes 393224 | tf_op jit(solution)/shard_map/ppermute | solution.py:427
  38.1 11.0 %collective-permute-start.14 = (bf16[128,512]{1,0:T(8,128)(2,1)S(1)}, bf16[128,512]{1,0:T(8,128)(2,1)S(1)}, u32[]{:S(2)}, u32[]{:S(2)}) collective-permute-start(bf16[128,512]{1,0:T(8,128)(2,1)S(1)} %get-tuple-element.66), channel_id=1, source_target_pairs={{0,16},{8,24},{16,0},{24,8},{1,17},{9,25},{17,1},{25,9},{2,18},{10... | collective-permute-start | bytes 393224 | tf_op jit(solution)/shard_map/ppermute | solution.py:424
  40.0 9.0 %collective-permute-start.15 = (bf16[128,512]{1,0:T(8,128)(2,1)S(1)}, bf16[128,512]{1,0:T(8,128)(2,1)S(1)}, u32[]{:S(2)}, u32[]{:S(2)}) collective-permute-start(bf16[128,512]{1,0:T(8,128)(2,1)S(1)} %get-tuple-element.67), channel_id=1, source_target_pairs={{0,17},{1,16},{2,19},{3,18},{4,21},{5,20},{6,23},{7,22},{8,25},{9,... | collective-permute-start | bytes 393224 | tf_op jit(solution)/shard_map/ppermute | solution.py:427
  43.5 8.2 %collective-permute-start.19 = (bf16[2,64,512]{2,1,0:T(8,128)(2,1)S(1)}, bf16[2,64,512]{2,1,0:T(8,128)(2,1)S(1)}, u32[]{:S(2)}, u32[]{:S(2)}) collective-permute-start(bf16[2,64,512]{2,1,0:T(8,128)(2,1)S(1)} %get-tuple-element.65.refs_0_), channel_id=1, source_target_pairs={{0,4},{1,5},{2,6},{3,7},{4,0},{5,1},{6,2},{7,3},{8,12},{9,13},{10,... | collective-permute-start | bytes 393224 | tf_op jit(solution)/shard_map/ppermute | solution.py:418
  46.2 7.2 %collective-permute-start.20 = (bf16[2,64,512]{2,1,0:T(8,128)(2,1)S(1)}, bf16[2,64,512]{2,1,0:T(8,128)(2,1)S(1)}, u32[]{:S(2)}, u32[]{:S(2)}) collective-permute-start(bf16[2,64,512]{2,1,0:T(8,128)(2,1)S(1)} %get-tuple-element.73), channel_id=1, source_target_pairs={{0,6},{1,7},{2,4},{3,5},{4,2},{5,3},{6,0},{7,1},{8,14},{9,15},{10,... | collective-permute-start | bytes 393224 | tf_op jit(solution)/shard_map/ppermute | solution.py:418
  49.1 5.6 %collective-permute-start.18 = (bf16[2,64,512]{2,1,0:T(8,128)(2,1)S(1)}, bf16[2,64,512]{2,1,0:T(8,128)(2,1)S(1)}, u32[]{:S(2)}, u32[]{:S(2)}) collective-permute-start(bf16[2,64,512]{2,1,0:T(8,128)(2,1)S(1)} %get-tuple-element.72), channel_id=1, source_target_pairs={{0,2},{1,3},{2,0},{3,1},{4,6},{5,7},{6,4},{7,5},{8,10},{9,11},{10,... | collective-permute-start | bytes 393224 | tf_op jit(solution)/shard_map/ppermute | solution.py:418
  51.2 3.7 %collective-permute-start.16 = (bf16[64,2048]{1,0:T(8,128)(2,1)S(1)}, bf16[64,2048]{1,0:T(8,128)(2,1)S(1)}, u32[]{:S(2)}, u32[]{:S(2)}) collective-permute-start(bf16[64,2048]{1,0:T(8,128)(2,1)S(1)} %get-tuple-element.69), channel_id=1, source_target_pairs={{0,8},{8,0},{16,24},{24,16},{1,9},{9,1},{17,25},{25,17},{2,10},{10... | collective-permute-start | bytes 786440 | tf_op jit(solution)/shard_map/ppermute | solution.py:474
  51.2 3.6 %collective-permute-start.17 = (bf16[64,2048]{1,0:T(8,128)(2,1)S(1)}, bf16[64,2048]{1,0:T(8,128)(2,1)S(1)}, u32[]{:S(2)}, u32[]{:S(2)}) collective-permute-start(bf16[64,2048]{1,0:T(8,128)(2,1)S(1)} %get-tuple-element.70), channel_id=1, source_target_pairs={{0,8},{8,0},{16,24},{24,16},{1,9},{9,1},{17,25},{25,17},{2,10},{10... | collective-permute-start | bytes 786440 | tf_op jit(solution)/shard_map/ppermute | solution.py:474
  54.8 1.6 %collective-permute-start.21 = (bf16[2,8,16,512]{3,2,1,0:T(8,128)(2,1)S(1)}, bf16[2,8,16,512]{3,2,1,0:T(8,128)(2,1)S(1)}, u32[]{:S(2)}, u32[]{:S(2)}) collective-permute-start(bf16[2,8,16,512]{3,2,1,0:T(8,128)(2,1)S(1)} %get-tuple-element.77), channel_id=1, source_target_pairs={{0,8},{8,0},{16,24},{24,16},{1,9},{9,1},{17,25},{25,17},{2,10},{10... | collective-permute-start | bytes 786440 | tf_op jit(solution)/shard_map/ppermute | solution.py:547
where the time goes:
time: 58.2 us; the launch traced here: 57.4 us
  starting transfers between devices  28 us (48%)
  waiting for transfers between devices  14.9 us (26%)
  Pallas kernels  13.5 us (23%)
  between operations  0.96 us (2%)
    ppermute x6, starting transfers between devices, along_z(): lax.ppermute(part, 'enc', [(i, i ^ 2 * dz) for i in range(n_enc)])  11.7 us
    ppermute x6, waiting for transfers between devices, along_z(): lax.ppermute(part, 'enc', [(i, i ^ 2 * dz) for i in range(n_enc)])  9.7 us
    pallas_call x12, Pallas kernels, call(): return local_call(body, [IN_VMEM] * len(args), spec, **more)(*args)  8.91 us
    ppermute x4, starting transfers between devices, along_xy(): return lax.ppermute(part, ('ctx', 'enc'), swap_xy)  5.23 us
    ppermute x4, starting transfers between devices, along_y(): return lax.ppermute(part, 'ctx', swap_y)  5.01 us
    ppermute x3, starting transfers between devices, along_x(): return lax.ppermute(part, 'enc', swap_x)  4.8 us
    ppermute x4, waiting for transfers between devices, along_y(): return lax.ppermute(part, 'ctx', swap_y)  2.42 us
    ppermute x3, waiting for transfers between devices, along_x(): return lax.ppermute(part, 'enc', swap_x)  1.93 us
  transfers between devices with their start and end apart: 22, of which 8 were waited for; matrix products, arithmetic and copies ran while one was open for 0% of the time, Pallas kernels for 20%

commit v1 on v0

--- a/solution.py
+++ b/solution.py
@@ -135,7 +135,9 @@
     slot = piece * (SLOT_ROWS // pieces) + owner * slots + lax.rem(line, slots)
     for i in range(SAMP):
         count = jnp.where((sample ^ i) == 0, tiles[0:1, 0:1], tiles[0:1, 1:2])
-        bias[i] = jnp.where(slot < count * TILE_TOK, 0.0, BIG_NEGATIVE)
+        masked = jnp.where(slot < count * TILE_TOK, 0.0, BIG_NEGATIVE)
+        first = lax.broadcasted_iota(jnp.int32, masked.shape, 1) == 0
+        bias[i] = jnp.where(first, masked, 0.0).astype(BF16)
     for copy in copies[2:]:
         copy.wait()
 
@@ -162,16 +164,17 @@
 
 def block_place(b, n_outs):
     half, x, z = b // 4, b // 2 % 2, b % 2
-    return {1: (0, b), 2: (x, 2 * half + z), 4: (2 * half + x, z)}[n_outs]
-
-
-def add_kernel(z, own, back_x, back_y, back_xy, *outs):
+    whole = 2 * half + z
+    return {1: (0, b), 3: (1 + half, z) if x else (0, whole), 4: (2 * half + x, z)}[n_outs]
+
+
+def add_kernel(z, own, back_y, back_xy, back_x, *outs):
     rows = outs[0].shape[1]
     for dz, out in enumerate(outs):
-        near = slice((z + dz) * rows, (z + dz + 1) * rows)
-        far = slice(dz * rows, (dz + 1) * rows)
-        for dx, (here, back) in enumerate(((own, back_y), (back_x, back_xy))):
-            out[dx] = (here[near, :].astype(F32) + back[far, :].astype(F32)).astype(out.dtype)
+        whole = slice((z + dz) * rows, (z + dz + 1) * rows)
+        part = slice(dz * rows, (dz + 1) * rows)
+        out[0] = (own[whole, :] + back_y[part, :].astype(F32)).astype(out.dtype)
+        out[1] = (back_x[part, :].astype(F32) + back_xy[part, :].astype(F32)).astype(out.dtype)
 
 
 def nothing_kernel(*refs):
@@ -277,7 +280,8 @@
             return
         mine = jnp.concatenate([rows[t] for t in which for _ in range(RATIO)], axis=1)
         mine = mine == sample.astype(F32)
-        masks = jnp.concatenate([bias[role]] * (len(which) * RATIO), axis=1)
+        masks = bias[role]
+        ones = jnp.ones((len(which) * RATIO * tokens, HD), BF16)
 
         def products(h):
             def stacked(part):
@@ -291,7 +295,12 @@
 
             q, g = stacked(0), stacked(2)
             k, v = (key_rows(kvs, block_rows, first, h) for first in (0, block_rows))
-            s = lax.dot_general(k, q, NT, preferred_element_type=F32)
+            s = lax.dot_general(
+                jnp.concatenate([k, masks], axis=1),
+                jnp.concatenate([q, ones], axis=1),
+                NT,
+                preferred_element_type=F32,
+            )
             gp = lax.dot_general(v, g, NT, preferred_element_type=F32)
             return q, g, s, gp
 
@@ -301,14 +310,14 @@
             q, g, s, gp = ahead
             if early and h + 1 < HALF_KV:
                 ahead = products(h + 1)
-            s = s + masks
             top = jnp.max(s, axis=0, keepdims=True)
             e = jnp.exp2((s - top) * (SCALE * LOG2E))
             total = jnp.sum(e, axis=0, keepdims=True)
             p = e * jnp.where(mine, 1.0 / total, 0.0)
             row_dot = jnp.sum(p * gp, axis=0, keepdims=True)
-            ds = (p * (gp - row_dot)).astype(BF16)
-            dv = jnp.dot(p.astype(BF16), g, preferred_element_type=F32)
+            ph = p.astype(BF16)
+            ds = ph * (gp - row_dot).astype(BF16)
+            dv = jnp.dot(ph, g, preferred_element_type=F32)
             dk = jnp.dot(ds, q, preferred_element_type=F32) * SCALE
             wide = RATIO * tokens
             for i, t in enumerate(which):
@@ -383,7 +392,7 @@
         ((2 * tokens + SAMP_ROWS, HALF_QCOLS), BF16, IN_VMEM),
         ((tokens + SAMP_ROWS, HALF_QCOLS), BF16, IN_VMEM),
         ((tokens, HALF_QCOLS), BF16, IN_VMEM),
-        ((SAMP, SLOT_ROWS, HD), F32, IN_VMEM),
+        ((SAMP, SLOT_ROWS, HD), BF16, IN_VMEM),
     ]
 
     def split_the_text(n_blocks, pieces, where):
@@ -448,21 +457,20 @@
             )
             own += [here, along_x(beside)]
             far += [along_y(here), along_xy(beside)]
-        own_ds, own_here, own_beside = sample_pass(
-            near_place, 0, n_enc, bias, text, own, [(whole, F32), (whole, BF16)]
+        own_ds, own_here, *own_beside = sample_pass(
+            near_place, 0, n_enc, bias, text, own, [(whole, F32)] + [(quarter, BF16)] * 2
         )
-        (own_beside,) = hand_on(own_beside, far[2])
-        back_x = along_x(own_beside)
         far_ds, *far_grads = sample_pass(
-            near_place, 1, n_enc, bias, text, far, [(quarter, BF16)] * 4, (own_beside,)
+            near_place, 1, n_enc, bias, text, far, [(quarter, BF16)] * 4, (own_here,)
         )
         dq = text_grads(near_place, n_enc, text, (own, far), (own_ds, far_ds))
         returned = [None] * n_z
         for z in (2, 0):
             here, beside = far_grads[z : z + 2]
-            back_y = along_y(here)
+            (own_part,) = hand_on(own_beside[z // 2], here)
+            back_y, back_xy, back_x = along_y(here), along_xy(beside), along_x(own_part)
             totals = in_vmem(functools.partial(add_kernel, z), [(pair, BF16)] * 2)(
-                own_here, back_x, back_y, along_xy(beside)
+                own_here, back_y, back_xy, back_x
             )
             for dz, total in enumerate(totals, z):
                 returned[dz] = along_z(total, dz)

time: 58.2 us -> 56.8 us (0.976)
  Pallas kernels: 13.5 us -> 10.2 us
  starting transfers between devices: 28 us -> 29.2 us
  waiting for transfers between devices: 14.9 us -> 16 us
    pallas_call x12 -> x13, Pallas kernels: 8.91 us -> 5.65 us  [call(): return local_call(body, [IN_VMEM] * len(args), spec, **more)(*args)]
    ppermute x6, waiting for transfers between devices: 9.7 us -> 11 us  [along_z(): lax.ppermute(part, 'enc', [(i, i ^ 2 * dz) for i in range(n_enc)])]
    ppermute x4, waiting for transfers between devices: 2.42 us -> 1.33 us  [along_y(): return lax.ppermute(part, 'ctx', swap_y)]
    ppermute x3 -> x4, waiting for transfers between devices: 1.93 us -> 2.83 us  [along_x(): return lax.ppermute(part, 'enc', swap_x)]
    ppermute x6, starting transfers between devices: 11.7 us -> 12.4 us  [along_z(): lax.ppermute(part, 'enc', [(i, i ^ 2 * dz) for i in range(n_enc)])]
    ppermute x3 -> x4, starting transfers between devices: 4.8 us -> 5.49 us  [along_x(): return lax.ppermute(part, 'enc', swap_x)]
  transfers between devices with their start and end apart: 22 -> 23, of which waited for: 8 -> 10; matrix products, arithmetic and copies ran while one was open for 0% -> 0% of each run, Pallas kernels for 20% -> 14%
where the time goes in v1:
time: 56.8 us; the launch traced here: 56.4 us
  starting transfers between devices  29.2 us (51%)
  waiting for transfers between devices  16 us (28%)
  Pallas kernels  10.2 us (18%)
  between operations  0.97 us (2%)
    ppermute x6, starting transfers between devices, along_z(): lax.ppermute(part, 'enc', [(i, i ^ 2 * dz) for i in range(n_enc)])  12.4 us
    ppermute x6, waiting for transfers between devices, along_z(): lax.ppermute(part, 'enc', [(i, i ^ 2 * dz) for i in range(n_enc)])  11 us
    pallas_call x13, Pallas kernels, call(): return local_call(body, [IN_VMEM] * len(args), spec, **more)(*args)  5.65 us
    ppermute x4, starting transfers between devices, along_x(): return lax.ppermute(part, 'enc', swap_x)  5.49 us
    ppermute x4, starting transfers between devices, along_xy(): return lax.ppermute(part, ('ctx', 'enc'), swap_xy)  5.1 us
    ppermute x4, starting transfers between devices, along_y(): return lax.ppermute(part, 'ctx', swap_y)  4.93 us
    ppermute x4, waiting for transfers between devices, along_x(): return lax.ppermute(part, 'enc', swap_x)  2.83 us
    pallas_call x1, Pallas kernels, split_the_text(): local_call(functools.partial(split_text, n_blocks, pieces, where), [IN_HB...  1.6 us
  transfers between devices with their start and end apart: 23, of which 10 were waited for; matrix products, arithmetic and copies ran while one was open for 0% of the time, Pallas kernels for 14%

profile of v1, /device:TPU:0, one launch (start us, length us, event | category | flops | bytes accessed | tf_op | source)
XLA Modules:
  0.0 56.4 jit_solution(17406417258387884973)
XLA Ops:
  0.6 1.1 %shard_map.86 = (bf16[2,8,16,512]{3,2,1,0:T(8,128)(2,1)S(1)}, bf16[2,8,16,512]{3,2,1,0:T(8,128)(2,1)S(1)}) custom-call(bf16[8,16,1024]{2,1,0:T(8,128)(2,1)} %k_ref.1, bf16[8,16,1024]{2,1,0:T(8,128)(2,1)} %v_ref.1), custom_call_target="tpu_custom_call" | custom-call | bytes 524288 | tf_op jit(solution)/shard_map/pallas_call | solution.py:438
  1.8 0.5 collective-permute-start
  2.3 1.6 %shard_map.85 = (bf16[272,2048]{1,0:T(8,128)(2,1)S(1)}, bf16[144,2048]{1,0:T(8,128)(2,1)S(1)}, bf16[128,2048]{1,0:T(8,128)(2,1)S(1)}, bf16[2,256,128]{2,1,0:T(8,128)(2,1)S(1)}) custom-call(bf16[1,128,4096]{2,1,0:T(8,128)(2,1)} %q_ref.1, bf16[1,128,4096]{2,1,0:T(8,128)(2,1)} %g_ref.1, s32[1,128]{1,0:T(1,128)} %samp_hbm.1, s32[1,2]{1,0:T(1,128)} %tiles_hbm.1), custom_call_target="tpu_custom_call" | custom-call | bytes 4194304 | tf_op jit(solution)/shard_map/pallas_call | solution.py:399
  3.9 0.0 collective-permute-done.got
  3.9 0.1 shard_map.87
  4.0 0.1 collective-permute-start.1
  4.1 3.0 %collective-permute-start.2 = (bf16[2,64,512]{2,1,0:T(8,128)(2,1)S(1)}, bf16[2,64,512]{2,1,0:T(8,128)(2,1)S(1)}, u32[]{:S(2)}, u32[]{:S(2)}) collective-permute-start(bf16[2,64,512]{2,1,0:T(8,128)(2,1)S(1)} %get-tuple-element.49), channel_id=1, source_target_pairs={{0,2},{1,3},{2,0},{3,1},{4,6},{5,7},{6,4},{7,5},{8,10},{9,11},{10,... | collective-permute-start | bytes 393224 | tf_op jit(solution)/shard_map/ppermute | solution.py:427
  7.1 2.6 %collective-permute-start.4 = (bf16[2,64,512]{2,1,0:T(8,128)(2,1)S(1)}, bf16[2,64,512]{2,1,0:T(8,128)(2,1)S(1)}, u32[]{:S(2)}, u32[]{:S(2)}) collective-permute-start(bf16[2,64,512]{2,1,0:T(8,128)(2,1)S(1)} %get-tuple-element.52), channel_id=1, source_target_pairs={{0,4},{1,5},{2,6},{3,7},{4,0},{5,1},{6,2},{7,3},{8,12},{9,13},{10,... | collective-permute-start | bytes 393224 | tf_op jit(solution)/shard_map/ppermute | solution.py:427
  9.7 0.0 collective-permute-start.5
  9.7 3.0 %collective-permute-done.2.refs_1_ = bf16[2,64,512]{2,1,0:T(8,128)(2,1)S(1)} collective-permute-done((bf16[2,64,512]{2,1,0:T(8,128)(2,1)S(1)}, bf16[2,64,512]{2,1,0:T(8,128)(2,1)S(1)}, u32[]{:S(2)}, u32[]{:S(2)}) %collective-permute-start.2) | collective-permute-done | bytes 131104 | tf_op jit(solution)/shard_map/ppermute | solution.py:427
  12.7 0.0 collective-permute-done.1.refs_2_.got
  12.7 1.8 %collective-permute-start.6 = (bf16[128,512]{1,0:T(8,128)(2,1)S(1)}, bf16[128,512]{1,0:T(8,128)(2,1)S(1)}, u32[]{:S(2)}, u32[]{:S(2)}) collective-permute-start(bf16[128,512]{1,0:T(8,128)(2,1)S(1)} %get-tuple-element.50.rest_0_), channel_id=1, source_target_pairs={{0,16},{8,24},{16,0},{24,8},{1,17},{9,25},{17,1},{25,9},{2,18},{10... | collective-permute-start | bytes 393224 | tf_op jit(solution)/shard_map/ppermute | solution.py:433
  14.5 1.4 %collective-permute-start.7 = (bf16[128,512]{1,0:T(8,128)(2,1)S(1)}, bf16[128,512]{1,0:T(8,128)(2,1)S(1)}, u32[]{:S(2)}, u32[]{:S(2)}) collective-permute-start(bf16[128,512]{1,0:T(8,128)(2,1)S(1)} %get-tuple-element.51), channel_id=1, source_target_pairs={{0,17},{1,16},{2,19},{3,18},{4,21},{5,20},{6,23},{7,22},{8,25},{9,... | collective-permute-start | bytes 393224 | tf_op jit(solution)/shard_map/ppermute | solution.py:436
  15.9 0.3 collective-permute-start.3
  16.3 3.8 %collective-permute-done.4.refs_0_ = bf16[2,64,512]{2,1,0:T(8,128)(2,1)S(1)} collective-permute-done((bf16[2,64,512]{2,1,0:T(8,128)(2,1)S(1)}, bf16[2,64,512]{2,1,0:T(8,128)(2,1)S(1)}, u32[]{:S(2)}, u32[]{:S(2)}) %collective-permute-start.4) | collective-permute-done | bytes 131104 | tf_op jit(solution)/shard_map/ppermute | solution.py:427
  20.0 0.0 collective-permute-done.6.refs_3_.rest_0_.rest_4_
  20.0 0.3 collective-permute-done.7.refs_4_.rest_1_.rest_5_
  20.4 1.6 %collective-permute-start.8 = (bf16[128,512]{1,0:T(8,128)(2,1)S(1)}, bf16[128,512]{1,0:T(8,128)(2,1)S(1)}, u32[]{:S(2)}, u32[]{:S(2)}) collective-permute-start(bf16[128,512]{1,0:T(8,128)(2,1)S(1)} %get-tuple-element.55), channel_id=1, source_target_pairs={{0,1},{1,0},{2,3},{3,2},{4,5},{5,4},{6,7},{7,6},{8,9},{9,8},{10,11... | collective-permute-start | bytes 393224 | tf_op jit(solution)/shard_map/ppermute | solution.py:430
  22.0 1.2 %collective-permute-start.9 = (bf16[128,512]{1,0:T(8,128)(2,1)S(1)}, bf16[128,512]{1,0:T(8,128)(2,1)S(1)}, u32[]{:S(2)}, u32[]{:S(2)}) collective-permute-start(bf16[128,512]{1,0:T(8,128)(2,1)S(1)} %get-tuple-element.54.rest_2_), channel_id=1, source_target_pairs={{0,16},{8,24},{16,0},{24,8},{1,17},{9,25},{17,1},{25,9},{2,18},{10... | collective-permute-start | bytes 393224 | tf_op jit(solution)/shard_map/ppermute | solution.py:433
  23.1 0.8 %collective-permute-start.10 = (bf16[128,512]{1,0:T(8,128)(2,1)S(1)}, bf16[128,512]{1,0:T(8,128)(2,1)S(1)}, u32[]{:S(2)}, u32[]{:S(2)}) collective-permute-start(bf16[128,512]{1,0:T(8,128)(2,1)S(1)} %get-tuple-element.55), channel_id=1, source_target_pairs={{0,17},{1,16},{2,19},{3,18},{4,21},{5,20},{6,23},{7,22},{8,25},{9,... | collective-permute-start | bytes 393224 | tf_op jit(solution)/shard_map/ppermute | solution.py:436
  24.0 0.0 collective-permute-done.3.rest_1_
  24.0 1.9 %collective-permute-done.8.rest_3_ = bf16[128,512]{1,0:T(8,128)(2,1)S(1)} collective-permute-done((bf16[128,512]{1,0:T(8,128)(2,1)S(1)}, bf16[128,512]{1,0:T(8,128)(2,1)S(1)}, u32[]{:S(2)}, u32[]{:S(2)}) %collective-permute-start.8) | collective-permute-done | bytes 131104 | tf_op jit(solution)/shard_map/ppermute | solution.py:430
  25.9 3.8 %shard_map.90 = (bf16[4,256,1024]{2,1,0:T(8,128)(2,1)S(1)}, f32[256,512]{1,0:T(8,128)S(1)}, bf16[128,512]{1,0:T(8,128)(2,1)S(1)}, bf16[128,512]{1,0:T(8,128)(2,1)S(1)}) custom-call(bf16[2,256,128]{2,1,0:T(8,128)(2,1)S(1)} %get-tuple-element.56.bias, bf16[144,2048]{1,0:T(8,128)(2,1)S(1)} %get-tuple-element.43.q_a, ...), custom_call_target="tpu_custom_call" | custom-call | flops 1073741824 | bytes 16777216 | tf_op jit(solution)/shard_map/pallas_call | solution.py:55
  29.7 0.0 collective-permute-done.9.rest_2_.rest_6_
  29.7 0.4 shard_map.91
  30.1 3.5 %collective-permute-start.13 = (bf16[128,512]{1,0:T(8,128)(2,1)S(1)}, bf16[128,512]{1,0:T(8,128)(2,1)S(1)}, u32[]{:S(2)}, u32[]{:S(2)}) collective-permute-start(bf16[128,512]{1,0:T(8,128)(2,1)S(1)} %shard_map.93), channel_id=1, source_target_pairs={{0,1},{1,0},{2,3},{3,2},{4,5},{5,4},{6,7},{7,6},{8,9},{9,8},{10,11... | collective-permute-start | bytes 393224 | tf_op jit(solution)/shard_map/ppermute | solution.py:430
  33.6 0.0 collective-permute-start.11
  33.7 1.5 %collective-permute-start.12 = (bf16[128,512]{1,0:T(8,128)(2,1)S(1)}, bf16[128,512]{1,0:T(8,128)(2,1)S(1)}, u32[]{:S(2)}, u32[]{:S(2)}) collective-permute-start(bf16[128,512]{1,0:T(8,128)(2,1)S(1)} %get-tuple-element.64), channel_id=1, source_target_pairs={{0,17},{1,16},{2,19},{3,18},{4,21},{5,20},{6,23},{7,22},{8,25},{9,... | collective-permute-start | bytes 393224 | tf_op jit(solution)/shard_map/ppermute | solution.py:436
  35.2 1.9 %collective-permute-start.14 = (bf16[128,512]{1,0:T(8,128)(2,1)S(1)}, bf16[128,512]{1,0:T(8,128)(2,1)S(1)}, u32[]{:S(2)}, u32[]{:S(2)}) collective-permute-start(bf16[128,512]{1,0:T(8,128)(2,1)S(1)} %get-tuple-element.67.refs_1_), channel_id=1, source_target_pairs={{0,16},{8,24},{16,0},{24,8},{1,17},{9,25},{17,1},{25,9},{2,18},{10... | collective-permute-start | bytes 393224 | tf_op jit(solution)/shard_map/ppermute | solution.py:433
  37.1 0.1 collective-permute-start.16
  37.2 0.9 %collective-permute-done.13.back_x = bf16[128,512]{1,0:T(8,128)(2,1)S(1)} collective-permute-done((bf16[128,512]{1,0:T(8,128)(2,1)S(1)}, bf16[128,512]{1,0:T(8,128)(2,1)S(1)}, u32[]{:S(2)}, u32[]{:S(2)}) %collective-permute-start.13) | collective-permute-done | bytes 131104 | tf_op jit(solution)/shard_map/ppermute | solution.py:430
  38.1 1.4 %collective-permute-start.15 = (bf16[128,512]{1,0:T(8,128)(2,1)S(1)}, bf16[128,512]{1,0:T(8,128)(2,1)S(1)}, u32[]{:S(2)}, u32[]{:S(2)}) collective-permute-start(bf16[128,512]{1,0:T(8,128)(2,1)S(1)} %get-tuple-element.68), channel_id=1, source_target_pairs={{0,17},{1,16},{2,19},{3,18},{4,21},{5,20},{6,23},{7,22},{8,25},{9,... | collective-permute-start | bytes 393224 | tf_op jit(solution)/shard_map/ppermute | solution.py:436
  39.4 1.3 %collective-permute-done.11.back_y = bf16[128,512]{1,0:T(8,128)(2,1)S(1)} collective-permute-done((bf16[128,512]{1,0:T(8,128)(2,1)S(1)}, bf16[128,512]{1,0:T(8,128)(2,1)S(1)}, u32[]{:S(2)}, u32[]{:S(2)}) %collective-permute-start.11) | collective-permute-done | bytes 131104 | tf_op jit(solution)/shard_map/ppermute | solution.py:433
  40.7 0.1 shard_map.94
  40.8 5.6 %collective-permute-start.20 = (bf16[2,64,512]{2,1,0:T(8,128)(2,1)S(1)}, bf16[2,64,512]{2,1,0:T(8,128)(2,1)S(1)}, u32[]{:S(2)}, u32[]{:S(2)}) collective-permute-start(bf16[2,64,512]{2,1,0:T(8,128)(2,1)S(1)} %get-tuple-element.66.refs_0_), channel_id=1, source_target_pairs={{0,4},{1,5},{2,6},{3,7},{4,0},{5,1},{6,2},{7,3},{8,12},{9,13},{10,... | collective-permute-start | bytes 393224 | tf_op jit(solution)/shard_map/ppermute | solution.py:427
  46.4 0.9 %collective-permute-start.21 = (bf16[2,64,512]{2,1,0:T(8,128)(2,1)S(1)}, bf16[2,64,512]{2,1,0:T(8,128)(2,1)S(1)}, u32[]{:S(2)}, u32[]{:S(2)}) collective-permute-start(bf16[2,64,512]{2,1,0:T(8,128)(2,1)S(1)} %get-tuple-element.75), channel_id=1, source_target_pairs={{0,6},{1,7},{2,4},{3,5},{4,2},{5,3},{6,0},{7,1},{8,14},{9,15},{10,... | collective-permute-start | bytes 393224 | tf_op jit(solution)/shard_map/ppermute | solution.py:427
  47.3 0.1 shard_map.96
  47.3 0.4 collective-permute-start.19
  47.7 1.2 %shard_map.92 = (bf16[128,2048]{1,0:T(8,128)(2,1)S(1)}, bf16[128,2048]{1,0:T(8,128)(2,1)S(1)}) custom-call(bf16[144,2048]{1,0:T(8,128)(2,1)S(1)} %get-tuple-element.43.q_a, bf16[272,2048]{1,0:T(8,128)(2,1)S(1)} %collective-permute-done.1.refs_2_.got, bf16[128,512]{1,0:T(8,128)(2,1)S(1)} %get-tuple-element.50.rest_0_, ...), custom_call_target="tpu_custom_call" | custom-call | flops 536870912 | bytes 8388608 | tf_op jit(solution)/shard_map/pallas_call | solution.py:55
  48.9 0.1 collective-permute-start.17
  49.0 0.5 collective-permute-start.18
  49.5 0.4 collective-permute-done.20.refs_0_
  49.9 3.4 %collective-permute-done.21.refs_1_ = bf16[2,64,512]{2,1,0:T(8,128)(2,1)S(1)} collective-permute-done((bf16[2,64,512]{2,1,0:T(8,128)(2,1)S(1)}, bf16[2,64,512]{2,1,0:T(8,128)(2,1)S(1)}, u32[]{:S(2)}, u32[]{:S(2)}) %collective-permute-start.21) | collective-permute-done | bytes 131104 | tf_op jit(solution)/shard_map/ppermute | solution.py:427
  53.3 0.4 collective-permute-done.19.refs_1_
  53.8 0.1 collective-permute-start.22
  53.9 1.0 %shard_map.98 = (bf16[1,128,4096]{2,1,0:T(8,128)(2,1)}, f32[8,128]{1,0:T(8,128)S(1)}) custom-call(bf16[128,2048]{1,0:T(8,128)(2,1)S(1)} %get-tuple-element.61.mine, bf16[64,2048]{1,0:T(8,128)(2,1)S(1)} %collective-permute-done.17.refs_0_, bf16[64,2048]{1,0:T(8,128)(2,1)S(1)} %collective-permute-done.18.refs_1_), custom_call_target="tpu_custom_call" | custom-call | bytes 524288 | tf_op jit(solution)/shard_map/pallas_call | solution.py:535
  54.9 0.5 collective-permute-done.22.got
  55.4 0.8 %shard_map.101 = (bf16[8,16,1024]{2,1,0:T(8,128)(2,1)}, bf16[8,16,1024]{2,1,0:T(8,128)(2,1)}) custom-call(bf16[2,8,16,512]{3,2,1,0:T(8,128)(2,1)S(1)} %get-tuple-element.78.mine, bf16[2,8,16,512]{3,2,1,0:T(8,128)(2,1)S(1)} %collective-permute-done.22.got, f32[8,128]{1,0:T(8,128)S(1)} %get-tuple-element.80._), custom_call_target="tpu_custom_call" | custom-call | bytes 524288 | tf_op jit(solution)/shard_map/pallas_call | solution.py:550
  (15 shorter events, 0.2 us)
Async XLA Ops:
  1.8 2.1 %collective-permute-start = (bf16[2,8,16,512]{3,2,1,0:T(8,128)(2,1)S(1)}, bf16[2,8,16,512]{3,2,1,0:T(8,128)(2,1)S(1)}, u32[]{:S(2)}, u32[]{:S(2)}) collective-permute-start(bf16[2,8,16,512]{3,2,1,0:T(8,128)(2,1)S(1)} %get-tuple-element.45), channel_id=1, source_target_pairs={{0,8},{8,0},{16,24},{24,16},{1,9},{9,1},{17,25},{25,17},{2,10},{10... | collective-permute-start | bytes 786440 | tf_op jit(solution)/shard_map/ppermute | solution.py:449
  4.0 8.7 %collective-permute-start.1 = (bf16[272,2048]{1,0:T(8,128)(2,1)S(1)}, bf16[272,2048]{1,0:T(8,128)(2,1)S(1)}, u32[]{:S(2)}, u32[]{:S(2)}) collective-permute-start(bf16[272,2048]{1,0:T(8,128)(2,1)S(1)} %get-tuple-element.47), channel_id=1, source_target_pairs={{0,8},{8,0},{16,24},{24,16},{1,9},{9,1},{17,25},{25,17},{2,10},{10... | collective-permute-start | bytes 3342344 | tf_op jit(solution)/shard_map/ppermute | solution.py:450
  4.1 8.6 %collective-permute-start.2 = (bf16[2,64,512]{2,1,0:T(8,128)(2,1)S(1)}, bf16[2,64,512]{2,1,0:T(8,128)(2,1)S(1)}, u32[]{:S(2)}, u32[]{:S(2)}) collective-permute-start(bf16[2,64,512]{2,1,0:T(8,128)(2,1)S(1)} %get-tuple-element.49), channel_id=1, source_target_pairs={{0,2},{1,3},{2,0},{3,1},{4,6},{5,7},{6,4},{7,5},{8,10},{9,11},{10,... | collective-permute-start | bytes 393224 | tf_op jit(solution)/shard_map/ppermute | solution.py:427
  7.1 12.9 %collective-permute-start.4 = (bf16[2,64,512]{2,1,0:T(8,128)(2,1)S(1)}, bf16[2,64,512]{2,1,0:T(8,128)(2,1)S(1)}, u32[]{:S(2)}, u32[]{:S(2)}) collective-permute-start(bf16[2,64,512]{2,1,0:T(8,128)(2,1)S(1)} %get-tuple-element.52), channel_id=1, source_target_pairs={{0,4},{1,5},{2,6},{3,7},{4,0},{5,1},{6,2},{7,3},{8,12},{9,13},{10,... | collective-permute-start | bytes 393224 | tf_op jit(solution)/shard_map/ppermute | solution.py:427
  9.7 10.3 %collective-permute-start.5 = (bf16[2,64,512]{2,1,0:T(8,128)(2,1)S(1)}, bf16[2,64,512]{2,1,0:T(8,128)(2,1)S(1)}, u32[]{:S(2)}, u32[]{:S(2)}) collective-permute-start(bf16[2,64,512]{2,1,0:T(8,128)(2,1)S(1)} %get-tuple-element.53), channel_id=1, source_target_pairs={{0,6},{1,7},{2,4},{3,5},{4,2},{5,3},{6,0},{7,1},{8,14},{9,15},{10,... | collective-permute-start | bytes 393224 | tf_op jit(solution)/shard_map/ppermute | solution.py:427
  12.7 7.3 %collective-permute-start.6 = (bf16[128,512]{1,0:T(8,128)(2,1)S(1)}, bf16[128,512]{1,0:T(8,128)(2,1)S(1)}, u32[]{:S(2)}, u32[]{:S(2)}) collective-permute-start(bf16[128,512]{1,0:T(8,128)(2,1)S(1)} %get-tuple-element.50.rest_0_), channel_id=1, source_target_pairs={{0,16},{8,24},{16,0},{24,8},{1,17},{9,25},{17,1},{25,9},{2,18},{10... | collective-permute-start | bytes 393224 | tf_op jit(solution)/shard_map/ppermute | solution.py:433
  14.5 5.9 %collective-permute-start.7 = (bf16[128,512]{1,0:T(8,128)(2,1)S(1)}, bf16[128,512]{1,0:T(8,128)(2,1)S(1)}, u32[]{:S(2)}, u32[]{:S(2)}) collective-permute-start(bf16[128,512]{1,0:T(8,128)(2,1)S(1)} %get-tuple-element.51), channel_id=1, source_target_pairs={{0,17},{1,16},{2,19},{3,18},{4,21},{5,20},{6,23},{7,22},{8,25},{9,... | collective-permute-start | bytes 393224 | tf_op jit(solution)/shard_map/ppermute | solution.py:436
  15.9 8.0 %collective-permute-start.3 = (bf16[128,512]{1,0:T(8,128)(2,1)S(1)}, bf16[128,512]{1,0:T(8,128)(2,1)S(1)}, u32[]{:S(2)}, u32[]{:S(2)}) collective-permute-start(bf16[128,512]{1,0:T(8,128)(2,1)S(1)} %get-tuple-element.51), channel_id=1, source_target_pairs={{0,1},{1,0},{2,3},{3,2},{4,5},{5,4},{6,7},{7,6},{8,9},{9,8},{10,11... | collective-permute-start | bytes 393224 | tf_op jit(solution)/shard_map/ppermute | solution.py:430
  20.4 5.5 %collective-permute-start.8 = (bf16[128,512]{1,0:T(8,128)(2,1)S(1)}, bf16[128,512]{1,0:T(8,128)(2,1)S(1)}, u32[]{:S(2)}, u32[]{:S(2)}) collective-permute-start(bf16[128,512]{1,0:T(8,128)(2,1)S(1)} %get-tuple-element.55), channel_id=1, source_target_pairs={{0,1},{1,0},{2,3},{3,2},{4,5},{5,4},{6,7},{7,6},{8,9},{9,8},{10,11... | collective-permute-start | bytes 393224 | tf_op jit(solution)/shard_map/ppermute | solution.py:430
  22.0 7.7 %collective-permute-start.9 = (bf16[128,512]{1,0:T(8,128)(2,1)S(1)}, bf16[128,512]{1,0:T(8,128)(2,1)S(1)}, u32[]{:S(2)}, u32[]{:S(2)}) collective-permute-start(bf16[128,512]{1,0:T(8,128)(2,1)S(1)} %get-tuple-element.54.rest_2_), channel_id=1, source_target_pairs={{0,16},{8,24},{16,0},{24,8},{1,17},{9,25},{17,1},{25,9},{2,18},{10... | collective-permute-start | bytes 393224 | tf_op jit(solution)/shard_map/ppermute | solution.py:433
  23.1 6.6 %collective-permute-start.10 = (bf16[128,512]{1,0:T(8,128)(2,1)S(1)}, bf16[128,512]{1,0:T(8,128)(2,1)S(1)}, u32[]{:S(2)}, u32[]{:S(2)}) collective-permute-start(bf16[128,512]{1,0:T(8,128)(2,1)S(1)} %get-tuple-element.55), channel_id=1, source_target_pairs={{0,17},{1,16},{2,19},{3,18},{4,21},{5,20},{6,23},{7,22},{8,25},{9,... | collective-permute-start | bytes 393224 | tf_op jit(solution)/shard_map/ppermute | solution.py:436
  30.1 8.0 %collective-permute-start.13 = (bf16[128,512]{1,0:T(8,128)(2,1)S(1)}, bf16[128,512]{1,0:T(8,128)(2,1)S(1)}, u32[]{:S(2)}, u32[]{:S(2)}) collective-permute-start(bf16[128,512]{1,0:T(8,128)(2,1)S(1)} %shard_map.93), channel_id=1, source_target_pairs={{0,1},{1,0},{2,3},{3,2},{4,5},{5,4},{6,7},{7,6},{8,9},{9,8},{10,11... | collective-permute-start | bytes 393224 | tf_op jit(solution)/shard_map/ppermute | solution.py:430
  33.6 7.1 %collective-permute-start.11 = (bf16[128,512]{1,0:T(8,128)(2,1)S(1)}, bf16[128,512]{1,0:T(8,128)(2,1)S(1)}, u32[]{:S(2)}, u32[]{:S(2)}) collective-permute-start(bf16[128,512]{1,0:T(8,128)(2,1)S(1)} %get-tuple-element.63.refs_1_), channel_id=1, source_target_pairs={{0,16},{8,24},{16,0},{24,8},{1,17},{9,25},{17,1},{25,9},{2,18},{10... | collective-permute-start | bytes 393224 | tf_op jit(solution)/shard_map/ppermute | solution.py:433
  33.7 7.1 %collective-permute-start.12 = (bf16[128,512]{1,0:T(8,128)(2,1)S(1)}, bf16[128,512]{1,0:T(8,128)(2,1)S(1)}, u32[]{:S(2)}, u32[]{:S(2)}) collective-permute-start(bf16[128,512]{1,0:T(8,128)(2,1)S(1)} %get-tuple-element.64), channel_id=1, source_target_pairs={{0,17},{1,16},{2,19},{3,18},{4,21},{5,20},{6,23},{7,22},{8,25},{9,... | collective-permute-start | bytes 393224 | tf_op jit(solution)/shard_map/ppermute | solution.py:436
  35.2 12.1 %collective-permute-start.14 = (bf16[128,512]{1,0:T(8,128)(2,1)S(1)}, bf16[128,512]{1,0:T(8,128)(2,1)S(1)}, u32[]{:S(2)}, u32[]{:S(2)}) collective-permute-start(bf16[128,512]{1,0:T(8,128)(2,1)S(1)} %get-tuple-element.67.refs_1_), channel_id=1, source_target_pairs={{0,16},{8,24},{16,0},{24,8},{1,17},{9,25},{17,1},{25,9},{2,18},{10... | collective-permute-start | bytes 393224 | tf_op jit(solution)/shard_map/ppermute | solution.py:433
  37.1 10.2 %collective-permute-start.16 = (bf16[128,512]{1,0:T(8,128)(2,1)S(1)}, bf16[128,512]{1,0:T(8,128)(2,1)S(1)}, u32[]{:S(2)}, u32[]{:S(2)}) collective-permute-start(bf16[128,512]{1,0:T(8,128)(2,1)S(1)} %shard_map.95), channel_id=1, source_target_pairs={{0,1},{1,0},{2,3},{3,2},{4,5},{5,4},{6,7},{7,6},{8,9},{9,8},{10,11... | collective-permute-start | bytes 393224 | tf_op jit(solution)/shard_map/ppermute | solution.py:430
  38.1 9.2 %collective-permute-start.15 = (bf16[128,512]{1,0:T(8,128)(2,1)S(1)}, bf16[128,512]{1,0:T(8,128)(2,1)S(1)}, u32[]{:S(2)}, u32[]{:S(2)}) collective-permute-start(bf16[128,512]{1,0:T(8,128)(2,1)S(1)} %get-tuple-element.68), channel_id=1, source_target_pairs={{0,17},{1,16},{2,19},{3,18},{4,21},{5,20},{6,23},{7,22},{8,25},{9,... | collective-permute-start | bytes 393224 | tf_op jit(solution)/shard_map/ppermute | solution.py:436
  40.8 9.1 %collective-permute-start.20 = (bf16[2,64,512]{2,1,0:T(8,128)(2,1)S(1)}, bf16[2,64,512]{2,1,0:T(8,128)(2,1)S(1)}, u32[]{:S(2)}, u32[]{:S(2)}) collective-permute-start(bf16[2,64,512]{2,1,0:T(8,128)(2,1)S(1)} %get-tuple-element.66.refs_0_), channel_id=1, source_target_pairs={{0,4},{1,5},{2,6},{3,7},{4,0},{5,1},{6,2},{7,3},{8,12},{9,13},{10,... | collective-permute-start | bytes 393224 | tf_op jit(solution)/shard_map/ppermute | solution.py:427
  46.4 6.9 %collective-permute-start.21 = (bf16[2,64,512]{2,1,0:T(8,128)(2,1)S(1)}, bf16[2,64,512]{2,1,0:T(8,128)(2,1)S(1)}, u32[]{:S(2)}, u32[]{:S(2)}) collective-permute-start(bf16[2,64,512]{2,1,0:T(8,128)(2,1)S(1)} %get-tuple-element.75), channel_id=1, source_target_pairs={{0,6},{1,7},{2,4},{3,5},{4,2},{5,3},{6,0},{7,1},{8,14},{9,15},{10,... | collective-permute-start | bytes 393224 | tf_op jit(solution)/shard_map/ppermute | solution.py:427
  47.3 6.4 %collective-permute-start.19 = (bf16[2,64,512]{2,1,0:T(8,128)(2,1)S(1)}, bf16[2,64,512]{2,1,0:T(8,128)(2,1)S(1)}, u32[]{:S(2)}, u32[]{:S(2)}) collective-permute-start(bf16[2,64,512]{2,1,0:T(8,128)(2,1)S(1)} %get-tuple-element.74), channel_id=1, source_target_pairs={{0,2},{1,3},{2,0},{3,1},{4,6},{5,7},{6,4},{7,5},{8,10},{9,11},{10,... | collective-permute-start | bytes 393224 | tf_op jit(solution)/shard_map/ppermute | solution.py:427
  48.9 5.0 %collective-permute-start.17 = (bf16[64,2048]{1,0:T(8,128)(2,1)S(1)}, bf16[64,2048]{1,0:T(8,128)(2,1)S(1)}, u32[]{:S(2)}, u32[]{:S(2)}) collective-permute-start(bf16[64,2048]{1,0:T(8,128)(2,1)S(1)} %get-tuple-element.71), channel_id=1, source_target_pairs={{0,8},{8,0},{16,24},{24,16},{1,9},{9,1},{17,25},{25,17},{2,10},{10... | collective-permute-start | bytes 786440 | tf_op jit(solution)/shard_map/ppermute | solution.py:482
  49.0 4.9 %collective-permute-start.18 = (bf16[64,2048]{1,0:T(8,128)(2,1)S(1)}, bf16[64,2048]{1,0:T(8,128)(2,1)S(1)}, u32[]{:S(2)}, u32[]{:S(2)}) collective-permute-start(bf16[64,2048]{1,0:T(8,128)(2,1)S(1)} %get-tuple-element.72), channel_id=1, source_target_pairs={{0,8},{8,0},{16,24},{24,16},{1,9},{9,1},{17,25},{25,17},{2,10},{10... | collective-permute-start | bytes 786440 | tf_op jit(solution)/shard_map/ppermute | solution.py:482
  53.8 1.6 %collective-permute-start.22 = (bf16[2,8,16,512]{3,2,1,0:T(8,128)(2,1)S(1)}, bf16[2,8,16,512]{3,2,1,0:T(8,128)(2,1)S(1)}, u32[]{:S(2)}, u32[]{:S(2)}) collective-permute-start(bf16[2,8,16,512]{3,2,1,0:T(8,128)(2,1)S(1)} %get-tuple-element.79), channel_id=1, source_target_pairs={{0,8},{8,0},{16,24},{24,16},{1,9},{9,1},{17,25},{25,17},{2,10},{10... | collective-permute-start | bytes 786440 | tf_op jit(solution)/shard_map/ppermute | solution.py:555

commit v2 on v1

--- a/solution.py
+++ b/solution.py
@@ -265,8 +265,8 @@
             branch(which)
 
 
-def pass_kernel(role, n_blocks, n_kv, n_grads, where, bias, q_a, g_a, got, *rest):
-    kvs, (ds_out, *grads) = rest[:n_kv], rest[-1 - n_grads :]
+def pass_kernel(role, n_blocks, n_kv, n_grads, n_through, where, bias, q_a, g_a, got, *rest):
+    kvs, (ds_out, *grads) = rest[:n_kv], rest[n_kv + n_through : n_kv + n_through + 1 + n_grads]
     sample = where()[0] ^ role
     tokens = g_a.shape[0]
     block_rows = SLOT_ROWS // n_blocks
@@ -361,15 +361,16 @@
         choose([present[role][t] for role in range(SAMP)], one_block)
 
 
-def sample_pass(where, role, n_blocks, bias, text, kvs, grads, after=()):
+def sample_pass(where, role, n_blocks, bias, text, kvs, grads, through=()):
     tokens = text[1].shape[0]
     ds = ((HALF_KV, SLOT_ROWS, CORES * RATIO * tokens), BF16)
     return in_vmem(
-        functools.partial(pass_kernel, role, n_blocks, len(kvs), len(grads), where),
-        [ds, *grads],
+        functools.partial(pass_kernel, role, n_blocks, len(kvs), len(grads), len(through), where),
+        [ds, *grads] + [(part.shape, part.dtype) for part in through],
+        aliases={4 + len(kvs) + i: 1 + len(grads) + i for i in range(len(through))},
         flops=8 * tokens * WIDE * SLOT_ROWS * CORES * HALF_KV,
         moved=16 * 2**20,
-    )(bias, *text, *kvs, *after)
+    )(bias, *text, *kvs, *through)
 
 
 def text_grads(where, n_blocks, text, keys, ds):
@@ -461,14 +462,14 @@
             near_place, 0, n_enc, bias, text, own, [(whole, F32)] + [(quarter, BF16)] * 2
         )
         far_ds, *far_grads = sample_pass(
-            near_place, 1, n_enc, bias, text, far, [(quarter, BF16)] * 4, (own_here,)
+            near_place, 1, n_enc, bias, text, far, [(quarter, BF16)] * 4, own_beside
         )
+        own_beside = far_grads[4:]
         dq = text_grads(near_place, n_enc, text, (own, far), (own_ds, far_ds))
         returned = [None] * n_z
         for z in (2, 0):
             here, beside = far_grads[z : z + 2]
-            (own_part,) = hand_on(own_beside[z // 2], here)
-            back_y, back_xy, back_x = along_y(here), along_xy(beside), along_x(own_part)
+            back_y, back_xy, back_x = along_y(here), along_xy(beside), along_x(own_beside[z // 2])
             totals = in_vmem(functools.partial(add_kernel, z), [(pair, BF16)] * 2)(
                 own_here, back_y, back_xy, back_x
             )

time: 56.8 us -> 57 us (level)
  Pallas kernels: 10.2 us -> 12.4 us
  waiting for transfers between devices: 16 us -> 14.4 us
  starting transfers between devices: 29.2 us -> 28.3 us
    pallas_call x13 -> x11, Pallas kernels: 5.65 us -> 7.89 us  [call(): return local_call(body, [IN_VMEM] * len(args), spec, **more)(*args)]
    ppermute x4, starting transfers between devices: 5.1 us -> 7.14 us  [along_xy(): return lax.ppermute(part, ('ctx', 'enc'), swap_xy)]
    ppermute x4, starting transfers between devices: 4.93 us -> 3.14 us  [along_y(): return lax.ppermute(part, 'ctx', swap_y)]
    ppermute x4, starting transfers between devices: 5.49 us -> 4.24 us  [along_x(): return lax.ppermute(part, 'enc', swap_x)]
    ppermute x4, waiting for transfers between devices: 2.83 us -> 1.94 us  [along_x(): return lax.ppermute(part, 'enc', swap_x)]
    ppermute x6, waiting for transfers between devices: 11 us -> 10.3 us  [along_z(): lax.ppermute(part, 'enc', [(i, i ^ 2 * dz) for i in range(n_enc)])]
  transfers between devices with their start and end apart: 23 -> 23, of which waited for: 10 -> 8; matrix products, arithmetic and copies ran while one was open for 0% -> 0% of each run, Pallas kernels for 14% -> 14%
where the time goes in v2:
time: 57 us; the launch traced here: 56.1 us
  starting transfers between devices  28.3 us (50%)
  waiting for transfers between devices  14.4 us (25%)
  Pallas kernels  12.4 us (22%)
  between operations  0.97 us (2%)
    ppermute x6, starting transfers between devices, along_z(): lax.ppermute(part, 'enc', [(i, i ^ 2 * dz) for i in range(n_enc)])  12.5 us
    ppermute x6, waiting for transfers between devices, along_z(): lax.ppermute(part, 'enc', [(i, i ^ 2 * dz) for i in range(n_enc)])  10.3 us
    pallas_call x11, Pallas kernels, call(): return local_call(body, [IN_VMEM] * len(args), spec, **more)(*args)  7.89 us
    ppermute x4, starting transfers between devices, along_xy(): return lax.ppermute(part, ('ctx', 'enc'), swap_xy)  7.14 us
    ppermute x4, starting transfers between devices, along_x(): return lax.ppermute(part, 'enc', swap_x)  4.24 us
    ppermute x4, starting transfers between devices, along_y(): return lax.ppermute(part, 'ctx', swap_y)  3.14 us
    ppermute x4, waiting for transfers between devices, along_x(): return lax.ppermute(part, 'enc', swap_x)  1.94 us
    pallas_call x1, Pallas kernels, split_the_text(): local_call(functools.partial(split_text, n_blocks, pieces, where), [IN_HB...  1.6 us
  transfers between devices with their start and end apart: 23, of which 8 were waited for; matrix products, arithmetic and copies ran while one was open for 0% of the time, Pallas kernels for 14%

profile of v2, /device:TPU:0, one launch (start us, length us, event | category | flops | bytes accessed | tf_op | source)
XLA Modules:
  0.0 56.1 jit_solution(5670977945320397944)
XLA Ops:
  0.6 1.1 %shard_map.86 = (bf16[2,8,16,512]{3,2,1,0:T(8,128)(2,1)S(1)}, bf16[2,8,16,512]{3,2,1,0:T(8,128)(2,1)S(1)}) custom-call(bf16[8,16,1024]{2,1,0:T(8,128)(2,1)} %k_ref.1, bf16[8,16,1024]{2,1,0:T(8,128)(2,1)} %v_ref.1), custom_call_target="tpu_custom_call" | custom-call | bytes 524288 | tf_op jit(solution)/shard_map/pallas_call | solution.py:439
  1.8 0.5 collective-permute-start
  2.3 1.6 %shard_map.85 = (bf16[272,2048]{1,0:T(8,128)(2,1)S(1)}, bf16[144,2048]{1,0:T(8,128)(2,1)S(1)}, bf16[128,2048]{1,0:T(8,128)(2,1)S(1)}, bf16[2,256,128]{2,1,0:T(8,128)(2,1)S(1)}) custom-call(bf16[1,128,4096]{2,1,0:T(8,128)(2,1)} %q_ref.1, bf16[1,128,4096]{2,1,0:T(8,128)(2,1)} %g_ref.1, s32[1,128]{1,0:T(1,128)} %samp_hbm.1, s32[1,2]{1,0:T(1,128)} %tiles_hbm.1), custom_call_target="tpu_custom_call" | custom-call | bytes 4194304 | tf_op jit(solution)/shard_map/pallas_call | solution.py:400
  3.9 0.0 collective-permute-done.got
  3.9 0.1 shard_map.87
  4.0 0.1 collective-permute-start.1
  4.1 3.0 %collective-permute-start.2 = (bf16[2,64,512]{2,1,0:T(8,128)(2,1)S(1)}, bf16[2,64,512]{2,1,0:T(8,128)(2,1)S(1)}, u32[]{:S(2)}, u32[]{:S(2)}) collective-permute-start(bf16[2,64,512]{2,1,0:T(8,128)(2,1)S(1)} %get-tuple-element.51), channel_id=1, source_target_pairs={{0,2},{1,3},{2,0},{3,1},{4,6},{5,7},{6,4},{7,5},{8,10},{9,11},{10,... | collective-permute-start | bytes 393224 | tf_op jit(solution)/shard_map/ppermute | solution.py:428
  7.1 2.6 %collective-permute-start.4 = (bf16[2,64,512]{2,1,0:T(8,128)(2,1)S(1)}, bf16[2,64,512]{2,1,0:T(8,128)(2,1)S(1)}, u32[]{:S(2)}, u32[]{:S(2)}) collective-permute-start(bf16[2,64,512]{2,1,0:T(8,128)(2,1)S(1)} %get-tuple-element.54), channel_id=1, source_target_pairs={{0,4},{1,5},{2,6},{3,7},{4,0},{5,1},{6,2},{7,3},{8,12},{9,13},{10,... | collective-permute-start | bytes 393224 | tf_op jit(solution)/shard_map/ppermute | solution.py:428
  9.7 0.0 collective-permute-start.5
  9.7 3.0 %collective-permute-done.2.refs_1_ = bf16[2,64,512]{2,1,0:T(8,128)(2,1)S(1)} collective-permute-done((bf16[2,64,512]{2,1,0:T(8,128)(2,1)S(1)}, bf16[2,64,512]{2,1,0:T(8,128)(2,1)S(1)}, u32[]{:S(2)}, u32[]{:S(2)}) %collective-permute-start.2) | collective-permute-done | bytes 131104 | tf_op jit(solution)/shard_map/ppermute | solution.py:428
  12.7 0.0 collective-permute-done.1.refs_2_.got
  12.7 1.8 %collective-permute-start.6 = (bf16[128,512]{1,0:T(8,128)(2,1)S(1)}, bf16[128,512]{1,0:T(8,128)(2,1)S(1)}, u32[]{:S(2)}, u32[]{:S(2)}) collective-permute-start(bf16[128,512]{1,0:T(8,128)(2,1)S(1)} %get-tuple-element.52.rest_0_), channel_id=1, source_target_pairs={{0,16},{8,24},{16,0},{24,8},{1,17},{9,25},{17,1},{25,9},{2,18},{10... | collective-permute-start | bytes 393224 | tf_op jit(solution)/shard_map/ppermute | solution.py:434
  14.5 1.4 %collective-permute-start.7 = (bf16[128,512]{1,0:T(8,128)(2,1)S(1)}, bf16[128,512]{1,0:T(8,128)(2,1)S(1)}, u32[]{:S(2)}, u32[]{:S(2)}) collective-permute-start(bf16[128,512]{1,0:T(8,128)(2,1)S(1)} %get-tuple-element.53), channel_id=1, source_target_pairs={{0,17},{1,16},{2,19},{3,18},{4,21},{5,20},{6,23},{7,22},{8,25},{9,... | collective-permute-start | bytes 393224 | tf_op jit(solution)/shard_map/ppermute | solution.py:437
  15.9 0.3 collective-permute-start.3
  16.3 3.8 %collective-permute-done.4.refs_0_ = bf16[2,64,512]{2,1,0:T(8,128)(2,1)S(1)} collective-permute-done((bf16[2,64,512]{2,1,0:T(8,128)(2,1)S(1)}, bf16[2,64,512]{2,1,0:T(8,128)(2,1)S(1)}, u32[]{:S(2)}, u32[]{:S(2)}) %collective-permute-start.4) | collective-permute-done | bytes 131104 | tf_op jit(solution)/shard_map/ppermute | solution.py:428
  20.0 0.0 collective-permute-done.5.refs_1_
  20.0 0.0 collective-permute-done.6.refs_3_.rest_0_.rest_4_
  20.0 0.3 collective-permute-done.7.refs_4_.rest_1_.rest_5_
  20.4 1.6 %collective-permute-start.8 = (bf16[128,512]{1,0:T(8,128)(2,1)S(1)}, bf16[128,512]{1,0:T(8,128)(2,1)S(1)}, u32[]{:S(2)}, u32[]{:S(2)}) collective-permute-start(bf16[128,512]{1,0:T(8,128)(2,1)S(1)} %get-tuple-element.57), channel_id=1, source_target_pairs={{0,1},{1,0},{2,3},{3,2},{4,5},{5,4},{6,7},{7,6},{8,9},{9,8},{10,11... | collective-permute-start | bytes 393224 | tf_op jit(solution)/shard_map/ppermute | solution.py:431
  22.0 1.2 %collective-permute-start.9 = (bf16[128,512]{1,0:T(8,128)(2,1)S(1)}, bf16[128,512]{1,0:T(8,128)(2,1)S(1)}, u32[]{:S(2)}, u32[]{:S(2)}) collective-permute-start(bf16[128,512]{1,0:T(8,128)(2,1)S(1)} %get-tuple-element.56.rest_2_), channel_id=1, source_target_pairs={{0,16},{8,24},{16,0},{24,8},{1,17},{9,25},{17,1},{25,9},{2,18},{10... | collective-permute-start | bytes 393224 | tf_op jit(solution)/shard_map/ppermute | solution.py:434
  23.1 0.8 %collective-permute-start.10 = (bf16[128,512]{1,0:T(8,128)(2,1)S(1)}, bf16[128,512]{1,0:T(8,128)(2,1)S(1)}, u32[]{:S(2)}, u32[]{:S(2)}) collective-permute-start(bf16[128,512]{1,0:T(8,128)(2,1)S(1)} %get-tuple-element.57), channel_id=1, source_target_pairs={{0,17},{1,16},{2,19},{3,18},{4,21},{5,20},{6,23},{7,22},{8,25},{9,... | collective-permute-start | bytes 393224 | tf_op jit(solution)/shard_map/ppermute | solution.py:437
  24.0 0.0 collective-permute-done.3.rest_1_
  24.0 1.9 %collective-permute-done.8.rest_3_ = bf16[128,512]{1,0:T(8,128)(2,1)S(1)} collective-permute-done((bf16[128,512]{1,0:T(8,128)(2,1)S(1)}, bf16[128,512]{1,0:T(8,128)(2,1)S(1)}, u32[]{:S(2)}, u32[]{:S(2)}) %collective-permute-start.8) | collective-permute-done | bytes 131104 | tf_op jit(solution)/shard_map/ppermute | solution.py:431
  25.9 3.8 %shard_map.90 = (bf16[4,256,1024]{2,1,0:T(8,128)(2,1)S(1)}, f32[256,512]{1,0:T(8,128)S(1)}, bf16[128,512]{1,0:T(8,128)(2,1)S(1)}, bf16[128,512]{1,0:T(8,128)(2,1)S(1)}) custom-call(bf16[2,256,128]{2,1,0:T(8,128)(2,1)S(1)} %get-tuple-element.58.bias, bf16[144,2048]{1,0:T(8,128)(2,1)S(1)} %get-tuple-element.45.q_a, ...), custom_call_target="tpu_custom_call" | custom-call | flops 1073741824 | bytes 16777216 | tf_op jit(solution)/shard_map/pallas_call | solution.py:55
  29.7 0.0 collective-permute-done.9.rest_2_.rest_6_
  29.7 0.0 collective-permute-done.10.rest_3_.rest_7_
  29.7 2.3 %shard_map.91 = (bf16[4,256,1024]{2,1,0:T(8,128)(2,1)S(1)}, bf16[128,512]{1,0:T(8,128)(2,1)S(1)}, bf16[128,512]{1,0:T(8,128)(2,1)S(1)}, bf16[128,512]{1,0:T(8,12...) custom-call(bf16[2,256,128]{2,1,0:T(8,128)(2,1)S(1)} %get-tuple-elem, ...), custom_call_target="tpu_custom_call", output_to_operand_aliasing={{5}: (8, {}), {6}: (9, {})} | custom-call | flops 1073741824 | bytes 16777216 | tf_op jit(solution)/shard_map/pallas_call | solution.py:55
  32.1 0.1 collective-permute-start.11
  32.1 2.5 %collective-permute-start.12 = (bf16[128,512]{1,0:T(8,128)(2,1)S(1)}, bf16[128,512]{1,0:T(8,128)(2,1)S(1)}, u32[]{:S(2)}, u32[]{:S(2)}) collective-permute-start(bf16[128,512]{1,0:T(8,128)(2,1)S(1)} %get-tuple-element.68), channel_id=1, source_target_pairs={{0,17},{1,16},{2,19},{3,18},{4,21},{5,20},{6,23},{7,22},{8,25},{9,... | collective-permute-start | bytes 393224 | tf_op jit(solution)/shard_map/ppermute | solution.py:437
  34.6 1.0 %collective-permute-start.13 = (bf16[128,512]{1,0:T(8,128)(2,1)S(1)}, bf16[128,512]{1,0:T(8,128)(2,1)S(1)}, u32[]{:S(2)}, u32[]{:S(2)}) collective-permute-start(bf16[128,512]{1,0:T(8,128)(2,1)S(1)} %get-tuple-element.69), channel_id=1, source_target_pairs={{0,1},{1,0},{2,3},{3,2},{4,5},{5,4},{6,7},{7,6},{8,9},{9,8},{10,11... | collective-permute-start | bytes 393224 | tf_op jit(solution)/shard_map/ppermute | solution.py:431
  35.6 0.1 collective-permute-start.14
  35.7 2.4 %collective-permute-start.15 = (bf16[128,512]{1,0:T(8,128)(2,1)S(1)}, bf16[128,512]{1,0:T(8,128)(2,1)S(1)}, u32[]{:S(2)}, u32[]{:S(2)}) collective-permute-start(bf16[128,512]{1,0:T(8,128)(2,1)S(1)} %get-tuple-element.72), channel_id=1, source_target_pairs={{0,17},{1,16},{2,19},{3,18},{4,21},{5,20},{6,23},{7,22},{8,25},{9,... | collective-permute-start | bytes 393224 | tf_op jit(solution)/shard_map/ppermute | solution.py:437
  38.1 1.3 %collective-permute-done.11.back_y = bf16[128,512]{1,0:T(8,128)(2,1)S(1)} collective-permute-done((bf16[128,512]{1,0:T(8,128)(2,1)S(1)}, bf16[128,512]{1,0:T(8,128)(2,1)S(1)}, u32[]{:S(2)}, u32[]{:S(2)}) %collective-permute-start.11) | collective-permute-done | bytes 131104 | tf_op jit(solution)/shard_map/ppermute | solution.py:434
  39.4 1.4 %collective-permute-start.16 = (bf16[128,512]{1,0:T(8,128)(2,1)S(1)}, bf16[128,512]{1,0:T(8,128)(2,1)S(1)}, u32[]{:S(2)}, u32[]{:S(2)}) collective-permute-start(bf16[128,512]{1,0:T(8,128)(2,1)S(1)} %get-tuple-element.73), channel_id=1, source_target_pairs={{0,1},{1,0},{2,3},{3,2},{4,5},{5,4},{6,7},{7,6},{8,9},{9,8},{10,11... | collective-permute-start | bytes 393224 | tf_op jit(solution)/shard_map/ppermute | solution.py:431
  40.8 0.1 shard_map.93
  40.9 5.1 %collective-permute-start.20 = (bf16[2,64,512]{2,1,0:T(8,128)(2,1)S(1)}, bf16[2,64,512]{2,1,0:T(8,128)(2,1)S(1)}, u32[]{:S(2)}, u32[]{:S(2)}) collective-permute-start(bf16[2,64,512]{2,1,0:T(8,128)(2,1)S(1)} %get-tuple-element.70.refs_0_), channel_id=1, source_target_pairs={{0,4},{1,5},{2,6},{3,7},{4,0},{5,1},{6,2},{7,3},{8,12},{9,13},{10,... | collective-permute-start | bytes 393224 | tf_op jit(solution)/shard_map/ppermute | solution.py:428
  46.0 1.0 %collective-permute-start.21 = (bf16[2,64,512]{2,1,0:T(8,128)(2,1)S(1)}, bf16[2,64,512]{2,1,0:T(8,128)(2,1)S(1)}, u32[]{:S(2)}, u32[]{:S(2)}) collective-permute-start(bf16[2,64,512]{2,1,0:T(8,128)(2,1)S(1)} %get-tuple-element.79), channel_id=1, source_target_pairs={{0,6},{1,7},{2,4},{3,5},{4,2},{5,3},{6,0},{7,1},{8,14},{9,15},{10,... | collective-permute-start | bytes 393224 | tf_op jit(solution)/shard_map/ppermute | solution.py:428
  47.0 0.1 shard_map.94
  47.1 0.8 %collective-permute-start.19 = (bf16[2,64,512]{2,1,0:T(8,128)(2,1)S(1)}, bf16[2,64,512]{2,1,0:T(8,128)(2,1)S(1)}, u32[]{:S(2)}, u32[]{:S(2)}) collective-permute-start(bf16[2,64,512]{2,1,0:T(8,128)(2,1)S(1)} %get-tuple-element.78), channel_id=1, source_target_pairs={{0,2},{1,3},{2,0},{3,1},{4,6},{5,7},{6,4},{7,5},{8,10},{9,11},{10,... | collective-permute-start | bytes 393224 | tf_op jit(solution)/shard_map/ppermute | solution.py:428
  47.8 1.5 %shard_map.92 = (bf16[128,2048]{1,0:T(8,128)(2,1)S(1)}, bf16[128,2048]{1,0:T(8,128)(2,1)S(1)}) custom-call(bf16[144,2048]{1,0:T(8,128)(2,1)S(1)} %get-tuple-element.45.q_a, bf16[272,2048]{1,0:T(8,128)(2,1)S(1)} %collective-permute-done.1.refs_2_.got, bf16[128,512]{1,0:T(8,128)(2,1)S(1)} %get-tuple-element.52.rest_0_, ...), custom_call_target="tpu_custom_call" | custom-call | flops 536870912 | bytes 8388608 | tf_op jit(solution)/shard_map/pallas_call | solution.py:55
  49.3 0.1 collective-permute-start.17
  49.4 0.5 collective-permute-start.18
  49.9 3.0 %collective-permute-done.21.refs_1_ = bf16[2,64,512]{2,1,0:T(8,128)(2,1)S(1)} collective-permute-done((bf16[2,64,512]{2,1,0:T(8,128)(2,1)S(1)}, bf16[2,64,512]{2,1,0:T(8,128)(2,1)S(1)}, u32[]{:S(2)}, u32[]{:S(2)}) %collective-permute-start.21) | collective-permute-done | bytes 131104 | tf_op jit(solution)/shard_map/ppermute | solution.py:428
  53.0 0.5 collective-permute-done.19.refs_1_
  53.5 0.1 collective-permute-start.22
  53.6 1.0 %shard_map.96 = (bf16[1,128,4096]{2,1,0:T(8,128)(2,1)}, f32[8,128]{1,0:T(8,128)S(1)}) custom-call(bf16[128,2048]{1,0:T(8,128)(2,1)S(1)} %get-tuple-element.64.mine, bf16[64,2048]{1,0:T(8,128)(2,1)S(1)} %collective-permute-done.17.refs_0_, bf16[64,2048]{1,0:T(8,128)(2,1)S(1)} %collective-permute-done.18.refs_1_), custom_call_target="tpu_custom_call" | custom-call | bytes 524288 | tf_op jit(solution)/shard_map/pallas_call | solution.py:536
  54.7 0.5 collective-permute-done.22.got
  55.1 0.8 %shard_map.99 = (bf16[8,16,1024]{2,1,0:T(8,128)(2,1)}, bf16[8,16,1024]{2,1,0:T(8,128)(2,1)}) custom-call(bf16[2,8,16,512]{3,2,1,0:T(8,128)(2,1)S(1)} %get-tuple-element.82.mine, bf16[2,8,16,512]{3,2,1,0:T(8,128)(2,1)S(1)} %collective-permute-done.22.got, f32[8,128]{1,0:T(8,128)S(1)} %get-tuple-element.84._), custom_call_target="tpu_custom_call" | custom-call | bytes 524288 | tf_op jit(solution)/shard_map/pallas_call | solution.py:551
  (13 shorter events, 0.2 us)
Async XLA Ops:
  1.8 2.1 %collective-permute-start = (bf16[2,8,16,512]{3,2,1,0:T(8,128)(2,1)S(1)}, bf16[2,8,16,512]{3,2,1,0:T(8,128)(2,1)S(1)}, u32[]{:S(2)}, u32[]{:S(2)}) collective-permute-start(bf16[2,8,16,512]{3,2,1,0:T(8,128)(2,1)S(1)} %get-tuple-element.47), channel_id=1, source_target_pairs={{0,8},{8,0},{16,24},{24,16},{1,9},{9,1},{17,25},{25,17},{2,10},{10... | collective-permute-start | bytes 786440 | tf_op jit(solution)/shard_map/ppermute | solution.py:450
  4.0 8.7 %collective-permute-start.1 = (bf16[272,2048]{1,0:T(8,128)(2,1)S(1)}, bf16[272,2048]{1,0:T(8,128)(2,1)S(1)}, u32[]{:S(2)}, u32[]{:S(2)}) collective-permute-start(bf16[272,2048]{1,0:T(8,128)(2,1)S(1)} %get-tuple-element.49), channel_id=1, source_target_pairs={{0,8},{8,0},{16,24},{24,16},{1,9},{9,1},{17,25},{25,17},{2,10},{10... | collective-permute-start | bytes 3342344 | tf_op jit(solution)/shard_map/ppermute | solution.py:451
  4.1 8.6 %collective-permute-start.2 = (bf16[2,64,512]{2,1,0:T(8,128)(2,1)S(1)}, bf16[2,64,512]{2,1,0:T(8,128)(2,1)S(1)}, u32[]{:S(2)}, u32[]{:S(2)}) collective-permute-start(bf16[2,64,512]{2,1,0:T(8,128)(2,1)S(1)} %get-tuple-element.51), channel_id=1, source_target_pairs={{0,2},{1,3},{2,0},{3,1},{4,6},{5,7},{6,4},{7,5},{8,10},{9,11},{10,... | collective-permute-start | bytes 393224 | tf_op jit(solution)/shard_map/ppermute | solution.py:428
  7.1 12.9 %collective-permute-start.4 = (bf16[2,64,512]{2,1,0:T(8,128)(2,1)S(1)}, bf16[2,64,512]{2,1,0:T(8,128)(2,1)S(1)}, u32[]{:S(2)}, u32[]{:S(2)}) collective-permute-start(bf16[2,64,512]{2,1,0:T(8,128)(2,1)S(1)} %get-tuple-element.54), channel_id=1, source_target_pairs={{0,4},{1,5},{2,6},{3,7},{4,0},{5,1},{6,2},{7,3},{8,12},{9,13},{10,... | collective-permute-start | bytes 393224 | tf_op jit(solution)/shard_map/ppermute | solution.py:428
  9.7 10.3 %collective-permute-start.5 = (bf16[2,64,512]{2,1,0:T(8,128)(2,1)S(1)}, bf16[2,64,512]{2,1,0:T(8,128)(2,1)S(1)}, u32[]{:S(2)}, u32[]{:S(2)}) collective-permute-start(bf16[2,64,512]{2,1,0:T(8,128)(2,1)S(1)} %get-tuple-element.55), channel_id=1, source_target_pairs={{0,6},{1,7},{2,4},{3,5},{4,2},{5,3},{6,0},{7,1},{8,14},{9,15},{10,... | collective-permute-start | bytes 393224 | tf_op jit(solution)/shard_map/ppermute | solution.py:428
  12.7 7.3 %collective-permute-start.6 = (bf16[128,512]{1,0:T(8,128)(2,1)S(1)}, bf16[128,512]{1,0:T(8,128)(2,1)S(1)}, u32[]{:S(2)}, u32[]{:S(2)}) collective-permute-start(bf16[128,512]{1,0:T(8,128)(2,1)S(1)} %get-tuple-element.52.rest_0_), channel_id=1, source_target_pairs={{0,16},{8,24},{16,0},{24,8},{1,17},{9,25},{17,1},{25,9},{2,18},{10... | collective-permute-start | bytes 393224 | tf_op jit(solution)/shard_map/ppermute | solution.py:434
  14.5 5.9 %collective-permute-start.7 = (bf16[128,512]{1,0:T(8,128)(2,1)S(1)}, bf16[128,512]{1,0:T(8,128)(2,1)S(1)}, u32[]{:S(2)}, u32[]{:S(2)}) collective-permute-start(bf16[128,512]{1,0:T(8,128)(2,1)S(1)} %get-tuple-element.53), channel_id=1, source_target_pairs={{0,17},{1,16},{2,19},{3,18},{4,21},{5,20},{6,23},{7,22},{8,25},{9,... | collective-permute-start | bytes 393224 | tf_op jit(solution)/shard_map/ppermute | solution.py:437
  15.9 8.0 %collective-permute-start.3 = (bf16[128,512]{1,0:T(8,128)(2,1)S(1)}, bf16[128,512]{1,0:T(8,128)(2,1)S(1)}, u32[]{:S(2)}, u32[]{:S(2)}) collective-permute-start(bf16[128,512]{1,0:T(8,128)(2,1)S(1)} %get-tuple-element.53), channel_id=1, source_target_pairs={{0,1},{1,0},{2,3},{3,2},{4,5},{5,4},{6,7},{7,6},{8,9},{9,8},{10,11... | collective-permute-start | bytes 393224 | tf_op jit(solution)/shard_map/ppermute | solution.py:431
  20.4 5.5 %collective-permute-start.8 = (bf16[128,512]{1,0:T(8,128)(2,1)S(1)}, bf16[128,512]{1,0:T(8,128)(2,1)S(1)}, u32[]{:S(2)}, u32[]{:S(2)}) collective-permute-start(bf16[128,512]{1,0:T(8,128)(2,1)S(1)} %get-tuple-element.57), channel_id=1, source_target_pairs={{0,1},{1,0},{2,3},{3,2},{4,5},{5,4},{6,7},{7,6},{8,9},{9,8},{10,11... | collective-permute-start | bytes 393224 | tf_op jit(solution)/shard_map/ppermute | solution.py:431
  22.0 7.7 %collective-permute-start.9 = (bf16[128,512]{1,0:T(8,128)(2,1)S(1)}, bf16[128,512]{1,0:T(8,128)(2,1)S(1)}, u32[]{:S(2)}, u32[]{:S(2)}) collective-permute-start(bf16[128,512]{1,0:T(8,128)(2,1)S(1)} %get-tuple-element.56.rest_2_), channel_id=1, source_target_pairs={{0,16},{8,24},{16,0},{24,8},{1,17},{9,25},{17,1},{25,9},{2,18},{10... | collective-permute-start | bytes 393224 | tf_op jit(solution)/shard_map/ppermute | solution.py:434
  23.1 6.6 %collective-permute-start.10 = (bf16[128,512]{1,0:T(8,128)(2,1)S(1)}, bf16[128,512]{1,0:T(8,128)(2,1)S(1)}, u32[]{:S(2)}, u32[]{:S(2)}) collective-permute-start(bf16[128,512]{1,0:T(8,128)(2,1)S(1)} %get-tuple-element.57), channel_id=1, source_target_pairs={{0,17},{1,16},{2,19},{3,18},{4,21},{5,20},{6,23},{7,22},{8,25},{9,... | collective-permute-start | bytes 393224 | tf_op jit(solution)/shard_map/ppermute | solution.py:437
  32.1 7.4 %collective-permute-start.11 = (bf16[128,512]{1,0:T(8,128)(2,1)S(1)}, bf16[128,512]{1,0:T(8,128)(2,1)S(1)}, u32[]{:S(2)}, u32[]{:S(2)}) collective-permute-start(bf16[128,512]{1,0:T(8,128)(2,1)S(1)} %get-tuple-element.67), channel_id=1, source_target_pairs={{0,16},{8,24},{16,0},{24,8},{1,17},{9,25},{17,1},{25,9},{2,18},{10... | collective-permute-start | bytes 393224 | tf_op jit(solution)/shard_map/ppermute | solution.py:434
  32.1 8.7 %collective-permute-start.12 = (bf16[128,512]{1,0:T(8,128)(2,1)S(1)}, bf16[128,512]{1,0:T(8,128)(2,1)S(1)}, u32[]{:S(2)}, u32[]{:S(2)}) collective-permute-start(bf16[128,512]{1,0:T(8,128)(2,1)S(1)} %get-tuple-element.68), channel_id=1, source_target_pairs={{0,17},{1,16},{2,19},{3,18},{4,21},{5,20},{6,23},{7,22},{8,25},{9,... | collective-permute-start | bytes 393224 | tf_op jit(solution)/shard_map/ppermute | solution.py:437
  34.6 6.2 %collective-permute-start.13 = (bf16[128,512]{1,0:T(8,128)(2,1)S(1)}, bf16[128,512]{1,0:T(8,128)(2,1)S(1)}, u32[]{:S(2)}, u32[]{:S(2)}) collective-permute-start(bf16[128,512]{1,0:T(8,128)(2,1)S(1)} %get-tuple-element.69), channel_id=1, source_target_pairs={{0,1},{1,0},{2,3},{3,2},{4,5},{5,4},{6,7},{7,6},{8,9},{9,8},{10,11... | collective-permute-start | bytes 393224 | tf_op jit(solution)/shard_map/ppermute | solution.py:431
  35.6 11.4 %collective-permute-start.14 = (bf16[128,512]{1,0:T(8,128)(2,1)S(1)}, bf16[128,512]{1,0:T(8,128)(2,1)S(1)}, u32[]{:S(2)}, u32[]{:S(2)}) collective-permute-start(bf16[128,512]{1,0:T(8,128)(2,1)S(1)} %get-tuple-element.71), channel_id=1, source_target_pairs={{0,16},{8,24},{16,0},{24,8},{1,17},{9,25},{17,1},{25,9},{2,18},{10... | collective-permute-start | bytes 393224 | tf_op jit(solution)/shard_map/ppermute | solution.py:434
  35.7 11.3 %collective-permute-start.15 = (bf16[128,512]{1,0:T(8,128)(2,1)S(1)}, bf16[128,512]{1,0:T(8,128)(2,1)S(1)}, u32[]{:S(2)}, u32[]{:S(2)}) collective-permute-start(bf16[128,512]{1,0:T(8,128)(2,1)S(1)} %get-tuple-element.72), channel_id=1, source_target_pairs={{0,17},{1,16},{2,19},{3,18},{4,21},{5,20},{6,23},{7,22},{8,25},{9,... | collective-permute-start | bytes 393224 | tf_op jit(solution)/shard_map/ppermute | solution.py:437
  39.4 7.6 %collective-permute-start.16 = (bf16[128,512]{1,0:T(8,128)(2,1)S(1)}, bf16[128,512]{1,0:T(8,128)(2,1)S(1)}, u32[]{:S(2)}, u32[]{:S(2)}) collective-permute-start(bf16[128,512]{1,0:T(8,128)(2,1)S(1)} %get-tuple-element.73), channel_id=1, source_target_pairs={{0,1},{1,0},{2,3},{3,2},{4,5},{5,4},{6,7},{7,6},{8,9},{9,8},{10,11... | collective-permute-start | bytes 393224 | tf_op jit(solution)/shard_map/ppermute | solution.py:431
  40.9 9.1 %collective-permute-start.20 = (bf16[2,64,512]{2,1,0:T(8,128)(2,1)S(1)}, bf16[2,64,512]{2,1,0:T(8,128)(2,1)S(1)}, u32[]{:S(2)}, u32[]{:S(2)}) collective-permute-start(bf16[2,64,512]{2,1,0:T(8,128)(2,1)S(1)} %get-tuple-element.70.refs_0_), channel_id=1, source_target_pairs={{0,4},{1,5},{2,6},{3,7},{4,0},{5,1},{6,2},{7,3},{8,12},{9,13},{10,... | collective-permute-start | bytes 393224 | tf_op jit(solution)/shard_map/ppermute | solution.py:428
  46.0 6.9 %collective-permute-start.21 = (bf16[2,64,512]{2,1,0:T(8,128)(2,1)S(1)}, bf16[2,64,512]{2,1,0:T(8,128)(2,1)S(1)}, u32[]{:S(2)}, u32[]{:S(2)}) collective-permute-start(bf16[2,64,512]{2,1,0:T(8,128)(2,1)S(1)} %get-tuple-element.79), channel_id=1, source_target_pairs={{0,6},{1,7},{2,4},{3,5},{4,2},{5,3},{6,0},{7,1},{8,14},{9,15},{10,... | collective-permute-start | bytes 393224 | tf_op jit(solution)/shard_map/ppermute | solution.py:428
  47.1 6.4 %collective-permute-start.19 = (bf16[2,64,512]{2,1,0:T(8,128)(2,1)S(1)}, bf16[2,64,512]{2,1,0:T(8,128)(2,1)S(1)}, u32[]{:S(2)}, u32[]{:S(2)}) collective-permute-start(bf16[2,64,512]{2,1,0:T(8,128)(2,1)S(1)} %get-tuple-element.78), channel_id=1, source_target_pairs={{0,2},{1,3},{2,0},{3,1},{4,6},{5,7},{6,4},{7,5},{8,10},{9,11},{10,... | collective-permute-start | bytes 393224 | tf_op jit(solution)/shard_map/ppermute | solution.py:428
  49.3 4.3 %collective-permute-start.17 = (bf16[64,2048]{1,0:T(8,128)(2,1)S(1)}, bf16[64,2048]{1,0:T(8,128)(2,1)S(1)}, u32[]{:S(2)}, u32[]{:S(2)}) collective-permute-start(bf16[64,2048]{1,0:T(8,128)(2,1)S(1)} %get-tuple-element.75), channel_id=1, source_target_pairs={{0,8},{8,0},{16,24},{24,16},{1,9},{9,1},{17,25},{25,17},{2,10},{10... | collective-permute-start | bytes 786440 | tf_op jit(solution)/shard_map/ppermute | solution.py:483
  49.4 4.2 %collective-permute-start.18 = (bf16[64,2048]{1,0:T(8,128)(2,1)S(1)}, bf16[64,2048]{1,0:T(8,128)(2,1)S(1)}, u32[]{:S(2)}, u32[]{:S(2)}) collective-permute-start(bf16[64,2048]{1,0:T(8,128)(2,1)S(1)} %get-tuple-element.76), channel_id=1, source_target_pairs={{0,8},{8,0},{16,24},{24,16},{1,9},{9,1},{17,25},{25,17},{2,10},{10... | collective-permute-start | bytes 786440 | tf_op jit(solution)/shard_map/ppermute | solution.py:483
  53.5 1.6 %collective-permute-start.22 = (bf16[2,8,16,512]{3,2,1,0:T(8,128)(2,1)S(1)}, bf16[2,8,16,512]{3,2,1,0:T(8,128)(2,1)S(1)}, u32[]{:S(2)}, u32[]{:S(2)}) collective-permute-start(bf16[2,8,16,512]{3,2,1,0:T(8,128)(2,1)S(1)} %get-tuple-element.83), channel_id=1, source_target_pairs={{0,8},{8,0},{16,24},{24,16},{1,9},{9,1},{17,25},{25,17},{2,10},{10... | collective-permute-start | bytes 786440 | tf_op jit(solution)/shard_map/ppermute | solution.py:556

commit v3 on v1

--- a/solution.py
+++ b/solution.py
@@ -467,7 +467,7 @@
         returned = [None] * n_z
         for z in (2, 0):
             here, beside = far_grads[z : z + 2]
-            (own_part,) = hand_on(own_beside[z // 2], here)
+            (own_part,) = hand_on(own_beside[z // 2], far_ds)
             back_y, back_xy, back_x = along_y(here), along_xy(beside), along_x(own_part)
             totals = in_vmem(functools.partial(add_kernel, z), [(pair, BF16)] * 2)(
                 own_here, back_y, back_xy, back_x

time: 56.8 us -> 56.3 us (level)
    ppermute x4, starting transfers between devices: 5.49 us -> 7.36 us  [along_x(): return lax.ppermute(part, 'enc', swap_x)]
    ppermute x4, starting transfers between devices: 4.93 us -> 3.06 us  [along_y(): return lax.ppermute(part, 'ctx', swap_y)]
where the time goes in v3:
time: 56.3 us; the launch traced here: 56.2 us
  starting transfers between devices  29.1 us (52%)
  waiting for transfers between devices  16 us (28%)
  Pallas kernels  10.2 us (18%)
  between operations  0.97 us (2%)
    ppermute x6, starting transfers between devices, along_z(): lax.ppermute(part, 'enc', [(i, i ^ 2 * dz) for i in range(n_enc)])  12.2 us
    ppermute x6, waiting for transfers between devices, along_z(): lax.ppermute(part, 'enc', [(i, i ^ 2 * dz) for i in range(n_enc)])  11 us
    ppermute x4, starting transfers between devices, along_x(): return lax.ppermute(part, 'enc', swap_x)  7.36 us
    pallas_call x13, Pallas kernels, call(): return local_call(body, [IN_VMEM] * len(args), spec, **more)(*args)  5.65 us
    ppermute x4, starting transfers between devices, along_xy(): return lax.ppermute(part, ('ctx', 'enc'), swap_xy)  5.16 us
    ppermute x4, starting transfers between devices, along_y(): return lax.ppermute(part, 'ctx', swap_y)  3.06 us
    ppermute x4, waiting for transfers between devices, along_x(): return lax.ppermute(part, 'enc', swap_x)  2.83 us
    pallas_call x1, Pallas kernels, split_the_text(): local_call(functools.partial(split_text, n_blocks, pieces, where), [IN_HB...  1.6 us
  transfers between devices with their start and end apart: 23, of which 10 were waited for; matrix products, arithmetic and copies ran while one was open for 0% of the time, Pallas kernels for 14%

profile of v3, /device:TPU:0, one launch (start us, length us, event | category | flops | bytes accessed | tf_op | source)
XLA Modules:
  0.0 56.2 jit_solution(573369830450371314)
XLA Ops:
  0.6 1.1 %shard_map.86 = (bf16[2,8,16,512]{3,2,1,0:T(8,128)(2,1)S(1)}, bf16[2,8,16,512]{3,2,1,0:T(8,128)(2,1)S(1)}) custom-call(bf16[8,16,1024]{2,1,0:T(8,128)(2,1)} %k_ref.1, bf16[8,16,1024]{2,1,0:T(8,128)(2,1)} %v_ref.1), custom_call_target="tpu_custom_call" | custom-call | bytes 524288 | tf_op jit(solution)/shard_map/pallas_call | solution.py:438
  1.8 0.5 collective-permute-start
  2.3 1.6 %shard_map.85 = (bf16[272,2048]{1,0:T(8,128)(2,1)S(1)}, bf16[144,2048]{1,0:T(8,128)(2,1)S(1)}, bf16[128,2048]{1,0:T(8,128)(2,1)S(1)}, bf16[2,256,128]{2,1,0:T(8,128)(2,1)S(1)}) custom-call(bf16[1,128,4096]{2,1,0:T(8,128)(2,1)} %q_ref.1, bf16[1,128,4096]{2,1,0:T(8,128)(2,1)} %g_ref.1, s32[1,128]{1,0:T(1,128)} %samp_hbm.1, s32[1,2]{1,0:T(1,128)} %tiles_hbm.1), custom_call_target="tpu_custom_call" | custom-call | bytes 4194304 | tf_op jit(solution)/shard_map/pallas_call | solution.py:399
  3.9 0.0 collective-permute-done.got
  3.9 0.1 shard_map.87
  4.0 0.1 collective-permute-start.1
  4.1 3.0 %collective-permute-start.2 = (bf16[2,64,512]{2,1,0:T(8,128)(2,1)S(1)}, bf16[2,64,512]{2,1,0:T(8,128)(2,1)S(1)}, u32[]{:S(2)}, u32[]{:S(2)}) collective-permute-start(bf16[2,64,512]{2,1,0:T(8,128)(2,1)S(1)} %get-tuple-element.49), channel_id=1, source_target_pairs={{0,2},{1,3},{2,0},{3,1},{4,6},{5,7},{6,4},{7,5},{8,10},{9,11},{10,... | collective-permute-start | bytes 393224 | tf_op jit(solution)/shard_map/ppermute | solution.py:427
  7.1 2.6 %collective-permute-start.4 = (bf16[2,64,512]{2,1,0:T(8,128)(2,1)S(1)}, bf16[2,64,512]{2,1,0:T(8,128)(2,1)S(1)}, u32[]{:S(2)}, u32[]{:S(2)}) collective-permute-start(bf16[2,64,512]{2,1,0:T(8,128)(2,1)S(1)} %get-tuple-element.52), channel_id=1, source_target_pairs={{0,4},{1,5},{2,6},{3,7},{4,0},{5,1},{6,2},{7,3},{8,12},{9,13},{10,... | collective-permute-start | bytes 393224 | tf_op jit(solution)/shard_map/ppermute | solution.py:427
  9.7 0.0 collective-permute-start.5
  9.7 3.0 %collective-permute-done.2.refs_1_ = bf16[2,64,512]{2,1,0:T(8,128)(2,1)S(1)} collective-permute-done((bf16[2,64,512]{2,1,0:T(8,128)(2,1)S(1)}, bf16[2,64,512]{2,1,0:T(8,128)(2,1)S(1)}, u32[]{:S(2)}, u32[]{:S(2)}) %collective-permute-start.2) | collective-permute-done | bytes 131104 | tf_op jit(solution)/shard_map/ppermute | solution.py:427
  12.7 0.0 collective-permute-done.1.refs_2_.got
  12.7 1.8 %collective-permute-start.6 = (bf16[128,512]{1,0:T(8,128)(2,1)S(1)}, bf16[128,512]{1,0:T(8,128)(2,1)S(1)}, u32[]{:S(2)}, u32[]{:S(2)}) collective-permute-start(bf16[128,512]{1,0:T(8,128)(2,1)S(1)} %get-tuple-element.50.rest_0_), channel_id=1, source_target_pairs={{0,16},{8,24},{16,0},{24,8},{1,17},{9,25},{17,1},{25,9},{2,18},{10... | collective-permute-start | bytes 393224 | tf_op jit(solution)/shard_map/ppermute | solution.py:433
  14.5 1.4 %collective-permute-start.7 = (bf16[128,512]{1,0:T(8,128)(2,1)S(1)}, bf16[128,512]{1,0:T(8,128)(2,1)S(1)}, u32[]{:S(2)}, u32[]{:S(2)}) collective-permute-start(bf16[128,512]{1,0:T(8,128)(2,1)S(1)} %get-tuple-element.51), channel_id=1, source_target_pairs={{0,17},{1,16},{2,19},{3,18},{4,21},{5,20},{6,23},{7,22},{8,25},{9,... | collective-permute-start | bytes 393224 | tf_op jit(solution)/shard_map/ppermute | solution.py:436
  15.9 0.3 collective-permute-start.3
  16.3 3.8 %collective-permute-done.4.refs_0_ = bf16[2,64,512]{2,1,0:T(8,128)(2,1)S(1)} collective-permute-done((bf16[2,64,512]{2,1,0:T(8,128)(2,1)S(1)}, bf16[2,64,512]{2,1,0:T(8,128)(2,1)S(1)}, u32[]{:S(2)}, u32[]{:S(2)}) %collective-permute-start.4) | collective-permute-done | bytes 131104 | tf_op jit(solution)/shard_map/ppermute | solution.py:427
  20.0 0.3 collective-permute-done.7.refs_4_.rest_1_.rest_5_
  20.4 1.6 %collective-permute-start.8 = (bf16[128,512]{1,0:T(8,128)(2,1)S(1)}, bf16[128,512]{1,0:T(8,128)(2,1)S(1)}, u32[]{:S(2)}, u32[]{:S(2)}) collective-permute-start(bf16[128,512]{1,0:T(8,128)(2,1)S(1)} %get-tuple-element.55), channel_id=1, source_target_pairs={{0,1},{1,0},{2,3},{3,2},{4,5},{5,4},{6,7},{7,6},{8,9},{9,8},{10,11... | collective-permute-start | bytes 393224 | tf_op jit(solution)/shard_map/ppermute | solution.py:430
  22.0 1.2 %collective-permute-start.9 = (bf16[128,512]{1,0:T(8,128)(2,1)S(1)}, bf16[128,512]{1,0:T(8,128)(2,1)S(1)}, u32[]{:S(2)}, u32[]{:S(2)}) collective-permute-start(bf16[128,512]{1,0:T(8,128)(2,1)S(1)} %get-tuple-element.54.rest_2_), channel_id=1, source_target_pairs={{0,16},{8,24},{16,0},{24,8},{1,17},{9,25},{17,1},{25,9},{2,18},{10... | collective-permute-start | bytes 393224 | tf_op jit(solution)/shard_map/ppermute | solution.py:433
  23.1 0.8 %collective-permute-start.10 = (bf16[128,512]{1,0:T(8,128)(2,1)S(1)}, bf16[128,512]{1,0:T(8,128)(2,1)S(1)}, u32[]{:S(2)}, u32[]{:S(2)}) collective-permute-start(bf16[128,512]{1,0:T(8,128)(2,1)S(1)} %get-tuple-element.55), channel_id=1, source_target_pairs={{0,17},{1,16},{2,19},{3,18},{4,21},{5,20},{6,23},{7,22},{8,25},{9,... | collective-permute-start | bytes 393224 | tf_op jit(solution)/shard_map/ppermute | solution.py:436
  24.0 1.9 %collective-permute-done.8.rest_3_ = bf16[128,512]{1,0:T(8,128)(2,1)S(1)} collective-permute-done((bf16[128,512]{1,0:T(8,128)(2,1)S(1)}, bf16[128,512]{1,0:T(8,128)(2,1)S(1)}, u32[]{:S(2)}, u32[]{:S(2)}) %collective-permute-start.8) | collective-permute-done | bytes 131104 | tf_op jit(solution)/shard_map/ppermute | solution.py:430
  25.9 3.8 %shard_map.90 = (bf16[4,256,1024]{2,1,0:T(8,128)(2,1)S(1)}, f32[256,512]{1,0:T(8,128)S(1)}, bf16[128,512]{1,0:T(8,128)(2,1)S(1)}, bf16[128,512]{1,0:T(8,128)(2,1)S(1)}) custom-call(bf16[2,256,128]{2,1,0:T(8,128)(2,1)S(1)} %get-tuple-element.56.bias, bf16[144,2048]{1,0:T(8,128)(2,1)S(1)} %get-tuple-element.43.q_a, ...), custom_call_target="tpu_custom_call" | custom-call | flops 1073741824 | bytes 16777216 | tf_op jit(solution)/shard_map/pallas_call | solution.py:55
  29.7 0.0 collective-permute-done.9.rest_2_.rest_6_
  29.7 0.4 shard_map.91
  30.1 3.5 %collective-permute-start.13 = (bf16[128,512]{1,0:T(8,128)(2,1)S(1)}, bf16[128,512]{1,0:T(8,128)(2,1)S(1)}, u32[]{:S(2)}, u32[]{:S(2)}) collective-permute-start(bf16[128,512]{1,0:T(8,128)(2,1)S(1)} %shard_map.93), channel_id=1, source_target_pairs={{0,1},{1,0},{2,3},{3,2},{4,5},{5,4},{6,7},{7,6},{8,9},{9,8},{10,11... | collective-permute-start | bytes 393224 | tf_op jit(solution)/shard_map/ppermute | solution.py:430
  33.6 0.0 collective-permute-start.11
  33.7 1.5 %collective-permute-start.12 = (bf16[128,512]{1,0:T(8,128)(2,1)S(1)}, bf16[128,512]{1,0:T(8,128)(2,1)S(1)}, u32[]{:S(2)}, u32[]{:S(2)}) collective-permute-start(bf16[128,512]{1,0:T(8,128)(2,1)S(1)} %get-tuple-element.64), channel_id=1, source_target_pairs={{0,17},{1,16},{2,19},{3,18},{4,21},{5,20},{6,23},{7,22},{8,25},{9,... | collective-permute-start | bytes 393224 | tf_op jit(solution)/shard_map/ppermute | solution.py:436
  35.2 1.9 %collective-permute-start.16 = (bf16[128,512]{1,0:T(8,128)(2,1)S(1)}, bf16[128,512]{1,0:T(8,128)(2,1)S(1)}, u32[]{:S(2)}, u32[]{:S(2)}) collective-permute-start(bf16[128,512]{1,0:T(8,128)(2,1)S(1)} %shard_map.95), channel_id=1, source_target_pairs={{0,1},{1,0},{2,3},{3,2},{4,5},{5,4},{6,7},{7,6},{8,9},{9,8},{10,11... | collective-permute-start | bytes 393224 | tf_op jit(solution)/shard_map/ppermute | solution.py:430
  37.1 0.0 collective-permute-start.14
  37.2 0.9 %collective-permute-done.13.back_x = bf16[128,512]{1,0:T(8,128)(2,1)S(1)} collective-permute-done((bf16[128,512]{1,0:T(8,128)(2,1)S(1)}, bf16[128,512]{1,0:T(8,128)(2,1)S(1)}, u32[]{:S(2)}, u32[]{:S(2)}) %collective-permute-start.13) | collective-permute-done | bytes 131104 | tf_op jit(solution)/shard_map/ppermute | solution.py:430
  38.1 1.4 %collective-permute-start.15 = (bf16[128,512]{1,0:T(8,128)(2,1)S(1)}, bf16[128,512]{1,0:T(8,128)(2,1)S(1)}, u32[]{:S(2)}, u32[]{:S(2)}) collective-permute-start(bf16[128,512]{1,0:T(8,128)(2,1)S(1)} %get-tuple-element.68), channel_id=1, source_target_pairs={{0,17},{1,16},{2,19},{3,18},{4,21},{5,20},{6,23},{7,22},{8,25},{9,... | collective-permute-start | bytes 393224 | tf_op jit(solution)/shard_map/ppermute | solution.py:436
  39.5 1.3 %collective-permute-done.11.back_y = bf16[128,512]{1,0:T(8,128)(2,1)S(1)} collective-permute-done((bf16[128,512]{1,0:T(8,128)(2,1)S(1)}, bf16[128,512]{1,0:T(8,128)(2,1)S(1)}, u32[]{:S(2)}, u32[]{:S(2)}) %collective-permute-start.11) | collective-permute-done | bytes 131104 | tf_op jit(solution)/shard_map/ppermute | solution.py:433
  40.7 0.1 shard_map.94
  40.8 5.2 %collective-permute-start.20 = (bf16[2,64,512]{2,1,0:T(8,128)(2,1)S(1)}, bf16[2,64,512]{2,1,0:T(8,128)(2,1)S(1)}, u32[]{:S(2)}, u32[]{:S(2)}) collective-permute-start(bf16[2,64,512]{2,1,0:T(8,128)(2,1)S(1)} %get-tuple-element.66.refs_0_), channel_id=1, source_target_pairs={{0,4},{1,5},{2,6},{3,7},{4,0},{5,1},{6,2},{7,3},{8,12},{9,13},{10,... | collective-permute-start | bytes 393224 | tf_op jit(solution)/shard_map/ppermute | solution.py:427
  46.0 1.1 %collective-permute-start.21 = (bf16[2,64,512]{2,1,0:T(8,128)(2,1)S(1)}, bf16[2,64,512]{2,1,0:T(8,128)(2,1)S(1)}, u32[]{:S(2)}, u32[]{:S(2)}) collective-permute-start(bf16[2,64,512]{2,1,0:T(8,128)(2,1)S(1)} %get-tuple-element.75), channel_id=1, source_target_pairs={{0,6},{1,7},{2,4},{3,5},{4,2},{5,3},{6,0},{7,1},{8,14},{9,15},{10,... | collective-permute-start | bytes 393224 | tf_op jit(solution)/shard_map/ppermute | solution.py:427
  47.1 0.0 collective-permute-done.16.back_x
  47.1 0.0 collective-permute-done.14.back_y
  47.1 0.1 shard_map.96
  47.2 0.3 collective-permute-start.19
  47.5 1.2 %shard_map.92 = (bf16[128,2048]{1,0:T(8,128)(2,1)S(1)}, bf16[128,2048]{1,0:T(8,128)(2,1)S(1)}) custom-call(bf16[144,2048]{1,0:T(8,128)(2,1)S(1)} %get-tuple-element.43.q_a, bf16[272,2048]{1,0:T(8,128)(2,1)S(1)} %collective-permute-done.1.refs_2_.got, bf16[128,512]{1,0:T(8,128)(2,1)S(1)} %get-tuple-element.50.rest_0_, ...), custom_call_target="tpu_custom_call" | custom-call | flops 536870912 | bytes 8388608 | tf_op jit(solution)/shard_map/pallas_call | solution.py:55
  48.7 0.1 collective-permute-start.17
  48.8 0.5 collective-permute-start.18
  49.3 0.2 collective-permute-done.20.refs_0_
  49.5 3.5 %collective-permute-done.21.refs_1_ = bf16[2,64,512]{2,1,0:T(8,128)(2,1)S(1)} collective-permute-done((bf16[2,64,512]{2,1,0:T(8,128)(2,1)S(1)}, bf16[2,64,512]{2,1,0:T(8,128)(2,1)S(1)}, u32[]{:S(2)}, u32[]{:S(2)}) %collective-permute-start.21) | collective-permute-done | bytes 131104 | tf_op jit(solution)/shard_map/ppermute | solution.py:427
  53.0 0.6 %collective-permute-done.19.refs_1_ = bf16[2,64,512]{2,1,0:T(8,128)(2,1)S(1)} collective-permute-done((bf16[2,64,512]{2,1,0:T(8,128)(2,1)S(1)}, bf16[2,64,512]{2,1,0:T(8,128)(2,1)S(1)}, u32[]{:S(2)}, u32[]{:S(2)}) %collective-permute-start.19) | collective-permute-done | bytes 131104 | tf_op jit(solution)/shard_map/ppermute | solution.py:427
  53.6 0.1 collective-permute-start.22
  53.7 1.0 %shard_map.98 = (bf16[1,128,4096]{2,1,0:T(8,128)(2,1)}, f32[8,128]{1,0:T(8,128)S(1)}) custom-call(bf16[128,2048]{1,0:T(8,128)(2,1)S(1)} %get-tuple-element.61.mine, bf16[64,2048]{1,0:T(8,128)(2,1)S(1)} %collective-permute-done.17.refs_0_, bf16[64,2048]{1,0:T(8,128)(2,1)S(1)} %collective-permute-done.18.refs_1_), custom_call_target="tpu_custom_call" | custom-call | bytes 524288 | tf_op jit(solution)/shard_map/pallas_call | solution.py:535
  54.8 0.5 collective-permute-done.22.got
  55.2 0.8 %shard_map.101 = (bf16[8,16,1024]{2,1,0:T(8,128)(2,1)}, bf16[8,16,1024]{2,1,0:T(8,128)(2,1)}) custom-call(bf16[2,8,16,512]{3,2,1,0:T(8,128)(2,1)S(1)} %get-tuple-element.78.mine, bf16[2,8,16,512]{3,2,1,0:T(8,128)(2,1)S(1)} %collective-permute-done.22.got, f32[8,128]{1,0:T(8,128)S(1)} %get-tuple-element.80._), custom_call_target="tpu_custom_call" | custom-call | bytes 524288 | tf_op jit(solution)/shard_map/pallas_call | solution.py:550
  (15 shorter events, 0.2 us)
Async XLA Ops:
  1.8 2.1 %collective-permute-start = (bf16[2,8,16,512]{3,2,1,0:T(8,128)(2,1)S(1)}, bf16[2,8,16,512]{3,2,1,0:T(8,128)(2,1)S(1)}, u32[]{:S(2)}, u32[]{:S(2)}) collective-permute-start(bf16[2,8,16,512]{3,2,1,0:T(8,128)(2,1)S(1)} %get-tuple-element.45), channel_id=1, source_target_pairs={{0,8},{8,0},{16,24},{24,16},{1,9},{9,1},{17,25},{25,17},{2,10},{10... | collective-permute-start | bytes 786440 | tf_op jit(solution)/shard_map/ppermute | solution.py:449
  4.0 8.7 %collective-permute-start.1 = (bf16[272,2048]{1,0:T(8,128)(2,1)S(1)}, bf16[272,2048]{1,0:T(8,128)(2,1)S(1)}, u32[]{:S(2)}, u32[]{:S(2)}) collective-permute-start(bf16[272,2048]{1,0:T(8,128)(2,1)S(1)} %get-tuple-element.47), channel_id=1, source_target_pairs={{0,8},{8,0},{16,24},{24,16},{1,9},{9,1},{17,25},{25,17},{2,10},{10... | collective-permute-start | bytes 3342344 | tf_op jit(solution)/shard_map/ppermute | solution.py:450
  4.1 8.6 %collective-permute-start.2 = (bf16[2,64,512]{2,1,0:T(8,128)(2,1)S(1)}, bf16[2,64,512]{2,1,0:T(8,128)(2,1)S(1)}, u32[]{:S(2)}, u32[]{:S(2)}) collective-permute-start(bf16[2,64,512]{2,1,0:T(8,128)(2,1)S(1)} %get-tuple-element.49), channel_id=1, source_target_pairs={{0,2},{1,3},{2,0},{3,1},{4,6},{5,7},{6,4},{7,5},{8,10},{9,11},{10,... | collective-permute-start | bytes 393224 | tf_op jit(solution)/shard_map/ppermute | solution.py:427
  7.1 12.9 %collective-permute-start.4 = (bf16[2,64,512]{2,1,0:T(8,128)(2,1)S(1)}, bf16[2,64,512]{2,1,0:T(8,128)(2,1)S(1)}, u32[]{:S(2)}, u32[]{:S(2)}) collective-permute-start(bf16[2,64,512]{2,1,0:T(8,128)(2,1)S(1)} %get-tuple-element.52), channel_id=1, source_target_pairs={{0,4},{1,5},{2,6},{3,7},{4,0},{5,1},{6,2},{7,3},{8,12},{9,13},{10,... | collective-permute-start | bytes 393224 | tf_op jit(solution)/shard_map/ppermute | solution.py:427
  9.7 10.3 %collective-permute-start.5 = (bf16[2,64,512]{2,1,0:T(8,128)(2,1)S(1)}, bf16[2,64,512]{2,1,0:T(8,128)(2,1)S(1)}, u32[]{:S(2)}, u32[]{:S(2)}) collective-permute-start(bf16[2,64,512]{2,1,0:T(8,128)(2,1)S(1)} %get-tuple-element.53), channel_id=1, source_target_pairs={{0,6},{1,7},{2,4},{3,5},{4,2},{5,3},{6,0},{7,1},{8,14},{9,15},{10,... | collective-permute-start | bytes 393224 | tf_op jit(solution)/shard_map/ppermute | solution.py:427
  12.7 7.3 %collective-permute-start.6 = (bf16[128,512]{1,0:T(8,128)(2,1)S(1)}, bf16[128,512]{1,0:T(8,128)(2,1)S(1)}, u32[]{:S(2)}, u32[]{:S(2)}) collective-permute-start(bf16[128,512]{1,0:T(8,128)(2,1)S(1)} %get-tuple-element.50.rest_0_), channel_id=1, source_target_pairs={{0,16},{8,24},{16,0},{24,8},{1,17},{9,25},{17,1},{25,9},{2,18},{10... | collective-permute-start | bytes 393224 | tf_op jit(solution)/shard_map/ppermute | solution.py:433
  14.5 5.9 %collective-permute-start.7 = (bf16[128,512]{1,0:T(8,128)(2,1)S(1)}, bf16[128,512]{1,0:T(8,128)(2,1)S(1)}, u32[]{:S(2)}, u32[]{:S(2)}) collective-permute-start(bf16[128,512]{1,0:T(8,128)(2,1)S(1)} %get-tuple-element.51), channel_id=1, source_target_pairs={{0,17},{1,16},{2,19},{3,18},{4,21},{5,20},{6,23},{7,22},{8,25},{9,... | collective-permute-start | bytes 393224 | tf_op jit(solution)/shard_map/ppermute | solution.py:436
  15.9 8.0 %collective-permute-start.3 = (bf16[128,512]{1,0:T(8,128)(2,1)S(1)}, bf16[128,512]{1,0:T(8,128)(2,1)S(1)}, u32[]{:S(2)}, u32[]{:S(2)}) collective-permute-start(bf16[128,512]{1,0:T(8,128)(2,1)S(1)} %get-tuple-element.51), channel_id=1, source_target_pairs={{0,1},{1,0},{2,3},{3,2},{4,5},{5,4},{6,7},{7,6},{8,9},{9,8},{10,11... | collective-permute-start | bytes 393224 | tf_op jit(solution)/shard_map/ppermute | solution.py:430
  20.4 5.5 %collective-permute-start.8 = (bf16[128,512]{1,0:T(8,128)(2,1)S(1)}, bf16[128,512]{1,0:T(8,128)(2,1)S(1)}, u32[]{:S(2)}, u32[]{:S(2)}) collective-permute-start(bf16[128,512]{1,0:T(8,128)(2,1)S(1)} %get-tuple-element.55), channel_id=1, source_target_pairs={{0,1},{1,0},{2,3},{3,2},{4,5},{5,4},{6,7},{7,6},{8,9},{9,8},{10,11... | collective-permute-start | bytes 393224 | tf_op jit(solution)/shard_map/ppermute | solution.py:430
  22.0 7.7 %collective-permute-start.9 = (bf16[128,512]{1,0:T(8,128)(2,1)S(1)}, bf16[128,512]{1,0:T(8,128)(2,1)S(1)}, u32[]{:S(2)}, u32[]{:S(2)}) collective-permute-start(bf16[128,512]{1,0:T(8,128)(2,1)S(1)} %get-tuple-element.54.rest_2_), channel_id=1, source_target_pairs={{0,16},{8,24},{16,0},{24,8},{1,17},{9,25},{17,1},{25,9},{2,18},{10... | collective-permute-start | bytes 393224 | tf_op jit(solution)/shard_map/ppermute | solution.py:433
  23.1 6.6 %collective-permute-start.10 = (bf16[128,512]{1,0:T(8,128)(2,1)S(1)}, bf16[128,512]{1,0:T(8,128)(2,1)S(1)}, u32[]{:S(2)}, u32[]{:S(2)}) collective-permute-start(bf16[128,512]{1,0:T(8,128)(2,1)S(1)} %get-tuple-element.55), channel_id=1, source_target_pairs={{0,17},{1,16},{2,19},{3,18},{4,21},{5,20},{6,23},{7,22},{8,25},{9,... | collective-permute-start | bytes 393224 | tf_op jit(solution)/shard_map/ppermute | solution.py:436
  30.1 8.0 %collective-permute-start.13 = (bf16[128,512]{1,0:T(8,128)(2,1)S(1)}, bf16[128,512]{1,0:T(8,128)(2,1)S(1)}, u32[]{:S(2)}, u32[]{:S(2)}) collective-permute-start(bf16[128,512]{1,0:T(8,128)(2,1)S(1)} %shard_map.93), channel_id=1, source_target_pairs={{0,1},{1,0},{2,3},{3,2},{4,5},{5,4},{6,7},{7,6},{8,9},{9,8},{10,11... | collective-permute-start | bytes 393224 | tf_op jit(solution)/shard_map/ppermute | solution.py:430
  33.6 7.1 %collective-permute-start.11 = (bf16[128,512]{1,0:T(8,128)(2,1)S(1)}, bf16[128,512]{1,0:T(8,128)(2,1)S(1)}, u32[]{:S(2)}, u32[]{:S(2)}) collective-permute-start(bf16[128,512]{1,0:T(8,128)(2,1)S(1)} %get-tuple-element.63), channel_id=1, source_target_pairs={{0,16},{8,24},{16,0},{24,8},{1,17},{9,25},{17,1},{25,9},{2,18},{10... | collective-permute-start | bytes 393224 | tf_op jit(solution)/shard_map/ppermute | solution.py:433
  33.7 7.1 %collective-permute-start.12 = (bf16[128,512]{1,0:T(8,128)(2,1)S(1)}, bf16[128,512]{1,0:T(8,128)(2,1)S(1)}, u32[]{:S(2)}, u32[]{:S(2)}) collective-permute-start(bf16[128,512]{1,0:T(8,128)(2,1)S(1)} %get-tuple-element.64), channel_id=1, source_target_pairs={{0,17},{1,16},{2,19},{3,18},{4,21},{5,20},{6,23},{7,22},{8,25},{9,... | collective-permute-start | bytes 393224 | tf_op jit(solution)/shard_map/ppermute | solution.py:436
  35.2 11.9 %collective-permute-start.16 = (bf16[128,512]{1,0:T(8,128)(2,1)S(1)}, bf16[128,512]{1,0:T(8,128)(2,1)S(1)}, u32[]{:S(2)}, u32[]{:S(2)}) collective-permute-start(bf16[128,512]{1,0:T(8,128)(2,1)S(1)} %shard_map.95), channel_id=1, source_target_pairs={{0,1},{1,0},{2,3},{3,2},{4,5},{5,4},{6,7},{7,6},{8,9},{9,8},{10,11... | collective-permute-start | bytes 393224 | tf_op jit(solution)/shard_map/ppermute | solution.py:430
  37.1 9.9 %collective-permute-start.14 = (bf16[128,512]{1,0:T(8,128)(2,1)S(1)}, bf16[128,512]{1,0:T(8,128)(2,1)S(1)}, u32[]{:S(2)}, u32[]{:S(2)}) collective-permute-start(bf16[128,512]{1,0:T(8,128)(2,1)S(1)} %get-tuple-element.67), channel_id=1, source_target_pairs={{0,16},{8,24},{16,0},{24,8},{1,17},{9,25},{17,1},{25,9},{2,18},{10... | collective-permute-start | bytes 393224 | tf_op jit(solution)/shard_map/ppermute | solution.py:433
  38.1 9.0 %collective-permute-start.15 = (bf16[128,512]{1,0:T(8,128)(2,1)S(1)}, bf16[128,512]{1,0:T(8,128)(2,1)S(1)}, u32[]{:S(2)}, u32[]{:S(2)}) collective-permute-start(bf16[128,512]{1,0:T(8,128)(2,1)S(1)} %get-tuple-element.68), channel_id=1, source_target_pairs={{0,17},{1,16},{2,19},{3,18},{4,21},{5,20},{6,23},{7,22},{8,25},{9,... | collective-permute-start | bytes 393224 | tf_op jit(solution)/shard_map/ppermute | solution.py:436
  40.8 8.7 %collective-permute-start.20 = (bf16[2,64,512]{2,1,0:T(8,128)(2,1)S(1)}, bf16[2,64,512]{2,1,0:T(8,128)(2,1)S(1)}, u32[]{:S(2)}, u32[]{:S(2)}) collective-permute-start(bf16[2,64,512]{2,1,0:T(8,128)(2,1)S(1)} %get-tuple-element.66.refs_0_), channel_id=1, source_target_pairs={{0,4},{1,5},{2,6},{3,7},{4,0},{5,1},{6,2},{7,3},{8,12},{9,13},{10,... | collective-permute-start | bytes 393224 | tf_op jit(solution)/shard_map/ppermute | solution.py:427
  46.0 6.9 %collective-permute-start.21 = (bf16[2,64,512]{2,1,0:T(8,128)(2,1)S(1)}, bf16[2,64,512]{2,1,0:T(8,128)(2,1)S(1)}, u32[]{:S(2)}, u32[]{:S(2)}) collective-permute-start(bf16[2,64,512]{2,1,0:T(8,128)(2,1)S(1)} %get-tuple-element.75), channel_id=1, source_target_pairs={{0,6},{1,7},{2,4},{3,5},{4,2},{5,3},{6,0},{7,1},{8,14},{9,15},{10,... | collective-permute-start | bytes 393224 | tf_op jit(solution)/shard_map/ppermute | solution.py:427
  47.2 6.4 %collective-permute-start.19 = (bf16[2,64,512]{2,1,0:T(8,128)(2,1)S(1)}, bf16[2,64,512]{2,1,0:T(8,128)(2,1)S(1)}, u32[]{:S(2)}, u32[]{:S(2)}) collective-permute-start(bf16[2,64,512]{2,1,0:T(8,128)(2,1)S(1)} %get-tuple-element.74), channel_id=1, source_target_pairs={{0,2},{1,3},{2,0},{3,1},{4,6},{5,7},{6,4},{7,5},{8,10},{9,11},{10,... | collective-permute-start | bytes 393224 | tf_op jit(solution)/shard_map/ppermute | solution.py:427
  48.7 5.0 %collective-permute-start.17 = (bf16[64,2048]{1,0:T(8,128)(2,1)S(1)}, bf16[64,2048]{1,0:T(8,128)(2,1)S(1)}, u32[]{:S(2)}, u32[]{:S(2)}) collective-permute-start(bf16[64,2048]{1,0:T(8,128)(2,1)S(1)} %get-tuple-element.71), channel_id=1, source_target_pairs={{0,8},{8,0},{16,24},{24,16},{1,9},{9,1},{17,25},{25,17},{2,10},{10... | collective-permute-start | bytes 786440 | tf_op jit(solution)/shard_map/ppermute | solution.py:482
  48.8 5.0 %collective-permute-start.18 = (bf16[64,2048]{1,0:T(8,128)(2,1)S(1)}, bf16[64,2048]{1,0:T(8,128)(2,1)S(1)}, u32[]{:S(2)}, u32[]{:S(2)}) collective-permute-start(bf16[64,2048]{1,0:T(8,128)(2,1)S(1)} %get-tuple-element.72), channel_id=1, source_target_pairs={{0,8},{8,0},{16,24},{24,16},{1,9},{9,1},{17,25},{25,17},{2,10},{10... | collective-permute-start | bytes 786440 | tf_op jit(solution)/shard_map/ppermute | solution.py:482
  53.6 1.6 %collective-permute-start.22 = (bf16[2,8,16,512]{3,2,1,0:T(8,128)(2,1)S(1)}, bf16[2,8,16,512]{3,2,1,0:T(8,128)(2,1)S(1)}, u32[]{:S(2)}, u32[]{:S(2)}) collective-permute-start(bf16[2,8,16,512]{3,2,1,0:T(8,128)(2,1)S(1)} %get-tuple-element.79), channel_id=1, source_target_pairs={{0,8},{8,0},{16,24},{24,16},{1,9},{9,1},{17,25},{25,17},{2,10},{10... | collective-permute-start | bytes 786440 | tf_op jit(solution)/shard_map/ppermute | solution.py:555

commit v4 on v3

--- a/solution.py
+++ b/solution.py
@@ -304,11 +304,10 @@
             gp = lax.dot_general(v, g, NT, preferred_element_type=F32)
             return q, g, s, gp
 
-        early = len(which) == 1
         ahead = products(0)
         for h in range(HALF_KV):
             q, g, s, gp = ahead
-            if early and h + 1 < HALF_KV:
+            if h + 1 < HALF_KV:
                 ahead = products(h + 1)
             top = jnp.max(s, axis=0, keepdims=True)
             e = jnp.exp2((s - top) * (SCALE * LOG2E))
@@ -329,8 +328,6 @@
                 out, first = grads[dx], at * 2 * block_rows
                 out[first : first + block_rows, cols] = dk[block].astype(out.dtype)
                 out[first + block_rows : first + 2 * block_rows, cols] = dv[block].astype(out.dtype)
-            if not early and h + 1 < HALF_KV:
-                ahead = products(h + 1)
 
     choose(present, one_pass)
 

time: 56.3 us -> 56.1 us (level)
  starting transfers between devices: 29.1 us -> 26 us
  Pallas kernels: 10.2 us -> 12.3 us
  waiting for transfers between devices: 16 us -> 17.1 us
    ppermute x4, starting transfers between devices: 7.36 us -> 2.02 us  [along_x(): return lax.ppermute(part, 'enc', swap_x)]
    ppermute x4, starting transfers between devices: 3.06 us -> 5.48 us  [along_y(): return lax.ppermute(part, 'ctx', swap_y)]
    ppermute x4, waiting for transfers between devices: 0.35 us -> 2.5 us  [along_xy(): return lax.ppermute(part, ('ctx', 'enc'), swap_xy)]
    pallas_call x13, Pallas kernels: 5.65 us -> 7.75 us  [call(): return local_call(body, [IN_VMEM] * len(args), spec, **more)(*args)]
    ppermute x4, waiting for transfers between devices: 1.27 us -> 0.01 us  [along_y(): return lax.ppermute(part, 'ctx', swap_y)]
    ppermute x4, waiting for transfers between devices: 2.83 us -> 3.59 us  [along_x(): return lax.ppermute(part, 'enc', swap_x)]
    ppermute x6, waiting for transfers between devices: 11 us -> 10.5 us  [along_z(): lax.ppermute(part, 'enc', [(i, i ^ 2 * dz) for i in range(n_enc)])]
  transfers between devices with their start and end apart: 23 -> 23, of which waited for: 10 -> 10; matrix products, arithmetic and copies ran while one was open for 0% -> 0% of each run, Pallas kernels for 14% -> 11%
where the time goes in v4:
time: 56.1 us; the launch traced here: 56.4 us
  starting transfers between devices  26 us (46%)
  waiting for transfers between devices  17.1 us (30%)
  Pallas kernels  12.3 us (22%)
  between operations  0.97 us (2%)
    ppermute x6, starting transfers between devices, along_z(): lax.ppermute(part, 'enc', [(i, i ^ 2 * dz) for i in range(n_enc)])  12.1 us
    ppermute x6, waiting for transfers between devices, along_z(): lax.ppermute(part, 'enc', [(i, i ^ 2 * dz) for i in range(n_enc)])  10.5 us
    pallas_call x13, Pallas kernels, call(): return local_call(body, [IN_VMEM] * len(args), spec, **more)(*args)  7.75 us
    ppermute x4, starting transfers between devices, along_y(): return lax.ppermute(part, 'ctx', swap_y)  5.48 us
    ppermute x4, starting transfers between devices, along_xy(): return lax.ppermute(part, ('ctx', 'enc'), swap_xy)  5.16 us
    ppermute x4, waiting for transfers between devices, along_x(): return lax.ppermute(part, 'enc', swap_x)  3.59 us
    ppermute x4, waiting for transfers between devices, along_xy(): return lax.ppermute(part, ('ctx', 'enc'), swap_xy)  2.5 us
    ppermute x4, starting transfers between devices, along_x(): return lax.ppermute(part, 'enc', swap_x)  2.02 us
  transfers between devices with their start and end apart: 23, of which 10 were waited for; matrix products, arithmetic and copies ran while one was open for 0% of the time, Pallas kernels for 11%

profile of v4, /device:TPU:0, one launch (start us, length us, event | category | flops | bytes accessed | tf_op | source)
XLA Modules:
  0.0 56.4 jit_solution(6420032606655964443)
XLA Ops:
  0.6 1.1 %shard_map.86 = (bf16[2,8,16,512]{3,2,1,0:T(8,128)(2,1)S(1)}, bf16[2,8,16,512]{3,2,1,0:T(8,128)(2,1)S(1)}) custom-call(bf16[8,16,1024]{2,1,0:T(8,128)(2,1)} %k_ref.1, bf16[8,16,1024]{2,1,0:T(8,128)(2,1)} %v_ref.1), custom_call_target="tpu_custom_call" | custom-call | bytes 524288 | tf_op jit(solution)/shard_map/pallas_call | solution.py:435
  1.8 0.5 collective-permute-start
  2.3 1.6 %shard_map.85 = (bf16[272,2048]{1,0:T(8,128)(2,1)S(1)}, bf16[144,2048]{1,0:T(8,128)(2,1)S(1)}, bf16[128,2048]{1,0:T(8,128)(2,1)S(1)}, bf16[2,256,128]{2,1,0:T(8,128)(2,1)S(1)}) custom-call(bf16[1,128,4096]{2,1,0:T(8,128)(2,1)} %q_ref.1, bf16[1,128,4096]{2,1,0:T(8,128)(2,1)} %g_ref.1, s32[1,128]{1,0:T(1,128)} %samp_hbm.1, s32[1,2]{1,0:T(1,128)} %tiles_hbm.1), custom_call_target="tpu_custom_call" | custom-call | bytes 4194304 | tf_op jit(solution)/shard_map/pallas_call | solution.py:396
  3.9 0.0 collective-permute-done.got
  3.9 0.1 shard_map.87
  4.0 0.1 collective-permute-start.1
  4.1 3.0 %collective-permute-start.2 = (bf16[2,64,512]{2,1,0:T(8,128)(2,1)S(1)}, bf16[2,64,512]{2,1,0:T(8,128)(2,1)S(1)}, u32[]{:S(2)}, u32[]{:S(2)}) collective-permute-start(bf16[2,64,512]{2,1,0:T(8,128)(2,1)S(1)} %get-tuple-element.49), channel_id=1, source_target_pairs={{0,2},{1,3},{2,0},{3,1},{4,6},{5,7},{6,4},{7,5},{8,10},{9,11},{10,... | collective-permute-start | bytes 393224 | tf_op jit(solution)/shard_map/ppermute | solution.py:424
  7.1 2.6 %collective-permute-start.4 = (bf16[2,64,512]{2,1,0:T(8,128)(2,1)S(1)}, bf16[2,64,512]{2,1,0:T(8,128)(2,1)S(1)}, u32[]{:S(2)}, u32[]{:S(2)}) collective-permute-start(bf16[2,64,512]{2,1,0:T(8,128)(2,1)S(1)} %get-tuple-element.52), channel_id=1, source_target_pairs={{0,4},{1,5},{2,6},{3,7},{4,0},{5,1},{6,2},{7,3},{8,12},{9,13},{10,... | collective-permute-start | bytes 393224 | tf_op jit(solution)/shard_map/ppermute | solution.py:424
  9.7 0.0 collective-permute-start.5
  9.7 3.0 %collective-permute-done.2.refs_1_ = bf16[2,64,512]{2,1,0:T(8,128)(2,1)S(1)} collective-permute-done((bf16[2,64,512]{2,1,0:T(8,128)(2,1)S(1)}, bf16[2,64,512]{2,1,0:T(8,128)(2,1)S(1)}, u32[]{:S(2)}, u32[]{:S(2)}) %collective-permute-start.2) | collective-permute-done | bytes 131104 | tf_op jit(solution)/shard_map/ppermute | solution.py:424
  12.7 0.0 collective-permute-done.1.refs_2_.got
  12.7 1.8 %collective-permute-start.6 = (bf16[128,512]{1,0:T(8,128)(2,1)S(1)}, bf16[128,512]{1,0:T(8,128)(2,1)S(1)}, u32[]{:S(2)}, u32[]{:S(2)}) collective-permute-start(bf16[128,512]{1,0:T(8,128)(2,1)S(1)} %get-tuple-element.50.rest_0_), channel_id=1, source_target_pairs={{0,16},{8,24},{16,0},{24,8},{1,17},{9,25},{17,1},{25,9},{2,18},{10... | collective-permute-start | bytes 393224 | tf_op jit(solution)/shard_map/ppermute | solution.py:430
  14.5 1.4 %collective-permute-start.7 = (bf16[128,512]{1,0:T(8,128)(2,1)S(1)}, bf16[128,512]{1,0:T(8,128)(2,1)S(1)}, u32[]{:S(2)}, u32[]{:S(2)}) collective-permute-start(bf16[128,512]{1,0:T(8,128)(2,1)S(1)} %get-tuple-element.51), channel_id=1, source_target_pairs={{0,17},{1,16},{2,19},{3,18},{4,21},{5,20},{6,23},{7,22},{8,25},{9,... | collective-permute-start | bytes 393224 | tf_op jit(solution)/shard_map/ppermute | solution.py:433
  15.9 0.3 collective-permute-start.3
  16.3 3.8 %collective-permute-done.4.refs_0_ = bf16[2,64,512]{2,1,0:T(8,128)(2,1)S(1)} collective-permute-done((bf16[2,64,512]{2,1,0:T(8,128)(2,1)S(1)}, bf16[2,64,512]{2,1,0:T(8,128)(2,1)S(1)}, u32[]{:S(2)}, u32[]{:S(2)}) %collective-permute-start.4) | collective-permute-done | bytes 131104 | tf_op jit(solution)/shard_map/ppermute | solution.py:424
  20.0 0.0 collective-permute-done.5.refs_1_
  20.0 0.0 collective-permute-done.6.refs_3_.rest_0_.rest_4_
  20.0 0.3 collective-permute-done.7.refs_4_.rest_1_.rest_5_
  20.4 1.6 %collective-permute-start.8 = (bf16[128,512]{1,0:T(8,128)(2,1)S(1)}, bf16[128,512]{1,0:T(8,128)(2,1)S(1)}, u32[]{:S(2)}, u32[]{:S(2)}) collective-permute-start(bf16[128,512]{1,0:T(8,128)(2,1)S(1)} %get-tuple-element.55), channel_id=1, source_target_pairs={{0,1},{1,0},{2,3},{3,2},{4,5},{5,4},{6,7},{7,6},{8,9},{9,8},{10,11... | collective-permute-start | bytes 393224 | tf_op jit(solution)/shard_map/ppermute | solution.py:427
  22.0 1.2 %collective-permute-start.9 = (bf16[128,512]{1,0:T(8,128)(2,1)S(1)}, bf16[128,512]{1,0:T(8,128)(2,1)S(1)}, u32[]{:S(2)}, u32[]{:S(2)}) collective-permute-start(bf16[128,512]{1,0:T(8,128)(2,1)S(1)} %get-tuple-element.54.rest_2_), channel_id=1, source_target_pairs={{0,16},{8,24},{16,0},{24,8},{1,17},{9,25},{17,1},{25,9},{2,18},{10... | collective-permute-start | bytes 393224 | tf_op jit(solution)/shard_map/ppermute | solution.py:430
  23.1 0.8 %collective-permute-start.10 = (bf16[128,512]{1,0:T(8,128)(2,1)S(1)}, bf16[128,512]{1,0:T(8,128)(2,1)S(1)}, u32[]{:S(2)}, u32[]{:S(2)}) collective-permute-start(bf16[128,512]{1,0:T(8,128)(2,1)S(1)} %get-tuple-element.55), channel_id=1, source_target_pairs={{0,17},{1,16},{2,19},{3,18},{4,21},{5,20},{6,23},{7,22},{8,25},{9,... | collective-permute-start | bytes 393224 | tf_op jit(solution)/shard_map/ppermute | solution.py:433
  24.0 0.0 collective-permute-done.3.rest_1_
  24.0 1.9 %collective-permute-done.8.rest_3_ = bf16[128,512]{1,0:T(8,128)(2,1)S(1)} collective-permute-done((bf16[128,512]{1,0:T(8,128)(2,1)S(1)}, bf16[128,512]{1,0:T(8,128)(2,1)S(1)}, u32[]{:S(2)}, u32[]{:S(2)}) %collective-permute-start.8) | collective-permute-done | bytes 131104 | tf_op jit(solution)/shard_map/ppermute | solution.py:427
  25.9 2.1 %shard_map.90 = (bf16[4,256,1024]{2,1,0:T(8,128)(2,1)S(1)}, f32[256,512]{1,0:T(8,128)S(1)}, bf16[128,512]{1,0:T(8,128)(2,1)S(1)}, bf16[128,512]{1,0:T(8,128)(2,1)S(1)}) custom-call(bf16[2,256,128]{2,1,0:T(8,128)(2,1)S(1)} %get-tuple-element.56.bias, bf16[144,2048]{1,0:T(8,128)(2,1)S(1)} %get-tuple-element.43.q_a, ...), custom_call_target="tpu_custom_call" | custom-call | flops 1073741824 | bytes 16777216 | tf_op jit(solution)/shard_map/pallas_call | solution.py:55
  28.0 1.0 %collective-permute-done.10.rest_3_.rest_7_ = bf16[128,512]{1,0:T(8,128)(2,1)S(1)} collective-permute-done((bf16[128,512]{1,0:T(8,128)(2,1)S(1)}, bf16[128,512]{1,0:T(8,128)(2,1)S(1)}, u32[]{:S(2)}, u32[]{:S(2)}) %collective-permute-start.10) | collective-permute-done | bytes 131104 | tf_op jit(solution)/shard_map/ppermute | solution.py:433
  29.0 3.9 %shard_map.91 = (bf16[4,256,1024]{2,1,0:T(8,128)(2,1)S(1)}, bf16[128,512]{1,0:T(8,128)(2,1)S(1)}, bf16[128,512]{1,0:T(8,128)(2,1)S(1)}, bf16[128,512]{1,0:T(8,128)(2,1)S(1)}, bf16[128,512]{1,0:T(8,128)(2,1)S(1)}) custom-call(bf16[2,256,128]{2,1,0:T(8,128)(2,1)S(1)} %get-tuple-element.56.bias, bf16[144,2048]{1,0:T(8,128)(2,1)S(1)} %get-tuple-element.43.q_a, ...), custom_call_target="tpu_custom_call" | custom-call | flops 1073741824 | bytes 16777216 | tf_op jit(solution)/shard_map/pallas_call | solution.py:55
  32.9 0.1 collective-permute-start.13
  33.0 1.3 %collective-permute-start.11 = (bf16[128,512]{1,0:T(8,128)(2,1)S(1)}, bf16[128,512]{1,0:T(8,128)(2,1)S(1)}, u32[]{:S(2)}, u32[]{:S(2)}) collective-permute-start(bf16[128,512]{1,0:T(8,128)(2,1)S(1)} %get-tuple-element.63), channel_id=1, source_target_pairs={{0,16},{8,24},{16,0},{24,8},{1,17},{9,25},{17,1},{25,9},{2,18},{10... | collective-permute-start | bytes 393224 | tf_op jit(solution)/shard_map/ppermute | solution.py:430
  34.3 2.2 %collective-permute-start.12 = (bf16[128,512]{1,0:T(8,128)(2,1)S(1)}, bf16[128,512]{1,0:T(8,128)(2,1)S(1)}, u32[]{:S(2)}, u32[]{:S(2)}) collective-permute-start(bf16[128,512]{1,0:T(8,128)(2,1)S(1)} %get-tuple-element.64), channel_id=1, source_target_pairs={{0,17},{1,16},{2,19},{3,18},{4,21},{5,20},{6,23},{7,22},{8,25},{9,... | collective-permute-start | bytes 393224 | tf_op jit(solution)/shard_map/ppermute | solution.py:433
  36.5 0.1 collective-permute-start.16
  36.6 1.2 %collective-permute-start.14 = (bf16[128,512]{1,0:T(8,128)(2,1)S(1)}, bf16[128,512]{1,0:T(8,128)(2,1)S(1)}, u32[]{:S(2)}, u32[]{:S(2)}) collective-permute-start(bf16[128,512]{1,0:T(8,128)(2,1)S(1)} %get-tuple-element.67), channel_id=1, source_target_pairs={{0,16},{8,24},{16,0},{24,8},{1,17},{9,25},{17,1},{25,9},{2,18},{10... | collective-permute-start | bytes 393224 | tf_op jit(solution)/shard_map/ppermute | solution.py:430
  37.8 1.7 %collective-permute-done.13.back_x = bf16[128,512]{1,0:T(8,128)(2,1)S(1)} collective-permute-done((bf16[128,512]{1,0:T(8,128)(2,1)S(1)}, bf16[128,512]{1,0:T(8,128)(2,1)S(1)}, u32[]{:S(2)}, u32[]{:S(2)}) %collective-permute-start.13) | collective-permute-done | bytes 131104 | tf_op jit(solution)/shard_map/ppermute | solution.py:427
  39.4 0.7 %collective-permute-start.15 = (bf16[128,512]{1,0:T(8,128)(2,1)S(1)}, bf16[128,512]{1,0:T(8,128)(2,1)S(1)}, u32[]{:S(2)}, u32[]{:S(2)}) collective-permute-start(bf16[128,512]{1,0:T(8,128)(2,1)S(1)} %get-tuple-element.68), channel_id=1, source_target_pairs={{0,17},{1,16},{2,19},{3,18},{4,21},{5,20},{6,23},{7,22},{8,25},{9,... | collective-permute-start | bytes 393224 | tf_op jit(solution)/shard_map/ppermute | solution.py:433
  40.2 1.1 %collective-permute-done.12.back_xy = bf16[128,512]{1,0:T(8,128)(2,1)S(1)} collective-permute-done((bf16[128,512]{1,0:T(8,128)(2,1)S(1)}, bf16[128,512]{1,0:T(8,128)(2,1)S(1)}, u32[]{:S(2)}, u32[]{:S(2)}) %collective-permute-start.12) | collective-permute-done | bytes 131104 | tf_op jit(solution)/shard_map/ppermute | solution.py:433
  41.3 0.1 shard_map.94
  41.4 4.5 %collective-permute-start.20 = (bf16[2,64,512]{2,1,0:T(8,128)(2,1)S(1)}, bf16[2,64,512]{2,1,0:T(8,128)(2,1)S(1)}, u32[]{:S(2)}, u32[]{:S(2)}) collective-permute-start(bf16[2,64,512]{2,1,0:T(8,128)(2,1)S(1)} %get-tuple-element.66.refs_0_), channel_id=1, source_target_pairs={{0,4},{1,5},{2,6},{3,7},{4,0},{5,1},{6,2},{7,3},{8,12},{9,13},{10,... | collective-permute-start | bytes 393224 | tf_op jit(solution)/shard_map/ppermute | solution.py:424
  45.9 1.3 %collective-permute-start.21 = (bf16[2,64,512]{2,1,0:T(8,128)(2,1)S(1)}, bf16[2,64,512]{2,1,0:T(8,128)(2,1)S(1)}, u32[]{:S(2)}, u32[]{:S(2)}) collective-permute-start(bf16[2,64,512]{2,1,0:T(8,128)(2,1)S(1)} %get-tuple-element.75), channel_id=1, source_target_pairs={{0,6},{1,7},{2,4},{3,5},{4,2},{5,3},{6,0},{7,1},{8,14},{9,15},{10,... | collective-permute-start | bytes 393224 | tf_op jit(solution)/shard_map/ppermute | solution.py:424
  47.2 0.1 shard_map.96
  47.3 0.6 %collective-permute-start.19 = (bf16[2,64,512]{2,1,0:T(8,128)(2,1)S(1)}, bf16[2,64,512]{2,1,0:T(8,128)(2,1)S(1)}, u32[]{:S(2)}, u32[]{:S(2)}) collective-permute-start(bf16[2,64,512]{2,1,0:T(8,128)(2,1)S(1)} %get-tuple-element.74), channel_id=1, source_target_pairs={{0,2},{1,3},{2,0},{3,1},{4,6},{5,7},{6,4},{7,5},{8,10},{9,11},{10,... | collective-permute-start | bytes 393224 | tf_op jit(solution)/shard_map/ppermute | solution.py:424
  47.9 1.4 %shard_map.92 = (bf16[128,2048]{1,0:T(8,128)(2,1)S(1)}, bf16[128,2048]{1,0:T(8,128)(2,1)S(1)}) custom-call(bf16[144,2048]{1,0:T(8,128)(2,1)S(1)} %get-tuple-element.43.q_a, bf16[272,2048]{1,0:T(8,128)(2,1)S(1)} %collective-permute-done.1.refs_2_.got, bf16[128,512]{1,0:T(8,128)(2,1)S(1)} %get-tuple-element.50.rest_0_, ...), custom_call_target="tpu_custom_call" | custom-call | flops 536870912 | bytes 8388608 | tf_op jit(solution)/shard_map/pallas_call | solution.py:55
  49.4 0.1 collective-permute-start.17
  49.5 0.5 collective-permute-start.18
  50.0 2.8 %collective-permute-done.21.refs_1_ = bf16[2,64,512]{2,1,0:T(8,128)(2,1)S(1)} collective-permute-done((bf16[2,64,512]{2,1,0:T(8,128)(2,1)S(1)}, bf16[2,64,512]{2,1,0:T(8,128)(2,1)S(1)}, u32[]{:S(2)}, u32[]{:S(2)}) %collective-permute-start.21) | collective-permute-done | bytes 131104 | tf_op jit(solution)/shard_map/ppermute | solution.py:424
  52.9 0.9 %collective-permute-done.19.refs_1_ = bf16[2,64,512]{2,1,0:T(8,128)(2,1)S(1)} collective-permute-done((bf16[2,64,512]{2,1,0:T(8,128)(2,1)S(1)}, bf16[2,64,512]{2,1,0:T(8,128)(2,1)S(1)}, u32[]{:S(2)}, u32[]{:S(2)}) %collective-permute-start.19) | collective-permute-done | bytes 131104 | tf_op jit(solution)/shard_map/ppermute | solution.py:424
  53.8 0.1 collective-permute-start.22
  53.9 1.0 %shard_map.98 = (bf16[1,128,4096]{2,1,0:T(8,128)(2,1)}, f32[8,128]{1,0:T(8,128)S(1)}) custom-call(bf16[128,2048]{1,0:T(8,128)(2,1)S(1)} %get-tuple-element.61.mine, bf16[64,2048]{1,0:T(8,128)(2,1)S(1)} %collective-permute-done.17.refs_0_, bf16[64,2048]{1,0:T(8,128)(2,1)S(1)} %collective-permute-done.18.refs_1_), custom_call_target="tpu_custom_call" | custom-call | bytes 524288 | tf_op jit(solution)/shard_map/pallas_call | solution.py:532
  54.9 0.5 collective-permute-done.22.got
  55.4 0.8 %shard_map.101 = (bf16[8,16,1024]{2,1,0:T(8,128)(2,1)}, bf16[8,16,1024]{2,1,0:T(8,128)(2,1)}) custom-call(bf16[2,8,16,512]{3,2,1,0:T(8,128)(2,1)S(1)} %get-tuple-element.78.mine, bf16[2,8,16,512]{3,2,1,0:T(8,128)(2,1)S(1)} %collective-permute-done.22.got, f32[8,128]{1,0:T(8,128)S(1)} %get-tuple-element.80._), custom_call_target="tpu_custom_call" | custom-call | bytes 524288 | tf_op jit(solution)/shard_map/pallas_call | solution.py:547
  (15 shorter events, 0.2 us)
Async XLA Ops:
  1.8 2.1 %collective-permute-start = (bf16[2,8,16,512]{3,2,1,0:T(8,128)(2,1)S(1)}, bf16[2,8,16,512]{3,2,1,0:T(8,128)(2,1)S(1)}, u32[]{:S(2)}, u32[]{:S(2)}) collective-permute-start(bf16[2,8,16,512]{3,2,1,0:T(8,128)(2,1)S(1)} %get-tuple-element.45), channel_id=1, source_target_pairs={{0,8},{8,0},{16,24},{24,16},{1,9},{9,1},{17,25},{25,17},{2,10},{10... | collective-permute-start | bytes 786440 | tf_op jit(solution)/shard_map/ppermute | solution.py:446
  4.0 8.7 %collective-permute-start.1 = (bf16[272,2048]{1,0:T(8,128)(2,1)S(1)}, bf16[272,2048]{1,0:T(8,128)(2,1)S(1)}, u32[]{:S(2)}, u32[]{:S(2)}) collective-permute-start(bf16[272,2048]{1,0:T(8,128)(2,1)S(1)} %get-tuple-element.47), channel_id=1, source_target_pairs={{0,8},{8,0},{16,24},{24,16},{1,9},{9,1},{17,25},{25,17},{2,10},{10... | collective-permute-start | bytes 3342344 | tf_op jit(solution)/shard_map/ppermute | solution.py:447
  4.1 8.6 %collective-permute-start.2 = (bf16[2,64,512]{2,1,0:T(8,128)(2,1)S(1)}, bf16[2,64,512]{2,1,0:T(8,128)(2,1)S(1)}, u32[]{:S(2)}, u32[]{:S(2)}) collective-permute-start(bf16[2,64,512]{2,1,0:T(8,128)(2,1)S(1)} %get-tuple-element.49), channel_id=1, source_target_pairs={{0,2},{1,3},{2,0},{3,1},{4,6},{5,7},{6,4},{7,5},{8,10},{9,11},{10,... | collective-permute-start | bytes 393224 | tf_op jit(solution)/shard_map/ppermute | solution.py:424
  7.1 12.9 %collective-permute-start.4 = (bf16[2,64,512]{2,1,0:T(8,128)(2,1)S(1)}, bf16[2,64,512]{2,1,0:T(8,128)(2,1)S(1)}, u32[]{:S(2)}, u32[]{:S(2)}) collective-permute-start(bf16[2,64,512]{2,1,0:T(8,128)(2,1)S(1)} %get-tuple-element.52), channel_id=1, source_target_pairs={{0,4},{1,5},{2,6},{3,7},{4,0},{5,1},{6,2},{7,3},{8,12},{9,13},{10,... | collective-permute-start | bytes 393224 | tf_op jit(solution)/shard_map/ppermute | solution.py:424
  9.7 10.3 %collective-permute-start.5 = (bf16[2,64,512]{2,1,0:T(8,128)(2,1)S(1)}, bf16[2,64,512]{2,1,0:T(8,128)(2,1)S(1)}, u32[]{:S(2)}, u32[]{:S(2)}) collective-permute-start(bf16[2,64,512]{2,1,0:T(8,128)(2,1)S(1)} %get-tuple-element.53), channel_id=1, source_target_pairs={{0,6},{1,7},{2,4},{3,5},{4,2},{5,3},{6,0},{7,1},{8,14},{9,15},{10,... | collective-permute-start | bytes 393224 | tf_op jit(solution)/shard_map/ppermute | solution.py:424
  12.7 7.3 %collective-permute-start.6 = (bf16[128,512]{1,0:T(8,128)(2,1)S(1)}, bf16[128,512]{1,0:T(8,128)(2,1)S(1)}, u32[]{:S(2)}, u32[]{:S(2)}) collective-permute-start(bf16[128,512]{1,0:T(8,128)(2,1)S(1)} %get-tuple-element.50.rest_0_), channel_id=1, source_target_pairs={{0,16},{8,24},{16,0},{24,8},{1,17},{9,25},{17,1},{25,9},{2,18},{10... | collective-permute-start | bytes 393224 | tf_op jit(solution)/shard_map/ppermute | solution.py:430
  14.5 5.9 %collective-permute-start.7 = (bf16[128,512]{1,0:T(8,128)(2,1)S(1)}, bf16[128,512]{1,0:T(8,128)(2,1)S(1)}, u32[]{:S(2)}, u32[]{:S(2)}) collective-permute-start(bf16[128,512]{1,0:T(8,128)(2,1)S(1)} %get-tuple-element.51), channel_id=1, source_target_pairs={{0,17},{1,16},{2,19},{3,18},{4,21},{5,20},{6,23},{7,22},{8,25},{9,... | collective-permute-start | bytes 393224 | tf_op jit(solution)/shard_map/ppermute | solution.py:433
  15.9 8.0 %collective-permute-start.3 = (bf16[128,512]{1,0:T(8,128)(2,1)S(1)}, bf16[128,512]{1,0:T(8,128)(2,1)S(1)}, u32[]{:S(2)}, u32[]{:S(2)}) collective-permute-start(bf16[128,512]{1,0:T(8,128)(2,1)S(1)} %get-tuple-element.51), channel_id=1, source_target_pairs={{0,1},{1,0},{2,3},{3,2},{4,5},{5,4},{6,7},{7,6},{8,9},{9,8},{10,11... | collective-permute-start | bytes 393224 | tf_op jit(solution)/shard_map/ppermute | solution.py:427
  20.4 5.5 %collective-permute-start.8 = (bf16[128,512]{1,0:T(8,128)(2,1)S(1)}, bf16[128,512]{1,0:T(8,128)(2,1)S(1)}, u32[]{:S(2)}, u32[]{:S(2)}) collective-permute-start(bf16[128,512]{1,0:T(8,128)(2,1)S(1)} %get-tuple-element.55), channel_id=1, source_target_pairs={{0,1},{1,0},{2,3},{3,2},{4,5},{5,4},{6,7},{7,6},{8,9},{9,8},{10,11... | collective-permute-start | bytes 393224 | tf_op jit(solution)/shard_map/ppermute | solution.py:427
  22.0 6.0 %collective-permute-start.9 = (bf16[128,512]{1,0:T(8,128)(2,1)S(1)}, bf16[128,512]{1,0:T(8,128)(2,1)S(1)}, u32[]{:S(2)}, u32[]{:S(2)}) collective-permute-start(bf16[128,512]{1,0:T(8,128)(2,1)S(1)} %get-tuple-element.54.rest_2_), channel_id=1, source_target_pairs={{0,16},{8,24},{16,0},{24,8},{1,17},{9,25},{17,1},{25,9},{2,18},{10... | collective-permute-start | bytes 393224 | tf_op jit(solution)/shard_map/ppermute | solution.py:430
  23.1 5.9 %collective-permute-start.10 = (bf16[128,512]{1,0:T(8,128)(2,1)S(1)}, bf16[128,512]{1,0:T(8,128)(2,1)S(1)}, u32[]{:S(2)}, u32[]{:S(2)}) collective-permute-start(bf16[128,512]{1,0:T(8,128)(2,1)S(1)} %get-tuple-element.55), channel_id=1, source_target_pairs={{0,17},{1,16},{2,19},{3,18},{4,21},{5,20},{6,23},{7,22},{8,25},{9,... | collective-permute-start | bytes 393224 | tf_op jit(solution)/shard_map/ppermute | solution.py:433
  32.9 6.5 %collective-permute-start.13 = (bf16[128,512]{1,0:T(8,128)(2,1)S(1)}, bf16[128,512]{1,0:T(8,128)(2,1)S(1)}, u32[]{:S(2)}, u32[]{:S(2)}) collective-permute-start(bf16[128,512]{1,0:T(8,128)(2,1)S(1)} %shard_map.93), channel_id=1, source_target_pairs={{0,1},{1,0},{2,3},{3,2},{4,5},{5,4},{6,7},{7,6},{8,9},{9,8},{10,11... | collective-permute-start | bytes 393224 | tf_op jit(solution)/shard_map/ppermute | solution.py:427
  33.0 7.1 %collective-permute-start.11 = (bf16[128,512]{1,0:T(8,128)(2,1)S(1)}, bf16[128,512]{1,0:T(8,128)(2,1)S(1)}, u32[]{:S(2)}, u32[]{:S(2)}) collective-permute-start(bf16[128,512]{1,0:T(8,128)(2,1)S(1)} %get-tuple-element.63), channel_id=1, source_target_pairs={{0,16},{8,24},{16,0},{24,8},{1,17},{9,25},{17,1},{25,9},{2,18},{10... | collective-permute-start | bytes 393224 | tf_op jit(solution)/shard_map/ppermute | solution.py:430
  34.3 7.0 %collective-permute-start.12 = (bf16[128,512]{1,0:T(8,128)(2,1)S(1)}, bf16[128,512]{1,0:T(8,128)(2,1)S(1)}, u32[]{:S(2)}, u32[]{:S(2)}) collective-permute-start(bf16[128,512]{1,0:T(8,128)(2,1)S(1)} %get-tuple-element.64), channel_id=1, source_target_pairs={{0,17},{1,16},{2,19},{3,18},{4,21},{5,20},{6,23},{7,22},{8,25},{9,... | collective-permute-start | bytes 393224 | tf_op jit(solution)/shard_map/ppermute | solution.py:433
  36.5 10.7 %collective-permute-start.16 = (bf16[128,512]{1,0:T(8,128)(2,1)S(1)}, bf16[128,512]{1,0:T(8,128)(2,1)S(1)}, u32[]{:S(2)}, u32[]{:S(2)}) collective-permute-start(bf16[128,512]{1,0:T(8,128)(2,1)S(1)} %shard_map.95), channel_id=1, source_target_pairs={{0,1},{1,0},{2,3},{3,2},{4,5},{5,4},{6,7},{7,6},{8,9},{9,8},{10,11... | collective-permute-start | bytes 393224 | tf_op jit(solution)/shard_map/ppermute | solution.py:427
  36.6 10.7 %collective-permute-start.14 = (bf16[128,512]{1,0:T(8,128)(2,1)S(1)}, bf16[128,512]{1,0:T(8,128)(2,1)S(1)}, u32[]{:S(2)}, u32[]{:S(2)}) collective-permute-start(bf16[128,512]{1,0:T(8,128)(2,1)S(1)} %get-tuple-element.67), channel_id=1, source_target_pairs={{0,16},{8,24},{16,0},{24,8},{1,17},{9,25},{17,1},{25,9},{2,18},{10... | collective-permute-start | bytes 393224 | tf_op jit(solution)/shard_map/ppermute | solution.py:430
  39.4 7.8 %collective-permute-start.15 = (bf16[128,512]{1,0:T(8,128)(2,1)S(1)}, bf16[128,512]{1,0:T(8,128)(2,1)S(1)}, u32[]{:S(2)}, u32[]{:S(2)}) collective-permute-start(bf16[128,512]{1,0:T(8,128)(2,1)S(1)} %get-tuple-element.68), channel_id=1, source_target_pairs={{0,17},{1,16},{2,19},{3,18},{4,21},{5,20},{6,23},{7,22},{8,25},{9,... | collective-permute-start | bytes 393224 | tf_op jit(solution)/shard_map/ppermute | solution.py:433
  41.4 8.6 %collective-permute-start.20 = (bf16[2,64,512]{2,1,0:T(8,128)(2,1)S(1)}, bf16[2,64,512]{2,1,0:T(8,128)(2,1)S(1)}, u32[]{:S(2)}, u32[]{:S(2)}) collective-permute-start(bf16[2,64,512]{2,1,0:T(8,128)(2,1)S(1)} %get-tuple-element.66.refs_0_), channel_id=1, source_target_pairs={{0,4},{1,5},{2,6},{3,7},{4,0},{5,1},{6,2},{7,3},{8,12},{9,13},{10,... | collective-permute-start | bytes 393224 | tf_op jit(solution)/shard_map/ppermute | solution.py:424
  45.9 6.9 %collective-permute-start.21 = (bf16[2,64,512]{2,1,0:T(8,128)(2,1)S(1)}, bf16[2,64,512]{2,1,0:T(8,128)(2,1)S(1)}, u32[]{:S(2)}, u32[]{:S(2)}) collective-permute-start(bf16[2,64,512]{2,1,0:T(8,128)(2,1)S(1)} %get-tuple-element.75), channel_id=1, source_target_pairs={{0,6},{1,7},{2,4},{3,5},{4,2},{5,3},{6,0},{7,1},{8,14},{9,15},{10,... | collective-permute-start | bytes 393224 | tf_op jit(solution)/shard_map/ppermute | solution.py:424
  47.3 6.4 %collective-permute-start.19 = (bf16[2,64,512]{2,1,0:T(8,128)(2,1)S(1)}, bf16[2,64,512]{2,1,0:T(8,128)(2,1)S(1)}, u32[]{:S(2)}, u32[]{:S(2)}) collective-permute-start(bf16[2,64,512]{2,1,0:T(8,128)(2,1)S(1)} %get-tuple-element.74), channel_id=1, source_target_pairs={{0,2},{1,3},{2,0},{3,1},{4,6},{5,7},{6,4},{7,5},{8,10},{9,11},{10,... | collective-permute-start | bytes 393224 | tf_op jit(solution)/shard_map/ppermute | solution.py:424
  49.4 4.5 %collective-permute-start.17 = (bf16[64,2048]{1,0:T(8,128)(2,1)S(1)}, bf16[64,2048]{1,0:T(8,128)(2,1)S(1)}, u32[]{:S(2)}, u32[]{:S(2)}) collective-permute-start(bf16[64,2048]{1,0:T(8,128)(2,1)S(1)} %get-tuple-element.71), channel_id=1, source_target_pairs={{0,8},{8,0},{16,24},{24,16},{1,9},{9,1},{17,25},{25,17},{2,10},{10... | collective-permute-start | bytes 786440 | tf_op jit(solution)/shard_map/ppermute | solution.py:479
  49.5 4.4 %collective-permute-start.18 = (bf16[64,2048]{1,0:T(8,128)(2,1)S(1)}, bf16[64,2048]{1,0:T(8,128)(2,1)S(1)}, u32[]{:S(2)}, u32[]{:S(2)}) collective-permute-start(bf16[64,2048]{1,0:T(8,128)(2,1)S(1)} %get-tuple-element.72), channel_id=1, source_target_pairs={{0,8},{8,0},{16,24},{24,16},{1,9},{9,1},{17,25},{25,17},{2,10},{10... | collective-permute-start | bytes 786440 | tf_op jit(solution)/shard_map/ppermute | solution.py:479
  53.8 1.6 %collective-permute-start.22 = (bf16[2,8,16,512]{3,2,1,0:T(8,128)(2,1)S(1)}, bf16[2,8,16,512]{3,2,1,0:T(8,128)(2,1)S(1)}, u32[]{:S(2)}, u32[]{:S(2)}) collective-permute-start(bf16[2,8,16,512]{3,2,1,0:T(8,128)(2,1)S(1)} %get-tuple-element.79), channel_id=1, source_target_pairs={{0,8},{8,0},{16,24},{24,16},{1,9},{9,1},{17,25},{25,17},{2,10},{10... | collective-permute-start | bytes 786440 | tf_op jit(solution)/shard_map/ppermute | solution.py:552

commit v5 on v4

--- a/solution.py
+++ b/solution.py
@@ -465,7 +465,11 @@
         for z in (2, 0):
             here, beside = far_grads[z : z + 2]
             (own_part,) = hand_on(own_beside[z // 2], far_ds)
-            back_y, back_xy, back_x = along_y(here), along_xy(beside), along_x(own_part)
+            back_x = along_x(own_part)
+            if not z:
+                (here,), (beside,) = hand_on(here, before), hand_on(beside, before)
+            before = back_x
+            back_y, back_xy = along_y(here), along_xy(beside)
             totals = in_vmem(functools.partial(add_kernel, z), [(pair, BF16)] * 2)(
                 own_here, back_y, back_xy, back_x
             )

time: 56.1 us -> 56.2 us (level)
  starting transfers between devices: 26 us -> 30.9 us
  waiting for transfers between devices: 17.1 us -> 14 us
  Pallas kernels: 12.3 us -> 10.2 us
    pallas_call x13 -> x15, Pallas kernels: 7.75 us -> 5.59 us  [call(): return local_call(body, [IN_VMEM] * len(args), spec, **more)(*args)]
    ppermute x4, starting transfers between devices: 2.02 us -> 3.79 us  [along_x(): return lax.ppermute(part, 'enc', swap_x)]
    ppermute x4, starting transfers between devices: 5.16 us -> 6.67 us  [along_xy(): return lax.ppermute(part, ('ctx', 'enc'), swap_xy)]
    ppermute x4, waiting for transfers between devices: 2.5 us -> 1.35 us  [along_xy(): return lax.ppermute(part, ('ctx', 'enc'), swap_xy)]
    ppermute x4, waiting for transfers between devices: 3.59 us -> 2.55 us  [along_x(): return lax.ppermute(part, 'enc', swap_x)]
    ppermute x6, starting transfers between devices: 12.1 us -> 13 us  [along_z(): lax.ppermute(part, 'enc', [(i, i ^ 2 * dz) for i in range(n_enc)])]
    ppermute x6, waiting for transfers between devices: 10.5 us -> 9.63 us  [along_z(): lax.ppermute(part, 'enc', [(i, i ^ 2 * dz) for i in range(n_enc)])]
    ppermute x4, starting transfers between devices: 5.48 us -> 6.21 us  [along_y(): return lax.ppermute(part, 'ctx', swap_y)]
  transfers between devices with their start and end apart: 23 -> 23, of which waited for: 10 -> 9; matrix products, arithmetic and copies ran while one was open for 0% -> 0% of each run, Pallas kernels for 11% -> 14%
where the time goes in v5:
time: 56.2 us; the launch traced here: 56.1 us
  starting transfers between devices  30.9 us (55%)
  waiting for transfers between devices  14 us (25%)
  Pallas kernels  10.2 us (18%)
  between operations  0.97 us (2%)
    ppermute x6, starting transfers between devices, along_z(): lax.ppermute(part, 'enc', [(i, i ^ 2 * dz) for i in range(n_enc)])  13 us
    ppermute x6, waiting for transfers between devices, along_z(): lax.ppermute(part, 'enc', [(i, i ^ 2 * dz) for i in range(n_enc)])  9.63 us
    ppermute x4, starting transfers between devices, along_xy(): return lax.ppermute(part, ('ctx', 'enc'), swap_xy)  6.67 us
    ppermute x4, starting transfers between devices, along_y(): return lax.ppermute(part, 'ctx', swap_y)  6.21 us
    pallas_call x15, Pallas kernels, call(): return local_call(body, [IN_VMEM] * len(args), spec, **more)(*args)  5.59 us
    ppermute x4, starting transfers between devices, along_x(): return lax.ppermute(part, 'enc', swap_x)  3.79 us
    ppermute x4, waiting for transfers between devices, along_x(): return lax.ppermute(part, 'enc', swap_x)  2.55 us
    pallas_call x1, Pallas kernels, split_the_text(): local_call(functools.partial(split_text, n_blocks, pieces, where), [IN_HB...  1.6 us
  transfers between devices with their start and end apart: 23, of which 9 were waited for; matrix products, arithmetic and copies ran while one was open for 0% of the time, Pallas kernels for 14%

profile of v5, /device:TPU:0, one launch (start us, length us, event | category | flops | bytes accessed | tf_op | source)
XLA Modules:
  0.0 56.1 jit_solution(18442441110072541979)
XLA Ops:
  0.6 1.1 %shard_map.86 = (bf16[2,8,16,512]{3,2,1,0:T(8,128)(2,1)S(1)}, bf16[2,8,16,512]{3,2,1,0:T(8,128)(2,1)S(1)}) custom-call(bf16[8,16,1024]{2,1,0:T(8,128)(2,1)} %k_ref.1, bf16[8,16,1024]{2,1,0:T(8,128)(2,1)} %v_ref.1), custom_call_target="tpu_custom_call" | custom-call | bytes 524288 | tf_op jit(solution)/shard_map/pallas_call | solution.py:435
  1.8 0.5 collective-permute-start
  2.3 1.6 %shard_map.85 = (bf16[272,2048]{1,0:T(8,128)(2,1)S(1)}, bf16[144,2048]{1,0:T(8,128)(2,1)S(1)}, bf16[128,2048]{1,0:T(8,128)(2,1)S(1)}, bf16[2,256,128]{2,1,0:T(8,128)(2,1)S(1)}) custom-call(bf16[1,128,4096]{2,1,0:T(8,128)(2,1)} %q_ref.1, bf16[1,128,4096]{2,1,0:T(8,128)(2,1)} %g_ref.1, s32[1,128]{1,0:T(1,128)} %samp_hbm.1, s32[1,2]{1,0:T(1,128)} %tiles_hbm.1), custom_call_target="tpu_custom_call" | custom-call | bytes 4194304 | tf_op jit(solution)/shard_map/pallas_call | solution.py:396
  3.9 0.0 collective-permute-done.got
  3.9 0.1 shard_map.87
  4.0 0.1 collective-permute-start.1
  4.1 3.0 %collective-permute-start.2 = (bf16[2,64,512]{2,1,0:T(8,128)(2,1)S(1)}, bf16[2,64,512]{2,1,0:T(8,128)(2,1)S(1)}, u32[]{:S(2)}, u32[]{:S(2)}) collective-permute-start(bf16[2,64,512]{2,1,0:T(8,128)(2,1)S(1)} %get-tuple-element.49), channel_id=1, source_target_pairs={{0,2},{1,3},{2,0},{3,1},{4,6},{5,7},{6,4},{7,5},{8,10},{9,11},{10,... | collective-permute-start | bytes 393224 | tf_op jit(solution)/shard_map/ppermute | solution.py:424
  7.1 2.6 %collective-permute-start.4 = (bf16[2,64,512]{2,1,0:T(8,128)(2,1)S(1)}, bf16[2,64,512]{2,1,0:T(8,128)(2,1)S(1)}, u32[]{:S(2)}, u32[]{:S(2)}) collective-permute-start(bf16[2,64,512]{2,1,0:T(8,128)(2,1)S(1)} %get-tuple-element.52), channel_id=1, source_target_pairs={{0,4},{1,5},{2,6},{3,7},{4,0},{5,1},{6,2},{7,3},{8,12},{9,13},{10,... | collective-permute-start | bytes 393224 | tf_op jit(solution)/shard_map/ppermute | solution.py:424
  9.7 3.0 %collective-permute-done.2.refs_1_ = bf16[2,64,512]{2,1,0:T(8,128)(2,1)S(1)} collective-permute-done((bf16[2,64,512]{2,1,0:T(8,128)(2,1)S(1)}, bf16[2,64,512]{2,1,0:T(8,128)(2,1)S(1)}, u32[]{:S(2)}, u32[]{:S(2)}) %collective-permute-start.2) | collective-permute-done | bytes 131104 | tf_op jit(solution)/shard_map/ppermute | solution.py:424
  12.7 0.0 collective-permute-done.1.refs_2_.got
  12.7 1.8 %collective-permute-start.6 = (bf16[128,512]{1,0:T(8,128)(2,1)S(1)}, bf16[128,512]{1,0:T(8,128)(2,1)S(1)}, u32[]{:S(2)}, u32[]{:S(2)}) collective-permute-start(bf16[128,512]{1,0:T(8,128)(2,1)S(1)} %get-tuple-element.50.rest_0_), channel_id=1, source_target_pairs={{0,16},{8,24},{16,0},{24,8},{1,17},{9,25},{17,1},{25,9},{2,18},{10... | collective-permute-start | bytes 393224 | tf_op jit(solution)/shard_map/ppermute | solution.py:430
  14.5 1.4 %collective-permute-start.7 = (bf16[128,512]{1,0:T(8,128)(2,1)S(1)}, bf16[128,512]{1,0:T(8,128)(2,1)S(1)}, u32[]{:S(2)}, u32[]{:S(2)}) collective-permute-start(bf16[128,512]{1,0:T(8,128)(2,1)S(1)} %get-tuple-element.51), channel_id=1, source_target_pairs={{0,17},{1,16},{2,19},{3,18},{4,21},{5,20},{6,23},{7,22},{8,25},{9,... | collective-permute-start | bytes 393224 | tf_op jit(solution)/shard_map/ppermute | solution.py:433
  15.9 0.3 collective-permute-start.3
  16.3 3.8 %collective-permute-done.4.refs_0_ = bf16[2,64,512]{2,1,0:T(8,128)(2,1)S(1)} collective-permute-done((bf16[2,64,512]{2,1,0:T(8,128)(2,1)S(1)}, bf16[2,64,512]{2,1,0:T(8,128)(2,1)S(1)}, u32[]{:S(2)}, u32[]{:S(2)}) %collective-permute-start.4) | collective-permute-done | bytes 131104 | tf_op jit(solution)/shard_map/ppermute | solution.py:424
  20.0 0.0 collective-permute-done.5.refs_1_
  20.0 0.0 collective-permute-done.6.refs_3_.rest_0_.rest_4_
  20.0 0.3 collective-permute-done.7.refs_4_.rest_1_.rest_5_
  20.4 1.6 %collective-permute-start.8 = (bf16[128,512]{1,0:T(8,128)(2,1)S(1)}, bf16[128,512]{1,0:T(8,128)(2,1)S(1)}, u32[]{:S(2)}, u32[]{:S(2)}) collective-permute-start(bf16[128,512]{1,0:T(8,128)(2,1)S(1)} %get-tuple-element.55), channel_id=1, source_target_pairs={{0,1},{1,0},{2,3},{3,2},{4,5},{5,4},{6,7},{7,6},{8,9},{9,8},{10,11... | collective-permute-start | bytes 393224 | tf_op jit(solution)/shard_map/ppermute | solution.py:427
  22.0 1.2 %collective-permute-start.9 = (bf16[128,512]{1,0:T(8,128)(2,1)S(1)}, bf16[128,512]{1,0:T(8,128)(2,1)S(1)}, u32[]{:S(2)}, u32[]{:S(2)}) collective-permute-start(bf16[128,512]{1,0:T(8,128)(2,1)S(1)} %get-tuple-element.54.rest_2_), channel_id=1, source_target_pairs={{0,16},{8,24},{16,0},{24,8},{1,17},{9,25},{17,1},{25,9},{2,18},{10... | collective-permute-start | bytes 393224 | tf_op jit(solution)/shard_map/ppermute | solution.py:430
  23.1 0.8 %collective-permute-start.10 = (bf16[128,512]{1,0:T(8,128)(2,1)S(1)}, bf16[128,512]{1,0:T(8,128)(2,1)S(1)}, u32[]{:S(2)}, u32[]{:S(2)}) collective-permute-start(bf16[128,512]{1,0:T(8,128)(2,1)S(1)} %get-tuple-element.55), channel_id=1, source_target_pairs={{0,17},{1,16},{2,19},{3,18},{4,21},{5,20},{6,23},{7,22},{8,25},{9,... | collective-permute-start | bytes 393224 | tf_op jit(solution)/shard_map/ppermute | solution.py:433
  24.0 0.0 collective-permute-done.3.rest_1_
  24.0 1.9 %collective-permute-done.8.rest_3_ = bf16[128,512]{1,0:T(8,128)(2,1)S(1)} collective-permute-done((bf16[128,512]{1,0:T(8,128)(2,1)S(1)}, bf16[128,512]{1,0:T(8,128)(2,1)S(1)}, u32[]{:S(2)}, u32[]{:S(2)}) %collective-permute-start.8) | collective-permute-done | bytes 131104 | tf_op jit(solution)/shard_map/ppermute | solution.py:427
  25.9 3.8 %shard_map.90 = (bf16[4,256,1024]{2,1,0:T(8,128)(2,1)S(1)}, f32[256,512]{1,0:T(8,128)S(1)}, bf16[128,512]{1,0:T(8,128)(2,1)S(1)}, bf16[128,512]{1,0:T(8,128)(2,1)S(1)}) custom-call(bf16[2,256,128]{2,1,0:T(8,128)(2,1)S(1)} %get-tuple-element.56.bias, bf16[144,2048]{1,0:T(8,128)(2,1)S(1)} %get-tuple-element.43.q_a, ...), custom_call_target="tpu_custom_call" | custom-call | flops 1073741824 | bytes 16777216 | tf_op jit(solution)/shard_map/pallas_call | solution.py:55
  29.6 0.0 collective-permute-done.9.rest_2_.rest_6_
  29.7 0.4 shard_map.91
  30.1 1.1 %collective-permute-start.13 = (bf16[128,512]{1,0:T(8,128)(2,1)S(1)}, bf16[128,512]{1,0:T(8,128)(2,1)S(1)}, u32[]{:S(2)}, u32[]{:S(2)}) collective-permute-start(bf16[128,512]{1,0:T(8,128)(2,1)S(1)} %shard_map.93), channel_id=1, source_target_pairs={{0,1},{1,0},{2,3},{3,2},{4,5},{5,4},{6,7},{7,6},{8,9},{9,8},{10,11... | collective-permute-start | bytes 393224 | tf_op jit(solution)/shard_map/ppermute | solution.py:427
  31.2 3.2 %collective-permute-start.11 = (bf16[128,512]{1,0:T(8,128)(2,1)S(1)}, bf16[128,512]{1,0:T(8,128)(2,1)S(1)}, u32[]{:S(2)}, u32[]{:S(2)}) collective-permute-start(bf16[128,512]{1,0:T(8,128)(2,1)S(1)} %get-tuple-element.63), channel_id=1, source_target_pairs={{0,16},{8,24},{16,0},{24,8},{1,17},{9,25},{17,1},{25,9},{2,18},{10... | collective-permute-start | bytes 393224 | tf_op jit(solution)/shard_map/ppermute | solution.py:430
  34.4 0.6 %collective-permute-start.12 = (bf16[128,512]{1,0:T(8,128)(2,1)S(1)}, bf16[128,512]{1,0:T(8,128)(2,1)S(1)}, u32[]{:S(2)}, u32[]{:S(2)}) collective-permute-start(bf16[128,512]{1,0:T(8,128)(2,1)S(1)} %get-tuple-element.64), channel_id=1, source_target_pairs={{0,17},{1,16},{2,19},{3,18},{4,21},{5,20},{6,23},{7,22},{8,25},{9,... | collective-permute-start | bytes 393224 | tf_op jit(solution)/shard_map/ppermute | solution.py:433
  35.0 0.8 %collective-permute-start.16 = (bf16[128,512]{1,0:T(8,128)(2,1)S(1)}, bf16[128,512]{1,0:T(8,128)(2,1)S(1)}, u32[]{:S(2)}, u32[]{:S(2)}) collective-permute-start(bf16[128,512]{1,0:T(8,128)(2,1)S(1)} %shard_map.97), channel_id=1, source_target_pairs={{0,1},{1,0},{2,3},{3,2},{4,5},{5,4},{6,7},{7,6},{8,9},{9,8},{10,11... | collective-permute-start | bytes 393224 | tf_op jit(solution)/shard_map/ppermute | solution.py:427
  35.8 0.6 %collective-permute-done.13.back_x.refs_1_ = bf16[128,512]{1,0:T(8,128)(2,1)S(1)} collective-permute-done((bf16[128,512]{1,0:T(8,128)(2,1)S(1)}, bf16[128,512]{1,0:T(8,128)(2,1)S(1)}, u32[]{:S(2)}, u32[]{:S(2)}) %collective-permute-start.13) | collective-permute-done | bytes 131104 | tf_op jit(solution)/shard_map/ppermute | solution.py:427
  36.5 3.8 %collective-permute-start.15 = (bf16[128,512]{1,0:T(8,128)(2,1)S(1)}, bf16[128,512]{1,0:T(8,128)(2,1)S(1)}, u32[]{:S(2)}, u32[]{:S(2)}) collective-permute-start(bf16[128,512]{1,0:T(8,128)(2,1)S(1)} %shard_map.96), channel_id=1, source_target_pairs={{0,17},{1,16},{2,19},{3,18},{4,21},{5,20},{6,23},{7,22},{8,25},{9,... | collective-permute-start | bytes 393224 | tf_op jit(solution)/shard_map/ppermute | solution.py:433
  40.2 1.0 %collective-permute-done.12.back_xy = bf16[128,512]{1,0:T(8,128)(2,1)S(1)} collective-permute-done((bf16[128,512]{1,0:T(8,128)(2,1)S(1)}, bf16[128,512]{1,0:T(8,128)(2,1)S(1)}, u32[]{:S(2)}, u32[]{:S(2)}) %collective-permute-start.12) | collective-permute-done | bytes 131104 | tf_op jit(solution)/shard_map/ppermute | solution.py:433
  41.3 0.1 shard_map.94
  41.3 4.6 %collective-permute-start.20 = (bf16[2,64,512]{2,1,0:T(8,128)(2,1)S(1)}, bf16[2,64,512]{2,1,0:T(8,128)(2,1)S(1)}, u32[]{:S(2)}, u32[]{:S(2)}) collective-permute-start(bf16[2,64,512]{2,1,0:T(8,128)(2,1)S(1)} %get-tuple-element.66.refs_0_), channel_id=1, source_target_pairs={{0,4},{1,5},{2,6},{3,7},{4,0},{5,1},{6,2},{7,3},{8,12},{9,13},{10,... | collective-permute-start | bytes 393224 | tf_op jit(solution)/shard_map/ppermute | solution.py:424
  45.9 1.1 %collective-permute-start.21 = (bf16[2,64,512]{2,1,0:T(8,128)(2,1)S(1)}, bf16[2,64,512]{2,1,0:T(8,128)(2,1)S(1)}, u32[]{:S(2)}, u32[]{:S(2)}) collective-permute-start(bf16[2,64,512]{2,1,0:T(8,128)(2,1)S(1)} %get-tuple-element.75), channel_id=1, source_target_pairs={{0,6},{1,7},{2,4},{3,5},{4,2},{5,3},{6,0},{7,1},{8,14},{9,15},{10,... | collective-permute-start | bytes 393224 | tf_op jit(solution)/shard_map/ppermute | solution.py:424
  47.0 0.0 collective-permute-done.16.back_x
  47.0 0.0 collective-permute-done.15.back_xy
  47.0 0.1 shard_map.98
  47.0 1.7 %collective-permute-start.19 = (bf16[2,64,512]{2,1,0:T(8,128)(2,1)S(1)}, bf16[2,64,512]{2,1,0:T(8,128)(2,1)S(1)}, u32[]{:S(2)}, u32[]{:S(2)}) collective-permute-start(bf16[2,64,512]{2,1,0:T(8,128)(2,1)S(1)} %get-tuple-element.74), channel_id=1, source_target_pairs={{0,2},{1,3},{2,0},{3,1},{4,6},{5,7},{6,4},{7,5},{8,10},{9,11},{10,... | collective-permute-start | bytes 393224 | tf_op jit(solution)/shard_map/ppermute | solution.py:424
  48.8 1.2 %shard_map.92 = (bf16[128,2048]{1,0:T(8,128)(2,1)S(1)}, bf16[128,2048]{1,0:T(8,128)(2,1)S(1)}) custom-call(bf16[144,2048]{1,0:T(8,128)(2,1)S(1)} %get-tuple-element.43.q_a, bf16[272,2048]{1,0:T(8,128)(2,1)S(1)} %collective-permute-done.1.refs_2_.got, bf16[128,512]{1,0:T(8,128)(2,1)S(1)} %get-tuple-element.50.rest_0_, ...), custom_call_target="tpu_custom_call" | custom-call | flops 536870912 | bytes 8388608 | tf_op jit(solution)/shard_map/pallas_call | solution.py:55
  50.0 0.1 collective-permute-start.17
  50.1 0.5 collective-permute-start.18
  50.6 2.3 %collective-permute-done.21.refs_1_ = bf16[2,64,512]{2,1,0:T(8,128)(2,1)S(1)} collective-permute-done((bf16[2,64,512]{2,1,0:T(8,128)(2,1)S(1)}, bf16[2,64,512]{2,1,0:T(8,128)(2,1)S(1)}, u32[]{:S(2)}, u32[]{:S(2)}) %collective-permute-start.21) | collective-permute-done | bytes 131104 | tf_op jit(solution)/shard_map/ppermute | solution.py:424
  52.8 0.6 %collective-permute-done.19.refs_1_ = bf16[2,64,512]{2,1,0:T(8,128)(2,1)S(1)} collective-permute-done((bf16[2,64,512]{2,1,0:T(8,128)(2,1)S(1)}, bf16[2,64,512]{2,1,0:T(8,128)(2,1)S(1)}, u32[]{:S(2)}, u32[]{:S(2)}) %collective-permute-start.19) | collective-permute-done | bytes 131104 | tf_op jit(solution)/shard_map/ppermute | solution.py:424
  53.5 0.1 collective-permute-start.22
  53.6 1.0 %shard_map.100 = (bf16[1,128,4096]{2,1,0:T(8,128)(2,1)}, f32[8,128]{1,0:T(8,128)S(1)}) custom-call(bf16[128,2048]{1,0:T(8,128)(2,1)S(1)} %get-tuple-element.61.mine, bf16[64,2048]{1,0:T(8,128)(2,1)S(1)} %collective-permute-done.17.refs_0_, bf16[64,2048]{1,0:T(8,128)(2,1)S(1)} %collective-permute-done.18.refs_1_), custom_call_target="tpu_custom_call" | custom-call | bytes 524288 | tf_op jit(solution)/shard_map/pallas_call | solution.py:536
  54.6 0.5 collective-permute-done.22.got
  55.1 0.8 %shard_map.103 = (bf16[8,16,1024]{2,1,0:T(8,128)(2,1)}, bf16[8,16,1024]{2,1,0:T(8,128)(2,1)}) custom-call(bf16[2,8,16,512]{3,2,1,0:T(8,128)(2,1)S(1)} %get-tuple-element.78.mine, bf16[2,8,16,512]{3,2,1,0:T(8,128)(2,1)S(1)} %collective-permute-done.22.got, f32[8,128]{1,0:T(8,128)S(1)} %get-tuple-element.80._), custom_call_target="tpu_custom_call" | custom-call | bytes 524288 | tf_op jit(solution)/shard_map/pallas_call | solution.py:551
  (17 shorter events, 0.2 us)
Async XLA Ops:
  1.8 2.1 %collective-permute-start = (bf16[2,8,16,512]{3,2,1,0:T(8,128)(2,1)S(1)}, bf16[2,8,16,512]{3,2,1,0:T(8,128)(2,1)S(1)}, u32[]{:S(2)}, u32[]{:S(2)}) collective-permute-start(bf16[2,8,16,512]{3,2,1,0:T(8,128)(2,1)S(1)} %get-tuple-element.45), channel_id=1, source_target_pairs={{0,8},{8,0},{16,24},{24,16},{1,9},{9,1},{17,25},{25,17},{2,10},{10... | collective-permute-start | bytes 786440 | tf_op jit(solution)/shard_map/ppermute | solution.py:446
  4.0 8.7 %collective-permute-start.1 = (bf16[272,2048]{1,0:T(8,128)(2,1)S(1)}, bf16[272,2048]{1,0:T(8,128)(2,1)S(1)}, u32[]{:S(2)}, u32[]{:S(2)}) collective-permute-start(bf16[272,2048]{1,0:T(8,128)(2,1)S(1)} %get-tuple-element.47), channel_id=1, source_target_pairs={{0,8},{8,0},{16,24},{24,16},{1,9},{9,1},{17,25},{25,17},{2,10},{10... | collective-permute-start | bytes 3342344 | tf_op jit(solution)/shard_map/ppermute | solution.py:447
  4.1 8.6 %collective-permute-start.2 = (bf16[2,64,512]{2,1,0:T(8,128)(2,1)S(1)}, bf16[2,64,512]{2,1,0:T(8,128)(2,1)S(1)}, u32[]{:S(2)}, u32[]{:S(2)}) collective-permute-start(bf16[2,64,512]{2,1,0:T(8,128)(2,1)S(1)} %get-tuple-element.49), channel_id=1, source_target_pairs={{0,2},{1,3},{2,0},{3,1},{4,6},{5,7},{6,4},{7,5},{8,10},{9,11},{10,... | collective-permute-start | bytes 393224 | tf_op jit(solution)/shard_map/ppermute | solution.py:424
  7.1 12.9 %collective-permute-start.4 = (bf16[2,64,512]{2,1,0:T(8,128)(2,1)S(1)}, bf16[2,64,512]{2,1,0:T(8,128)(2,1)S(1)}, u32[]{:S(2)}, u32[]{:S(2)}) collective-permute-start(bf16[2,64,512]{2,1,0:T(8,128)(2,1)S(1)} %get-tuple-element.52), channel_id=1, source_target_pairs={{0,4},{1,5},{2,6},{3,7},{4,0},{5,1},{6,2},{7,3},{8,12},{9,13},{10,... | collective-permute-start | bytes 393224 | tf_op jit(solution)/shard_map/ppermute | solution.py:424
  9.7 10.3 %collective-permute-start.5 = (bf16[2,64,512]{2,1,0:T(8,128)(2,1)S(1)}, bf16[2,64,512]{2,1,0:T(8,128)(2,1)S(1)}, u32[]{:S(2)}, u32[]{:S(2)}) collective-permute-start(bf16[2,64,512]{2,1,0:T(8,128)(2,1)S(1)} %get-tuple-element.53), channel_id=1, source_target_pairs={{0,6},{1,7},{2,4},{3,5},{4,2},{5,3},{6,0},{7,1},{8,14},{9,15},{10,... | collective-permute-start | bytes 393224 | tf_op jit(solution)/shard_map/ppermute | solution.py:424
  12.7 7.3 %collective-permute-start.6 = (bf16[128,512]{1,0:T(8,128)(2,1)S(1)}, bf16[128,512]{1,0:T(8,128)(2,1)S(1)}, u32[]{:S(2)}, u32[]{:S(2)}) collective-permute-start(bf16[128,512]{1,0:T(8,128)(2,1)S(1)} %get-tuple-element.50.rest_0_), channel_id=1, source_target_pairs={{0,16},{8,24},{16,0},{24,8},{1,17},{9,25},{17,1},{25,9},{2,18},{10... | collective-permute-start | bytes 393224 | tf_op jit(solution)/shard_map/ppermute | solution.py:430
  14.5 5.9 %collective-permute-start.7 = (bf16[128,512]{1,0:T(8,128)(2,1)S(1)}, bf16[128,512]{1,0:T(8,128)(2,1)S(1)}, u32[]{:S(2)}, u32[]{:S(2)}) collective-permute-start(bf16[128,512]{1,0:T(8,128)(2,1)S(1)} %get-tuple-element.51), channel_id=1, source_target_pairs={{0,17},{1,16},{2,19},{3,18},{4,21},{5,20},{6,23},{7,22},{8,25},{9,... | collective-permute-start | bytes 393224 | tf_op jit(solution)/shard_map/ppermute | solution.py:433
  15.9 8.0 %collective-permute-start.3 = (bf16[128,512]{1,0:T(8,128)(2,1)S(1)}, bf16[128,512]{1,0:T(8,128)(2,1)S(1)}, u32[]{:S(2)}, u32[]{:S(2)}) collective-permute-start(bf16[128,512]{1,0:T(8,128)(2,1)S(1)} %get-tuple-element.51), channel_id=1, source_target_pairs={{0,1},{1,0},{2,3},{3,2},{4,5},{5,4},{6,7},{7,6},{8,9},{9,8},{10,11... | collective-permute-start | bytes 393224 | tf_op jit(solution)/shard_map/ppermute | solution.py:427
  20.4 5.5 %collective-permute-start.8 = (bf16[128,512]{1,0:T(8,128)(2,1)S(1)}, bf16[128,512]{1,0:T(8,128)(2,1)S(1)}, u32[]{:S(2)}, u32[]{:S(2)}) collective-permute-start(bf16[128,512]{1,0:T(8,128)(2,1)S(1)} %get-tuple-element.55), channel_id=1, source_target_pairs={{0,1},{1,0},{2,3},{3,2},{4,5},{5,4},{6,7},{7,6},{8,9},{9,8},{10,11... | collective-permute-start | bytes 393224 | tf_op jit(solution)/shard_map/ppermute | solution.py:427
  22.0 7.7 %collective-permute-start.9 = (bf16[128,512]{1,0:T(8,128)(2,1)S(1)}, bf16[128,512]{1,0:T(8,128)(2,1)S(1)}, u32[]{:S(2)}, u32[]{:S(2)}) collective-permute-start(bf16[128,512]{1,0:T(8,128)(2,1)S(1)} %get-tuple-element.54.rest_2_), channel_id=1, source_target_pairs={{0,16},{8,24},{16,0},{24,8},{1,17},{9,25},{17,1},{25,9},{2,18},{10... | collective-permute-start | bytes 393224 | tf_op jit(solution)/shard_map/ppermute | solution.py:430
  23.1 6.5 %collective-permute-start.10 = (bf16[128,512]{1,0:T(8,128)(2,1)S(1)}, bf16[128,512]{1,0:T(8,128)(2,1)S(1)}, u32[]{:S(2)}, u32[]{:S(2)}) collective-permute-start(bf16[128,512]{1,0:T(8,128)(2,1)S(1)} %get-tuple-element.55), channel_id=1, source_target_pairs={{0,17},{1,16},{2,19},{3,18},{4,21},{5,20},{6,23},{7,22},{8,25},{9,... | collective-permute-start | bytes 393224 | tf_op jit(solution)/shard_map/ppermute | solution.py:433
  30.1 6.4 %collective-permute-start.13 = (bf16[128,512]{1,0:T(8,128)(2,1)S(1)}, bf16[128,512]{1,0:T(8,128)(2,1)S(1)}, u32[]{:S(2)}, u32[]{:S(2)}) collective-permute-start(bf16[128,512]{1,0:T(8,128)(2,1)S(1)} %shard_map.93), channel_id=1, source_target_pairs={{0,1},{1,0},{2,3},{3,2},{4,5},{5,4},{6,7},{7,6},{8,9},{9,8},{10,11... | collective-permute-start | bytes 393224 | tf_op jit(solution)/shard_map/ppermute | solution.py:427
  31.2 9.1 %collective-permute-start.11 = (bf16[128,512]{1,0:T(8,128)(2,1)S(1)}, bf16[128,512]{1,0:T(8,128)(2,1)S(1)}, u32[]{:S(2)}, u32[]{:S(2)}) collective-permute-start(bf16[128,512]{1,0:T(8,128)(2,1)S(1)} %get-tuple-element.63), channel_id=1, source_target_pairs={{0,16},{8,24},{16,0},{24,8},{1,17},{9,25},{17,1},{25,9},{2,18},{10... | collective-permute-start | bytes 393224 | tf_op jit(solution)/shard_map/ppermute | solution.py:430
  34.4 6.9 %collective-permute-start.12 = (bf16[128,512]{1,0:T(8,128)(2,1)S(1)}, bf16[128,512]{1,0:T(8,128)(2,1)S(1)}, u32[]{:S(2)}, u32[]{:S(2)}) collective-permute-start(bf16[128,512]{1,0:T(8,128)(2,1)S(1)} %get-tuple-element.64), channel_id=1, source_target_pairs={{0,17},{1,16},{2,19},{3,18},{4,21},{5,20},{6,23},{7,22},{8,25},{9,... | collective-permute-start | bytes 393224 | tf_op jit(solution)/shard_map/ppermute | solution.py:433
  35.0 11.9 %collective-permute-start.16 = (bf16[128,512]{1,0:T(8,128)(2,1)S(1)}, bf16[128,512]{1,0:T(8,128)(2,1)S(1)}, u32[]{:S(2)}, u32[]{:S(2)}) collective-permute-start(bf16[128,512]{1,0:T(8,128)(2,1)S(1)} %shard_map.97), channel_id=1, source_target_pairs={{0,1},{1,0},{2,3},{3,2},{4,5},{5,4},{6,7},{7,6},{8,9},{9,8},{10,11... | collective-permute-start | bytes 393224 | tf_op jit(solution)/shard_map/ppermute | solution.py:427
  36.5 10.5 %collective-permute-start.15 = (bf16[128,512]{1,0:T(8,128)(2,1)S(1)}, bf16[128,512]{1,0:T(8,128)(2,1)S(1)}, u32[]{:S(2)}, u32[]{:S(2)}) collective-permute-start(bf16[128,512]{1,0:T(8,128)(2,1)S(1)} %shard_map.96), channel_id=1, source_target_pairs={{0,17},{1,16},{2,19},{3,18},{4,21},{5,20},{6,23},{7,22},{8,25},{9,... | collective-permute-start | bytes 393224 | tf_op jit(solution)/shard_map/ppermute | solution.py:433
  40.2 6.7 %collective-permute-start.14 = (bf16[128,512]{1,0:T(8,128)(2,1)S(1)}, bf16[128,512]{1,0:T(8,128)(2,1)S(1)}, u32[]{:S(2)}, u32[]{:S(2)}) collective-permute-start(bf16[128,512]{1,0:T(8,128)(2,1)S(1)} %shard_map.95), channel_id=1, source_target_pairs={{0,16},{8,24},{16,0},{24,8},{1,17},{9,25},{17,1},{25,9},{2,18},{10... | collective-permute-start | bytes 393224 | tf_op jit(solution)/shard_map/ppermute | solution.py:430
  41.3 9.2 %collective-permute-start.20 = (bf16[2,64,512]{2,1,0:T(8,128)(2,1)S(1)}, bf16[2,64,512]{2,1,0:T(8,128)(2,1)S(1)}, u32[]{:S(2)}, u32[]{:S(2)}) collective-permute-start(bf16[2,64,512]{2,1,0:T(8,128)(2,1)S(1)} %get-tuple-element.66.refs_0_), channel_id=1, source_target_pairs={{0,4},{1,5},{2,6},{3,7},{4,0},{5,1},{6,2},{7,3},{8,12},{9,13},{10,... | collective-permute-start | bytes 393224 | tf_op jit(solution)/shard_map/ppermute | solution.py:424
  45.9 7.0 %collective-permute-start.21 = (bf16[2,64,512]{2,1,0:T(8,128)(2,1)S(1)}, bf16[2,64,512]{2,1,0:T(8,128)(2,1)S(1)}, u32[]{:S(2)}, u32[]{:S(2)}) collective-permute-start(bf16[2,64,512]{2,1,0:T(8,128)(2,1)S(1)} %get-tuple-element.75), channel_id=1, source_target_pairs={{0,6},{1,7},{2,4},{3,5},{4,2},{5,3},{6,0},{7,1},{8,14},{9,15},{10,... | collective-permute-start | bytes 393224 | tf_op jit(solution)/shard_map/ppermute | solution.py:424
  47.0 6.4 %collective-permute-start.19 = (bf16[2,64,512]{2,1,0:T(8,128)(2,1)S(1)}, bf16[2,64,512]{2,1,0:T(8,128)(2,1)S(1)}, u32[]{:S(2)}, u32[]{:S(2)}) collective-permute-start(bf16[2,64,512]{2,1,0:T(8,128)(2,1)S(1)} %get-tuple-element.74), channel_id=1, source_target_pairs={{0,2},{1,3},{2,0},{3,1},{4,6},{5,7},{6,4},{7,5},{8,10},{9,11},{10,... | collective-permute-start | bytes 393224 | tf_op jit(solution)/shard_map/ppermute | solution.py:424
  50.0 3.6 %collective-permute-start.17 = (bf16[64,2048]{1,0:T(8,128)(2,1)S(1)}, bf16[64,2048]{1,0:T(8,128)(2,1)S(1)}, u32[]{:S(2)}, u32[]{:S(2)}) collective-permute-start(bf16[64,2048]{1,0:T(8,128)(2,1)S(1)} %get-tuple-element.71), channel_id=1, source_target_pairs={{0,8},{8,0},{16,24},{24,16},{1,9},{9,1},{17,25},{25,17},{2,10},{10... | collective-permute-start | bytes 786440 | tf_op jit(solution)/shard_map/ppermute | solution.py:483
  50.1 3.6 %collective-permute-start.18 = (bf16[64,2048]{1,0:T(8,128)(2,1)S(1)}, bf16[64,2048]{1,0:T(8,128)(2,1)S(1)}, u32[]{:S(2)}, u32[]{:S(2)}) collective-permute-start(bf16[64,2048]{1,0:T(8,128)(2,1)S(1)} %get-tuple-element.72), channel_id=1, source_target_pairs={{0,8},{8,0},{16,24},{24,16},{1,9},{9,1},{17,25},{25,17},{2,10},{10... | collective-permute-start | bytes 786440 | tf_op jit(solution)/shard_map/ppermute | solution.py:483
  53.5 1.6 %collective-permute-start.22 = (bf16[2,8,16,512]{3,2,1,0:T(8,128)(2,1)S(1)}, bf16[2,8,16,512]{3,2,1,0:T(8,128)(2,1)S(1)}, u32[]{:S(2)}, u32[]{:S(2)}) collective-permute-start(bf16[2,8,16,512]{3,2,1,0:T(8,128)(2,1)S(1)} %get-tuple-element.79), channel_id=1, source_target_pairs={{0,8},{8,0},{16,24},{24,16},{1,9},{9,1},{17,25},{25,17},{2,10},{10... | collective-permute-start | bytes 786440 | tf_op jit(solution)/shard_map/ppermute | solution.py:556

commit v6 on v4

--- a/solution.py
+++ b/solution.py
@@ -313,10 +313,10 @@
             e = jnp.exp2((s - top) * (SCALE * LOG2E))
             total = jnp.sum(e, axis=0, keepdims=True)
             p = e * jnp.where(mine, 1.0 / total, 0.0)
+            ph = p.astype(BF16)
+            dv = jnp.dot(ph, g, preferred_element_type=F32)
             row_dot = jnp.sum(p * gp, axis=0, keepdims=True)
-            ph = p.astype(BF16)
             ds = ph * (gp - row_dot).astype(BF16)
-            dv = jnp.dot(ph, g, preferred_element_type=F32)
             dk = jnp.dot(ds, q, preferred_element_type=F32) * SCALE
             wide = RATIO * tokens
             for i, t in enumerate(which):

time: 56.1 us -> 56.5 us (level)
    ppermute x4, starting transfers between devices: 5.48 us -> 3 us  [along_y(): return lax.ppermute(part, 'ctx', swap_y)]
    ppermute x4, waiting for transfers between devices: 2.5 us -> 0.35 us  [along_xy(): return lax.ppermute(part, ('ctx', 'enc'), swap_xy)]
    ppermute x4, starting transfers between devices: 2.02 us -> 4.01 us  [along_x(): return lax.ppermute(part, 'enc', swap_x)]
    ppermute x4, waiting for transfers between devices: 0.01 us -> 1.84 us  [along_y(): return lax.ppermute(part, 'ctx', swap_y)]
  transfers between devices with their start and end apart: 23 -> 23, of which waited for: 10 -> 9; matrix products, arithmetic and copies ran while one was open for 0% -> 0% of each run, Pallas kernels for 11% -> 14%
where the time goes in v6:
time: 56.5 us; the launch traced here: 56.4 us
  starting transfers between devices  25.8 us (46%)
  waiting for transfers between devices  17.2 us (30%)
  Pallas kernels  12.4 us (22%)
  between operations  0.97 us (2%)
    ppermute x6, starting transfers between devices, along_z(): lax.ppermute(part, 'enc', [(i, i ^ 2 * dz) for i in range(n_enc)])  12.2 us
    ppermute x6, waiting for transfers between devices, along_z(): lax.ppermute(part, 'enc', [(i, i ^ 2 * dz) for i in range(n_enc)])  10.7 us
    pallas_call x13, Pallas kernels, call(): return local_call(body, [IN_VMEM] * len(args), spec, **more)(*args)  7.84 us
    ppermute x4, starting transfers between devices, along_xy(): return lax.ppermute(part, ('ctx', 'enc'), swap_xy)  5.24 us
    ppermute x4, starting transfers between devices, along_x(): return lax.ppermute(part, 'enc', swap_x)  4.01 us
    ppermute x4, waiting for transfers between devices, along_x(): return lax.ppermute(part, 'enc', swap_x)  3.84 us
    ppermute x4, starting transfers between devices, along_y(): return lax.ppermute(part, 'ctx', swap_y)  3 us
    ppermute x4, waiting for transfers between devices, along_y(): return lax.ppermute(part, 'ctx', swap_y)  1.84 us
  transfers between devices with their start and end apart: 23, of which 9 were waited for; matrix products, arithmetic and copies ran while one was open for 0% of the time, Pallas kernels for 14%

profile of v6, /device:TPU:0, one launch (start us, length us, event | category | flops | bytes accessed | tf_op | source)
XLA Modules:
  0.0 56.4 jit_solution(6570826877025341781)
XLA Ops:
  0.6 1.1 %shard_map.86 = (bf16[2,8,16,512]{3,2,1,0:T(8,128)(2,1)S(1)}, bf16[2,8,16,512]{3,2,1,0:T(8,128)(2,1)S(1)}) custom-call(bf16[8,16,1024]{2,1,0:T(8,128)(2,1)} %k_ref.1, bf16[8,16,1024]{2,1,0:T(8,128)(2,1)} %v_ref.1), custom_call_target="tpu_custom_call" | custom-call | bytes 524288 | tf_op jit(solution)/shard_map/pallas_call | solution.py:435
  1.8 0.5 collective-permute-start
  2.3 1.6 %shard_map.85 = (bf16[272,2048]{1,0:T(8,128)(2,1)S(1)}, bf16[144,2048]{1,0:T(8,128)(2,1)S(1)}, bf16[128,2048]{1,0:T(8,128)(2,1)S(1)}, bf16[2,256,128]{2,1,0:T(8,128)(2,1)S(1)}) custom-call(bf16[1,128,4096]{2,1,0:T(8,128)(2,1)} %q_ref.1, bf16[1,128,4096]{2,1,0:T(8,128)(2,1)} %g_ref.1, s32[1,128]{1,0:T(1,128)} %samp_hbm.1, s32[1,2]{1,0:T(1,128)} %tiles_hbm.1), custom_call_target="tpu_custom_call" | custom-call | bytes 4194304 | tf_op jit(solution)/shard_map/pallas_call | solution.py:396
  3.9 0.0 collective-permute-done.got
  3.9 0.1 shard_map.87
  4.0 0.1 collective-permute-start.1
  4.1 3.0 %collective-permute-start.2 = (bf16[2,64,512]{2,1,0:T(8,128)(2,1)S(1)}, bf16[2,64,512]{2,1,0:T(8,128)(2,1)S(1)}, u32[]{:S(2)}, u32[]{:S(2)}) collective-permute-start(bf16[2,64,512]{2,1,0:T(8,128)(2,1)S(1)} %get-tuple-element.49), channel_id=1, source_target_pairs={{0,2},{1,3},{2,0},{3,1},{4,6},{5,7},{6,4},{7,5},{8,10},{9,11},{10,... | collective-permute-start | bytes 393224 | tf_op jit(solution)/shard_map/ppermute | solution.py:424
  7.1 2.6 %collective-permute-start.4 = (bf16[2,64,512]{2,1,0:T(8,128)(2,1)S(1)}, bf16[2,64,512]{2,1,0:T(8,128)(2,1)S(1)}, u32[]{:S(2)}, u32[]{:S(2)}) collective-permute-start(bf16[2,64,512]{2,1,0:T(8,128)(2,1)S(1)} %get-tuple-element.52), channel_id=1, source_target_pairs={{0,4},{1,5},{2,6},{3,7},{4,0},{5,1},{6,2},{7,3},{8,12},{9,13},{10,... | collective-permute-start | bytes 393224 | tf_op jit(solution)/shard_map/ppermute | solution.py:424
  9.7 3.0 %collective-permute-done.2.refs_1_ = bf16[2,64,512]{2,1,0:T(8,128)(2,1)S(1)} collective-permute-done((bf16[2,64,512]{2,1,0:T(8,128)(2,1)S(1)}, bf16[2,64,512]{2,1,0:T(8,128)(2,1)S(1)}, u32[]{:S(2)}, u32[]{:S(2)}) %collective-permute-start.2) | collective-permute-done | bytes 131104 | tf_op jit(solution)/shard_map/ppermute | solution.py:424
  12.7 0.0 collective-permute-done.1.refs_2_.got
  12.7 1.8 %collective-permute-start.6 = (bf16[128,512]{1,0:T(8,128)(2,1)S(1)}, bf16[128,512]{1,0:T(8,128)(2,1)S(1)}, u32[]{:S(2)}, u32[]{:S(2)}) collective-permute-start(bf16[128,512]{1,0:T(8,128)(2,1)S(1)} %get-tuple-element.50.rest_0_), channel_id=1, source_target_pairs={{0,16},{8,24},{16,0},{24,8},{1,17},{9,25},{17,1},{25,9},{2,18},{10... | collective-permute-start | bytes 393224 | tf_op jit(solution)/shard_map/ppermute | solution.py:430
  14.5 1.4 %collective-permute-start.7 = (bf16[128,512]{1,0:T(8,128)(2,1)S(1)}, bf16[128,512]{1,0:T(8,128)(2,1)S(1)}, u32[]{:S(2)}, u32[]{:S(2)}) collective-permute-start(bf16[128,512]{1,0:T(8,128)(2,1)S(1)} %get-tuple-element.51), channel_id=1, source_target_pairs={{0,17},{1,16},{2,19},{3,18},{4,21},{5,20},{6,23},{7,22},{8,25},{9,... | collective-permute-start | bytes 393224 | tf_op jit(solution)/shard_map/ppermute | solution.py:433
  15.9 0.3 collective-permute-start.3
  16.3 3.8 %collective-permute-done.4.refs_0_ = bf16[2,64,512]{2,1,0:T(8,128)(2,1)S(1)} collective-permute-done((bf16[2,64,512]{2,1,0:T(8,128)(2,1)S(1)}, bf16[2,64,512]{2,1,0:T(8,128)(2,1)S(1)}, u32[]{:S(2)}, u32[]{:S(2)}) %collective-permute-start.4) | collective-permute-done | bytes 131104 | tf_op jit(solution)/shard_map/ppermute | solution.py:424
  20.0 0.0 collective-permute-done.5.refs_1_
  20.0 0.0 collective-permute-done.6.refs_3_.rest_0_.rest_4_
  20.0 0.3 collective-permute-done.7.refs_4_.rest_1_.rest_5_
  20.4 1.6 %collective-permute-start.8 = (bf16[128,512]{1,0:T(8,128)(2,1)S(1)}, bf16[128,512]{1,0:T(8,128)(2,1)S(1)}, u32[]{:S(2)}, u32[]{:S(2)}) collective-permute-start(bf16[128,512]{1,0:T(8,128)(2,1)S(1)} %get-tuple-element.55), channel_id=1, source_target_pairs={{0,1},{1,0},{2,3},{3,2},{4,5},{5,4},{6,7},{7,6},{8,9},{9,8},{10,11... | collective-permute-start | bytes 393224 | tf_op jit(solution)/shard_map/ppermute | solution.py:427
  22.0 1.2 %collective-permute-start.9 = (bf16[128,512]{1,0:T(8,128)(2,1)S(1)}, bf16[128,512]{1,0:T(8,128)(2,1)S(1)}, u32[]{:S(2)}, u32[]{:S(2)}) collective-permute-start(bf16[128,512]{1,0:T(8,128)(2,1)S(1)} %get-tuple-element.54.rest_2_), channel_id=1, source_target_pairs={{0,16},{8,24},{16,0},{24,8},{1,17},{9,25},{17,1},{25,9},{2,18},{10... | collective-permute-start | bytes 393224 | tf_op jit(solution)/shard_map/ppermute | solution.py:430
  23.1 0.8 %collective-permute-start.10 = (bf16[128,512]{1,0:T(8,128)(2,1)S(1)}, bf16[128,512]{1,0:T(8,128)(2,1)S(1)}, u32[]{:S(2)}, u32[]{:S(2)}) collective-permute-start(bf16[128,512]{1,0:T(8,128)(2,1)S(1)} %get-tuple-element.55), channel_id=1, source_target_pairs={{0,17},{1,16},{2,19},{3,18},{4,21},{5,20},{6,23},{7,22},{8,25},{9,... | collective-permute-start | bytes 393224 | tf_op jit(solution)/shard_map/ppermute | solution.py:433
  24.0 0.0 collective-permute-done.3.rest_1_
  24.0 1.9 %collective-permute-done.8.rest_3_ = bf16[128,512]{1,0:T(8,128)(2,1)S(1)} collective-permute-done((bf16[128,512]{1,0:T(8,128)(2,1)S(1)}, bf16[128,512]{1,0:T(8,128)(2,1)S(1)}, u32[]{:S(2)}, u32[]{:S(2)}) %collective-permute-start.8) | collective-permute-done | bytes 131104 | tf_op jit(solution)/shard_map/ppermute | solution.py:427
  25.9 3.8 %shard_map.90 = (bf16[4,256,1024]{2,1,0:T(8,128)(2,1)S(1)}, f32[256,512]{1,0:T(8,128)S(1)}, bf16[128,512]{1,0:T(8,128)(2,1)S(1)}, bf16[128,512]{1,0:T(8,128)(2,1)S(1)}) custom-call(bf16[2,256,128]{2,1,0:T(8,128)(2,1)S(1)} %get-tuple-element.56.bias, bf16[144,2048]{1,0:T(8,128)(2,1)S(1)} %get-tuple-element.43.q_a, ...), custom_call_target="tpu_custom_call" | custom-call | flops 1073741824 | bytes 16777216 | tf_op jit(solution)/shard_map/pallas_call | solution.py:55
  29.7 0.0 collective-permute-done.9.rest_2_.rest_6_
  29.7 0.0 collective-permute-done.10.rest_3_.rest_7_
  29.7 2.3 %shard_map.91 = (bf16[4,256,1024]{2,1,0:T(8,128)(2,1)S(1)}, bf16[128,512]{1,0:T(8,128)(2,1)S(1)}, bf16[128,512]{1,0:T(8,128)(2,1)S(1)}, bf16[128,512]{1,0:T(8,128)(2,1)S(1)}, bf16[128,512]{1,0:T(8,128)(2,1)S(1)}) custom-call(bf16[2,256,128]{2,1,0:T(8,128)(2,1)S(1)} %get-tuple-element.56.bias, bf16[144,2048]{1,0:T(8,128)(2,1)S(1)} %get-tuple-element.43.q_a, ...), custom_call_target="tpu_custom_call" | custom-call | flops 1073741824 | bytes 16777216 | tf_op jit(solution)/shard_map/pallas_call | solution.py:55
  32.0 1.1 %collective-permute-start.13 = (bf16[128,512]{1,0:T(8,128)(2,1)S(1)}, bf16[128,512]{1,0:T(8,128)(2,1)S(1)}, u32[]{:S(2)}, u32[]{:S(2)}) collective-permute-start(bf16[128,512]{1,0:T(8,128)(2,1)S(1)} %shard_map.93), channel_id=1, source_target_pairs={{0,1},{1,0},{2,3},{3,2},{4,5},{5,4},{6,7},{7,6},{8,9},{9,8},{10,11... | collective-permute-start | bytes 393224 | tf_op jit(solution)/shard_map/ppermute | solution.py:427
  33.1 0.0 collective-permute-start.11
  33.1 2.5 %collective-permute-start.12 = (bf16[128,512]{1,0:T(8,128)(2,1)S(1)}, bf16[128,512]{1,0:T(8,128)(2,1)S(1)}, u32[]{:S(2)}, u32[]{:S(2)}) collective-permute-start(bf16[128,512]{1,0:T(8,128)(2,1)S(1)} %get-tuple-element.64), channel_id=1, source_target_pairs={{0,17},{1,16},{2,19},{3,18},{4,21},{5,20},{6,23},{7,22},{8,25},{9,... | collective-permute-start | bytes 393224 | tf_op jit(solution)/shard_map/ppermute | solution.py:433
  35.6 1.0 %collective-permute-start.16 = (bf16[128,512]{1,0:T(8,128)(2,1)S(1)}, bf16[128,512]{1,0:T(8,128)(2,1)S(1)}, u32[]{:S(2)}, u32[]{:S(2)}) collective-permute-start(bf16[128,512]{1,0:T(8,128)(2,1)S(1)} %shard_map.95), channel_id=1, source_target_pairs={{0,1},{1,0},{2,3},{3,2},{4,5},{5,4},{6,7},{7,6},{8,9},{9,8},{10,11... | collective-permute-start | bytes 393224 | tf_op jit(solution)/shard_map/ppermute | solution.py:427
  36.6 0.0 collective-permute-start.14
  36.6 1.9 %collective-permute-done.13.back_x = bf16[128,512]{1,0:T(8,128)(2,1)S(1)} collective-permute-done((bf16[128,512]{1,0:T(8,128)(2,1)S(1)}, bf16[128,512]{1,0:T(8,128)(2,1)S(1)}, u32[]{:S(2)}, u32[]{:S(2)}) %collective-permute-start.13) | collective-permute-done | bytes 131104 | tf_op jit(solution)/shard_map/ppermute | solution.py:427
  38.5 0.5 collective-permute-start.15
  39.1 1.8 %collective-permute-done.11.back_y = bf16[128,512]{1,0:T(8,128)(2,1)S(1)} collective-permute-done((bf16[128,512]{1,0:T(8,128)(2,1)S(1)}, bf16[128,512]{1,0:T(8,128)(2,1)S(1)}, u32[]{:S(2)}, u32[]{:S(2)}) %collective-permute-start.11) | collective-permute-done | bytes 131104 | tf_op jit(solution)/shard_map/ppermute | solution.py:430
  40.9 0.1 shard_map.94
  41.0 4.8 %collective-permute-start.20 = (bf16[2,64,512]{2,1,0:T(8,128)(2,1)S(1)}, bf16[2,64,512]{2,1,0:T(8,128)(2,1)S(1)}, u32[]{:S(2)}, u32[]{:S(2)}) collective-permute-start(bf16[2,64,512]{2,1,0:T(8,128)(2,1)S(1)} %get-tuple-element.66.refs_0_), channel_id=1, source_target_pairs={{0,4},{1,5},{2,6},{3,7},{4,0},{5,1},{6,2},{7,3},{8,12},{9,13},{10,... | collective-permute-start | bytes 393224 | tf_op jit(solution)/shard_map/ppermute | solution.py:424
  45.8 1.4 %collective-permute-start.21 = (bf16[2,64,512]{2,1,0:T(8,128)(2,1)S(1)}, bf16[2,64,512]{2,1,0:T(8,128)(2,1)S(1)}, u32[]{:S(2)}, u32[]{:S(2)}) collective-permute-start(bf16[2,64,512]{2,1,0:T(8,128)(2,1)S(1)} %get-tuple-element.75), channel_id=1, source_target_pairs={{0,6},{1,7},{2,4},{3,5},{4,2},{5,3},{6,0},{7,1},{8,14},{9,15},{10,... | collective-permute-start | bytes 393224 | tf_op jit(solution)/shard_map/ppermute | solution.py:424
  47.2 0.1 shard_map.96
  47.3 0.4 collective-permute-start.19
  47.7 1.5 %shard_map.92 = (bf16[128,2048]{1,0:T(8,128)(2,1)S(1)}, bf16[128,2048]{1,0:T(8,128)(2,1)S(1)}) custom-call(bf16[144,2048]{1,0:T(8,128)(2,1)S(1)} %get-tuple-element.43.q_a, bf16[272,2048]{1,0:T(8,128)(2,1)S(1)} %collective-permute-done.1.refs_2_.got, bf16[128,512]{1,0:T(8,128)(2,1)S(1)} %get-tuple-element.50.rest_0_, ...), custom_call_target="tpu_custom_call" | custom-call | flops 536870912 | bytes 8388608 | tf_op jit(solution)/shard_map/pallas_call | solution.py:55
  49.2 0.1 collective-permute-start.17
  49.3 0.5 collective-permute-start.18
  49.8 3.0 %collective-permute-done.21.refs_1_ = bf16[2,64,512]{2,1,0:T(8,128)(2,1)S(1)} collective-permute-done((bf16[2,64,512]{2,1,0:T(8,128)(2,1)S(1)}, bf16[2,64,512]{2,1,0:T(8,128)(2,1)S(1)}, u32[]{:S(2)}, u32[]{:S(2)}) %collective-permute-start.21) | collective-permute-done | bytes 131104 | tf_op jit(solution)/shard_map/ppermute | solution.py:424
  52.8 1.0 %collective-permute-done.19.refs_1_ = bf16[2,64,512]{2,1,0:T(8,128)(2,1)S(1)} collective-permute-done((bf16[2,64,512]{2,1,0:T(8,128)(2,1)S(1)}, bf16[2,64,512]{2,1,0:T(8,128)(2,1)S(1)}, u32[]{:S(2)}, u32[]{:S(2)}) %collective-permute-start.19) | collective-permute-done | bytes 131104 | tf_op jit(solution)/shard_map/ppermute | solution.py:424
  53.8 0.1 collective-permute-start.22
  53.9 1.0 %shard_map.98 = (bf16[1,128,4096]{2,1,0:T(8,128)(2,1)}, f32[8,128]{1,0:T(8,128)S(1)}) custom-call(bf16[128,2048]{1,0:T(8,128)(2,1)S(1)} %get-tuple-element.61.mine, bf16[64,2048]{1,0:T(8,128)(2,1)S(1)} %collective-permute-done.17.refs_0_, bf16[64,2048]{1,0:T(8,128)(2,1)S(1)} %collective-permute-done.18.refs_1_), custom_call_target="tpu_custom_call" | custom-call | bytes 524288 | tf_op jit(solution)/shard_map/pallas_call | solution.py:532
  54.9 0.5 collective-permute-done.22.got
  55.4 0.8 %shard_map.101 = (bf16[8,16,1024]{2,1,0:T(8,128)(2,1)}, bf16[8,16,1024]{2,1,0:T(8,128)(2,1)}) custom-call(bf16[2,8,16,512]{3,2,1,0:T(8,128)(2,1)S(1)} %get-tuple-element.78.mine, bf16[2,8,16,512]{3,2,1,0:T(8,128)(2,1)S(1)} %collective-permute-done.22.got, f32[8,128]{1,0:T(8,128)S(1)} %get-tuple-element.80._), custom_call_target="tpu_custom_call" | custom-call | bytes 524288 | tf_op jit(solution)/shard_map/pallas_call | solution.py:547
  (15 shorter events, 0.2 us)
Async XLA Ops:
  1.8 2.1 %collective-permute-start = (bf16[2,8,16,512]{3,2,1,0:T(8,128)(2,1)S(1)}, bf16[2,8,16,512]{3,2,1,0:T(8,128)(2,1)S(1)}, u32[]{:S(2)}, u32[]{:S(2)}) collective-permute-start(bf16[2,8,16,512]{3,2,1,0:T(8,128)(2,1)S(1)} %get-tuple-element.45), channel_id=1, source_target_pairs={{0,8},{8,0},{16,24},{24,16},{1,9},{9,1},{17,25},{25,17},{2,10},{10... | collective-permute-start | bytes 786440 | tf_op jit(solution)/shard_map/ppermute | solution.py:446
  4.0 8.7 %collective-permute-start.1 = (bf16[272,2048]{1,0:T(8,128)(2,1)S(1)}, bf16[272,2048]{1,0:T(8,128)(2,1)S(1)}, u32[]{:S(2)}, u32[]{:S(2)}) collective-permute-start(bf16[272,2048]{1,0:T(8,128)(2,1)S(1)} %get-tuple-element.47), channel_id=1, source_target_pairs={{0,8},{8,0},{16,24},{24,16},{1,9},{9,1},{17,25},{25,17},{2,10},{10... | collective-permute-start | bytes 3342344 | tf_op jit(solution)/shard_map/ppermute | solution.py:447
  4.1 8.6 %collective-permute-start.2 = (bf16[2,64,512]{2,1,0:T(8,128)(2,1)S(1)}, bf16[2,64,512]{2,1,0:T(8,128)(2,1)S(1)}, u32[]{:S(2)}, u32[]{:S(2)}) collective-permute-start(bf16[2,64,512]{2,1,0:T(8,128)(2,1)S(1)} %get-tuple-element.49), channel_id=1, source_target_pairs={{0,2},{1,3},{2,0},{3,1},{4,6},{5,7},{6,4},{7,5},{8,10},{9,11},{10,... | collective-permute-start | bytes 393224 | tf_op jit(solution)/shard_map/ppermute | solution.py:424
  7.1 12.9 %collective-permute-start.4 = (bf16[2,64,512]{2,1,0:T(8,128)(2,1)S(1)}, bf16[2,64,512]{2,1,0:T(8,128)(2,1)S(1)}, u32[]{:S(2)}, u32[]{:S(2)}) collective-permute-start(bf16[2,64,512]{2,1,0:T(8,128)(2,1)S(1)} %get-tuple-element.52), channel_id=1, source_target_pairs={{0,4},{1,5},{2,6},{3,7},{4,0},{5,1},{6,2},{7,3},{8,12},{9,13},{10,... | collective-permute-start | bytes 393224 | tf_op jit(solution)/shard_map/ppermute | solution.py:424
  9.7 10.3 %collective-permute-start.5 = (bf16[2,64,512]{2,1,0:T(8,128)(2,1)S(1)}, bf16[2,64,512]{2,1,0:T(8,128)(2,1)S(1)}, u32[]{:S(2)}, u32[]{:S(2)}) collective-permute-start(bf16[2,64,512]{2,1,0:T(8,128)(2,1)S(1)} %get-tuple-element.53), channel_id=1, source_target_pairs={{0,6},{1,7},{2,4},{3,5},{4,2},{5,3},{6,0},{7,1},{8,14},{9,15},{10,... | collective-permute-start | bytes 393224 | tf_op jit(solution)/shard_map/ppermute | solution.py:424
  12.7 7.3 %collective-permute-start.6 = (bf16[128,512]{1,0:T(8,128)(2,1)S(1)}, bf16[128,512]{1,0:T(8,128)(2,1)S(1)}, u32[]{:S(2)}, u32[]{:S(2)}) collective-permute-start(bf16[128,512]{1,0:T(8,128)(2,1)S(1)} %get-tuple-element.50.rest_0_), channel_id=1, source_target_pairs={{0,16},{8,24},{16,0},{24,8},{1,17},{9,25},{17,1},{25,9},{2,18},{10... | collective-permute-start | bytes 393224 | tf_op jit(solution)/shard_map/ppermute | solution.py:430
  14.5 5.9 %collective-permute-start.7 = (bf16[128,512]{1,0:T(8,128)(2,1)S(1)}, bf16[128,512]{1,0:T(8,128)(2,1)S(1)}, u32[]{:S(2)}, u32[]{:S(2)}) collective-permute-start(bf16[128,512]{1,0:T(8,128)(2,1)S(1)} %get-tuple-element.51), channel_id=1, source_target_pairs={{0,17},{1,16},{2,19},{3,18},{4,21},{5,20},{6,23},{7,22},{8,25},{9,... | collective-permute-start | bytes 393224 | tf_op jit(solution)/shard_map/ppermute | solution.py:433
  15.9 8.0 %collective-permute-start.3 = (bf16[128,512]{1,0:T(8,128)(2,1)S(1)}, bf16[128,512]{1,0:T(8,128)(2,1)S(1)}, u32[]{:S(2)}, u32[]{:S(2)}) collective-permute-start(bf16[128,512]{1,0:T(8,128)(2,1)S(1)} %get-tuple-element.51), channel_id=1, source_target_pairs={{0,1},{1,0},{2,3},{3,2},{4,5},{5,4},{6,7},{7,6},{8,9},{9,8},{10,11... | collective-permute-start | bytes 393224 | tf_op jit(solution)/shard_map/ppermute | solution.py:427
  20.4 5.5 %collective-permute-start.8 = (bf16[128,512]{1,0:T(8,128)(2,1)S(1)}, bf16[128,512]{1,0:T(8,128)(2,1)S(1)}, u32[]{:S(2)}, u32[]{:S(2)}) collective-permute-start(bf16[128,512]{1,0:T(8,128)(2,1)S(1)} %get-tuple-element.55), channel_id=1, source_target_pairs={{0,1},{1,0},{2,3},{3,2},{4,5},{5,4},{6,7},{7,6},{8,9},{9,8},{10,11... | collective-permute-start | bytes 393224 | tf_op jit(solution)/shard_map/ppermute | solution.py:427
  22.0 7.7 %collective-permute-start.9 = (bf16[128,512]{1,0:T(8,128)(2,1)S(1)}, bf16[128,512]{1,0:T(8,128)(2,1)S(1)}, u32[]{:S(2)}, u32[]{:S(2)}) collective-permute-start(bf16[128,512]{1,0:T(8,128)(2,1)S(1)} %get-tuple-element.54.rest_2_), channel_id=1, source_target_pairs={{0,16},{8,24},{16,0},{24,8},{1,17},{9,25},{17,1},{25,9},{2,18},{10... | collective-permute-start | bytes 393224 | tf_op jit(solution)/shard_map/ppermute | solution.py:430
  23.1 6.5 %collective-permute-start.10 = (bf16[128,512]{1,0:T(8,128)(2,1)S(1)}, bf16[128,512]{1,0:T(8,128)(2,1)S(1)}, u32[]{:S(2)}, u32[]{:S(2)}) collective-permute-start(bf16[128,512]{1,0:T(8,128)(2,1)S(1)} %get-tuple-element.55), channel_id=1, source_target_pairs={{0,17},{1,16},{2,19},{3,18},{4,21},{5,20},{6,23},{7,22},{8,25},{9,... | collective-permute-start | bytes 393224 | tf_op jit(solution)/shard_map/ppermute | solution.py:433
  32.0 6.5 %collective-permute-start.13 = (bf16[128,512]{1,0:T(8,128)(2,1)S(1)}, bf16[128,512]{1,0:T(8,128)(2,1)S(1)}, u32[]{:S(2)}, u32[]{:S(2)}) collective-permute-start(bf16[128,512]{1,0:T(8,128)(2,1)S(1)} %shard_map.93), channel_id=1, source_target_pairs={{0,1},{1,0},{2,3},{3,2},{4,5},{5,4},{6,7},{7,6},{8,9},{9,8},{10,11... | collective-permute-start | bytes 393224 | tf_op jit(solution)/shard_map/ppermute | solution.py:427
  33.1 7.8 %collective-permute-start.11 = (bf16[128,512]{1,0:T(8,128)(2,1)S(1)}, bf16[128,512]{1,0:T(8,128)(2,1)S(1)}, u32[]{:S(2)}, u32[]{:S(2)}) collective-permute-start(bf16[128,512]{1,0:T(8,128)(2,1)S(1)} %get-tuple-element.63), channel_id=1, source_target_pairs={{0,16},{8,24},{16,0},{24,8},{1,17},{9,25},{17,1},{25,9},{2,18},{10... | collective-permute-start | bytes 393224 | tf_op jit(solution)/shard_map/ppermute | solution.py:430
  33.1 7.8 %collective-permute-start.12 = (bf16[128,512]{1,0:T(8,128)(2,1)S(1)}, bf16[128,512]{1,0:T(8,128)(2,1)S(1)}, u32[]{:S(2)}, u32[]{:S(2)}) collective-permute-start(bf16[128,512]{1,0:T(8,128)(2,1)S(1)} %get-tuple-element.64), channel_id=1, source_target_pairs={{0,17},{1,16},{2,19},{3,18},{4,21},{5,20},{6,23},{7,22},{8,25},{9,... | collective-permute-start | bytes 393224 | tf_op jit(solution)/shard_map/ppermute | solution.py:433
  35.6 11.7 %collective-permute-start.16 = (bf16[128,512]{1,0:T(8,128)(2,1)S(1)}, bf16[128,512]{1,0:T(8,128)(2,1)S(1)}, u32[]{:S(2)}, u32[]{:S(2)}) collective-permute-start(bf16[128,512]{1,0:T(8,128)(2,1)S(1)} %shard_map.95), channel_id=1, source_target_pairs={{0,1},{1,0},{2,3},{3,2},{4,5},{5,4},{6,7},{7,6},{8,9},{9,8},{10,11... | collective-permute-start | bytes 393224 | tf_op jit(solution)/shard_map/ppermute | solution.py:427
  36.6 10.6 %collective-permute-start.14 = (bf16[128,512]{1,0:T(8,128)(2,1)S(1)}, bf16[128,512]{1,0:T(8,128)(2,1)S(1)}, u32[]{:S(2)}, u32[]{:S(2)}) collective-permute-start(bf16[128,512]{1,0:T(8,128)(2,1)S(1)} %get-tuple-element.67), channel_id=1, source_target_pairs={{0,16},{8,24},{16,0},{24,8},{1,17},{9,25},{17,1},{25,9},{2,18},{10... | collective-permute-start | bytes 393224 | tf_op jit(solution)/shard_map/ppermute | solution.py:430
  38.5 8.7 %collective-permute-start.15 = (bf16[128,512]{1,0:T(8,128)(2,1)S(1)}, bf16[128,512]{1,0:T(8,128)(2,1)S(1)}, u32[]{:S(2)}, u32[]{:S(2)}) collective-permute-start(bf16[128,512]{1,0:T(8,128)(2,1)S(1)} %get-tuple-element.68), channel_id=1, source_target_pairs={{0,17},{1,16},{2,19},{3,18},{4,21},{5,20},{6,23},{7,22},{8,25},{9,... | collective-permute-start | bytes 393224 | tf_op jit(solution)/shard_map/ppermute | solution.py:433
  41.0 8.8 %collective-permute-start.20 = (bf16[2,64,512]{2,1,0:T(8,128)(2,1)S(1)}, bf16[2,64,512]{2,1,0:T(8,128)(2,1)S(1)}, u32[]{:S(2)}, u32[]{:S(2)}) collective-permute-start(bf16[2,64,512]{2,1,0:T(8,128)(2,1)S(1)} %get-tuple-element.66.refs_0_), channel_id=1, source_target_pairs={{0,4},{1,5},{2,6},{3,7},{4,0},{5,1},{6,2},{7,3},{8,12},{9,13},{10,... | collective-permute-start | bytes 393224 | tf_op jit(solution)/shard_map/ppermute | solution.py:424
  45.8 6.9 %collective-permute-start.21 = (bf16[2,64,512]{2,1,0:T(8,128)(2,1)S(1)}, bf16[2,64,512]{2,1,0:T(8,128)(2,1)S(1)}, u32[]{:S(2)}, u32[]{:S(2)}) collective-permute-start(bf16[2,64,512]{2,1,0:T(8,128)(2,1)S(1)} %get-tuple-element.75), channel_id=1, source_target_pairs={{0,6},{1,7},{2,4},{3,5},{4,2},{5,3},{6,0},{7,1},{8,14},{9,15},{10,... | collective-permute-start | bytes 393224 | tf_op jit(solution)/shard_map/ppermute | solution.py:424
  47.3 6.4 %collective-permute-start.19 = (bf16[2,64,512]{2,1,0:T(8,128)(2,1)S(1)}, bf16[2,64,512]{2,1,0:T(8,128)(2,1)S(1)}, u32[]{:S(2)}, u32[]{:S(2)}) collective-permute-start(bf16[2,64,512]{2,1,0:T(8,128)(2,1)S(1)} %get-tuple-element.74), channel_id=1, source_target_pairs={{0,2},{1,3},{2,0},{3,1},{4,6},{5,7},{6,4},{7,5},{8,10},{9,11},{10,... | collective-permute-start | bytes 393224 | tf_op jit(solution)/shard_map/ppermute | solution.py:424
  49.2 4.7 %collective-permute-start.17 = (bf16[64,2048]{1,0:T(8,128)(2,1)S(1)}, bf16[64,2048]{1,0:T(8,128)(2,1)S(1)}, u32[]{:S(2)}, u32[]{:S(2)}) collective-permute-start(bf16[64,2048]{1,0:T(8,128)(2,1)S(1)} %get-tuple-element.71), channel_id=1, source_target_pairs={{0,8},{8,0},{16,24},{24,16},{1,9},{9,1},{17,25},{25,17},{2,10},{10... | collective-permute-start | bytes 786440 | tf_op jit(solution)/shard_map/ppermute | solution.py:479
  49.3 4.6 %collective-permute-start.18 = (bf16[64,2048]{1,0:T(8,128)(2,1)S(1)}, bf16[64,2048]{1,0:T(8,128)(2,1)S(1)}, u32[]{:S(2)}, u32[]{:S(2)}) collective-permute-start(bf16[64,2048]{1,0:T(8,128)(2,1)S(1)} %get-tuple-element.72), channel_id=1, source_target_pairs={{0,8},{8,0},{16,24},{24,16},{1,9},{9,1},{17,25},{25,17},{2,10},{10... | collective-permute-start | bytes 786440 | tf_op jit(solution)/shard_map/ppermute | solution.py:479
  53.8 1.6 %collective-permute-start.22 = (bf16[2,8,16,512]{3,2,1,0:T(8,128)(2,1)S(1)}, bf16[2,8,16,512]{3,2,1,0:T(8,128)(2,1)S(1)}, u32[]{:S(2)}, u32[]{:S(2)}) collective-permute-start(bf16[2,8,16,512]{3,2,1,0:T(8,128)(2,1)S(1)} %get-tuple-element.79), channel_id=1, source_target_pairs={{0,8},{8,0},{16,24},{24,16},{1,9},{9,1},{17,25},{25,17},{2,10},{10... | collective-permute-start | bytes 786440 | tf_op jit(solution)/shard_map/ppermute | solution.py:552
